TPU v7x, 256 devices: a whole 4x4x8 slice. The times are simulated.
256 devices in a mesh: section: 4 (over y), tile: 16 (over z_hi, x, core), col: 4 (over z_lo).
Axes of the slice: x: 4, y: 4, z: 8 (z_hi: 2, z_lo: 4; z = z_hi * 4 + z_lo), core: 2. Of those that a mesh axis runs over, the one named last changes fastest.
Arguments:
- initial_states: float32 [8, 128, 32, 512], P(None, None, 'tile', 'col'), may hold values from -6 to 6
- targets: bfloat16 [4, 8, 128, 32, 512], P('section', None, None, 'tile', 'col'), may hold values from -6 to 6
- w_in: bfloat16 [4096, 128], replicated, may hold values from -0.5 to 0.5
- w_out: bfloat16 [128, 4096], replicated, may hold values from -0.09375 to 0.09375
- diffusivity: float32 [128], replicated, may hold values from 0.03 to 0.22
- stiffness: float32 [128], replicated, may hold values from 0.5 to 4000
- land_mask: int32 [32, 512], P('tile', 'col'), may hold values 0 or 1
- wet_levels: int32 [32, 512], P('tile', 'col'), may hold values from 1 to 16
- plan: int32 [8], replicated, may hold values from 0 to 7, each once
Outputs:
- trajectory: float32 [4, 8, 128, 32, 512], P('section', None, None, 'tile', 'col')
- grad_w_in: float32 [4096, 128], replicated
- grad_w_out: float32 [128, 4096], replicated
Inputs may be any that keep to these rules, and one draw needn't show every extreme that they name: `plan`: each of the 8 samples appears once.
All inputs are finite; a program needn't handle non-finite values. No bound on the sum of `land_mask` on one device may be relied on, other than what follows from the above.
Results may differ from a plain program's by a relative error of at most 0.0026.
Values may be sent and summed in bfloat16 or wider, within the bound.
No kernel may reach another device: no remote copies, remote signals or barrier semaphores. Data moves between devices by JAX's collectives and lax.ppermute only.
A program may use at most 64 MiB of HBM per device.

v0:
```python
import math

import jax
import jax.numpy as jnp
from jax import lax
from jax.sharding import PartitionSpec as P

V = 8
L = 16
H = 4096


def with_halo(block, sides, width):
    for axis, dim in sides:
        count = lax.axis_size(axis)
        forward = [(i, i + 1) for i in range(count - 1)]
        backward = [(target, source) for source, target in forward]
        low = lax.ppermute(
            lax.slice_in_dim(block, block.shape[dim] - width, None, axis=dim), axis, forward
        )
        high = lax.ppermute(lax.slice_in_dim(block, 0, width, axis=dim), axis, backward)
        block = jnp.concatenate([low, block, high], axis=dim)
    return block


def mode_table(level_count):
    order_index = jnp.arange(level_count).astype(jnp.float32)
    angles = jnp.pi * (order_index[None, :] + 0.5) * order_index[:, None] / level_count
    weights = jnp.where(
        order_index[:, None] == 0.0, math.sqrt(1.0 / level_count), math.sqrt(2.0 / level_count)
    )
    return jnp.cos(angles) * weights


def implicit_solve(right_side, coupling):
    cell_count = right_side.shape[1]
    ones_grid = jnp.ones((right_side.shape[0], cell_count), right_side.dtype)
    off_diag = -coupling[:, None] * ones_grid
    lower_diag = off_diag.at[:, 0].set(0.0)
    upper_diag = off_diag.at[:, cell_count - 1].set(0.0)
    middle = (1.0 + 2.0 * coupling[:, None]) * ones_grid
    return lax.linalg.tridiagonal_solve(lower_diag, middle, upper_diag, right_side)


def contract_rows(left_operand, right_operand):
    return lax.dot_general(
        left_operand, right_operand, (((1,), (1,)), ((), ())), preferred_element_type=jnp.float32
    )


def contract_lead(left_operand, right_operand):
    return lax.dot_general(
        left_operand, right_operand, (((0,), (0,)), ((), ())), preferred_element_type=jnp.float32
    )


def local(
    initial_states, targets, w_in, w_out, diffusivity, stiffness, land_mask, wet_levels, plan
):
    section_count = lax.axis_size("section")
    my_section = lax.axis_index("section")
    tile_count = lax.axis_size("tile")
    my_tile = lax.axis_index("tile")
    samples = initial_states.shape[0]
    features = initial_states.shape[1]
    x_cells = initial_states.shape[2]
    y_cells = initial_states.shape[3]
    columns = x_cells * y_cells
    modes_here = L // tile_count
    mode_matrix = mode_table(L)
    level_index = jnp.arange(L)
    wet_cells = ((land_mask[None] == 1) & (level_index[:, None, None] < wet_levels[None])).astype(
        jnp.float32
    )
    wet_rows = jnp.tile(wet_cells, (V, 1, 1)).reshape(features, columns)
    couple_all = stiffness.reshape(V, L)
    couple_here = lax.dynamic_slice_in_dim(couple_all, my_tile * modes_here, modes_here, 1).reshape(
        V * modes_here
    )
    grid_total = samples * section_count * x_cells * tile_count * y_cells * lax.axis_size("col")
    grad_scale = 1.0 / math.sqrt(grid_total)

    def solve_items(modal_piece):
        solved = implicit_solve(
            modal_piece.reshape(V * modes_here, modal_piece.shape[2], modal_piece.shape[3]),
            couple_here,
        )
        return lax.all_to_all(
            solved.reshape(modal_piece.shape), "tile", split_axis=2, concat_axis=1, tiled=True
        )

    def dynamics(column_state):
        padded = with_halo(column_state, (("tile", 1), ("col", 2)), 1)
        laplace = (
            padded[:, 2:, 1:-1]
            + padded[:, :-2, 1:-1]
            + padded[:, 1:-1, 2:]
            + padded[:, 1:-1, :-2]
            - 4.0 * column_state
        )
        smoothed = (column_state + diffusivity[:, None, None] * laplace).reshape(
            V, L, x_cells, y_cells
        ) * wet_cells[None]
        modal_fields = jnp.einsum(
            "ml,vlxy->vmxy", mode_matrix, smoothed, precision=lax.Precision.HIGHEST
        )
        relaxed = solve_items(
            lax.all_to_all(modal_fields, "tile", split_axis=1, concat_axis=2, tiled=True)
        )
        levels_back = jnp.einsum(
            "ml,vmxy->vlxy", mode_matrix, relaxed, precision=lax.Precision.HIGHEST
        )
        return (levels_back * wet_cells[None]).reshape(features, columns)

    def physics(column_state, target, weight_flag, grad_in, grad_out):
        after_dynamics = dynamics(column_state)
        inputs = after_dynamics.astype(jnp.bfloat16)
        hidden = jnp.tanh(jnp.dot(w_in, inputs, preferred_element_type=jnp.float32))
        hidden_bf = hidden.astype(jnp.bfloat16)
        tendency = jnp.dot(w_out, hidden_bf, preferred_element_type=jnp.float32)
        result = (wet_rows * (after_dynamics + tendency)).reshape(features, x_cells, y_cells)
        misfit = (
            wet_rows
            * (tendency - target.reshape(features, columns).astype(jnp.float32))
            * (grad_scale * weight_flag)
        ).astype(jnp.bfloat16)
        grad_out = grad_out + contract_rows(misfit, hidden_bf)
        back_hidden = (contract_lead(w_out, misfit) * (1.0 - hidden * hidden)).astype(jnp.bfloat16)
        grad_in = grad_in + contract_rows(back_hidden, inputs)
        return (result, grad_in, grad_out)

    zero_in = jnp.zeros((H, features), jnp.float32)
    zero_out = jnp.zeros((features, H), jnp.float32)
    own_count = samples // section_count
    ordered = jnp.take(targets[0], plan, axis=0)
    local_targets = lax.all_to_all(
        ordered[None], "section", split_axis=1, concat_axis=0, tiled=True
    )

    def rollout(turn, loop_state):
        carried, grad_in, grad_out, kept_states = loop_state
        own_slot = turn // section_count
        step_here = turn % section_count
        position = my_section * own_count + own_slot
        fresh = lax.dynamic_index_in_dim(initial_states, plan[position], 0, keepdims=False)
        column_state = jnp.where(step_here == 0, fresh, carried)
        target = local_targets[step_here, own_slot]
        result, grad_in, grad_out = physics(column_state, target, 1.0, grad_in, grad_out)
        kept_states = kept_states.at[step_here, own_slot].set(result)
        return (result, grad_in, grad_out, kept_states)

    start = (
        jnp.zeros((features, x_cells, y_cells), jnp.float32),
        zero_in,
        zero_out,
        jnp.zeros((section_count, own_count, features, x_cells, y_cells), jnp.float32),
    )
    final_state = lax.fori_loop(0, own_count * section_count, rollout, start)
    trajectory = lax.all_to_all(final_state[3], "section", split_axis=0, concat_axis=1, tiled=True)
    grad_in = final_state[1]
    grad_out = final_state[2]
    total_in, total_out = lax.psum((grad_in, grad_out), ("section", "tile", "col"))
    return (trajectory, total_in, total_out)


def solution(mesh):
    in_specs = (
        P(None, None, "tile", "col"),
        P("section", None, None, "tile", "col"),
        P(),
        P(),
        P(),
        P(),
        P("tile", "col"),
        P("tile", "col"),
        P(),
    )
    out_specs = (P("section", None, None, "tile", "col"), P(), P())
    return jax.shard_map(local, mesh=mesh, in_specs=in_specs, out_specs=out_specs, check_vma=False)
```

profile of v0, /device:TPU:1, one launch (start us, length us, event | category | flops | bytes accessed | tf_op | source)
XLA Modules:
  0.0 962.6 jit_solution(5746113608037929001)
XLA Ops:
  12.6 5.0 all-to-all-start.2
  17.6 7.0 all-to-all-done.2
  25.8 661.8 %while.26 = (s32[]{:T(128)}, f32[128,2,128]{0,2,1:T(8,128)S(1)}, f32[4096,128]{1,0:T(8,128)}, f32[128,4096]{1,0:T(8,128)}, f32[4,2,128,2,128]{2,4,3,1,0:T(8,128)...) while((s32[]{:T(128)}, f32[128,2,128]{0,2,1:T(8,128)S(1)}, ...), condition=%wide.region_3.4_spmd.clone.clone, body=%wide.region_0.0_spmd.clone.clone.sunk | while | flops 1364534016 | bytes 53896336 | solution.py:158
  29.5 5.4 collective-permute-start
  44.6 4.4 collective-permute-done.2
  49.0 4.3 collective-permute-done.3
  54.7 13.4 %all-to-all-start = ((f32[8,16,2,128]{3,2,0,1:T(2,128)}), f32[8,16,2,128]{3,2,0,1:T(2,128)S(1)}, u32[]{:S(2)}, u32[]{:S(2)}) async-start(f32[8,16,2,128]{3,2,0,1:T(2,128)} %copy.187), calls=%async_computation | async-start | bytes 262144 | tf_op jit(solution)/shard_map/while/body/eval_jaxpr/all_to_all | solution.py:108
  68.2 10.1 %all-to-all-done = f32[8,16,2,128]{3,2,0,1:T(2,128)S(1)} async-done(((f32[8,16,2,128]{3,2,0,1:T(2,128)}), f32[8,16,2,128]{3,2,0,1:T(2,128)S(1)}, u32[]{:S(2)}, u32[]{:S(2)}) %all-to-all-start) | async-done | bytes 131104 | tf_op jit(solution)/shard_map/while/body/eval_jaxpr/all_to_all | solution.py:108
  86.6 8.1 all-to-all-done.1
  98.1 4.8 convolution_add_fusion.4
  102.9 4.0 convolution_add_fusion.5
  119.9 4.6 collective-permute-start.2
  126.1 4.4 collective-permute-done.2
  130.5 4.0 collective-permute-done.3
  135.9 13.3 %all-to-all-start = ((f32[8,16,2,128]{3,2,0,1:T(2,128)}), f32[8,16,2,128]{3,2,0,1:T(2,128)S(1)}, u32[]{:S(2)}, u32[]{:S(2)}) async-start(f32[8,16,2,128]{3,2,0,1:T(2,128)} %copy.187), calls=%async_computation | async-start | bytes 262144 | tf_op jit(solution)/shard_map/while/body/eval_jaxpr/all_to_all | solution.py:108
  149.2 10.1 %all-to-all-done = f32[8,16,2,128]{3,2,0,1:T(2,128)S(1)} async-done(((f32[8,16,2,128]{3,2,0,1:T(2,128)}), f32[8,16,2,128]{3,2,0,1:T(2,128)S(1)}, u32[]{:S(2)}, u32[]{:S(2)}) %all-to-all-start) | async-done | bytes 131104 | tf_op jit(solution)/shard_map/while/body/eval_jaxpr/all_to_all | solution.py:108
  161.8 4.0 all-to-all-start.1
  167.7 8.3 all-to-all-done.1
  179.3 5.4 convolution_add_fusion.4
  184.7 4.7 convolution_add_fusion.5
  207.4 4.5 collective-permute-done.2
  211.9 4.6 collective-permute-done.3
  217.9 13.9 %all-to-all-start = ((f32[8,16,2,128]{3,2,0,1:T(2,128)}), f32[8,16,2,128]{3,2,0,1:T(2,128)S(1)}, u32[]{:S(2)}, u32[]{:S(2)}) async-start(f32[8,16,2,128]{3,2,0,1:T(2,128)} %copy.187), calls=%async_computation | async-start | bytes 262144 | tf_op jit(solution)/shard_map/while/body/eval_jaxpr/all_to_all | solution.py:108
  231.9 10.1 %all-to-all-done = f32[8,16,2,128]{3,2,0,1:T(2,128)S(1)} async-done(((f32[8,16,2,128]{3,2,0,1:T(2,128)}), f32[8,16,2,128]{3,2,0,1:T(2,128)S(1)}, u32[]{:S(2)}, u32[]{:S(2)}) %all-to-all-start) | async-done | bytes 131104 | tf_op jit(solution)/shard_map/while/body/eval_jaxpr/all_to_all | solution.py:108
  250.3 8.3 all-to-all-done.1
  262.0 5.5 convolution_add_fusion.4
  267.4 4.7 convolution_add_fusion.5
  290.2 4.5 collective-permute-done.2
  294.7 4.6 collective-permute-done.3
  300.6 13.9 %all-to-all-start = ((f32[8,16,2,128]{3,2,0,1:T(2,128)}), f32[8,16,2,128]{3,2,0,1:T(2,128)S(1)}, u32[]{:S(2)}, u32[]{:S(2)}) async-start(f32[8,16,2,128]{3,2,0,1:T(2,128)} %copy.187), calls=%async_computation | async-start | bytes 262144 | tf_op jit(solution)/shard_map/while/body/eval_jaxpr/all_to_all | solution.py:108
  314.6 10.1 %all-to-all-done = f32[8,16,2,128]{3,2,0,1:T(2,128)S(1)} async-done(((f32[8,16,2,128]{3,2,0,1:T(2,128)}), f32[8,16,2,128]{3,2,0,1:T(2,128)S(1)}, u32[]{:S(2)}, u32[]{:S(2)}) %all-to-all-start) | async-done | bytes 131104 | tf_op jit(solution)/shard_map/while/body/eval_jaxpr/all_to_all | solution.py:108
  333.0 8.3 all-to-all-done.1
  344.6 5.4 convolution_add_fusion.4
  350.1 4.7 convolution_add_fusion.5
  372.8 4.5 collective-permute-done.2
  377.3 4.6 collective-permute-done.3
  383.3 13.9 %all-to-all-start = ((f32[8,16,2,128]{3,2,0,1:T(2,128)}), f32[8,16,2,128]{3,2,0,1:T(2,128)S(1)}, u32[]{:S(2)}, u32[]{:S(2)}) async-start(f32[8,16,2,128]{3,2,0,1:T(2,128)} %copy.187), calls=%async_computation | async-start | bytes 262144 | tf_op jit(solution)/shard_map/while/body/eval_jaxpr/all_to_all | solution.py:108
  397.3 10.1 %all-to-all-done = f32[8,16,2,128]{3,2,0,1:T(2,128)S(1)} async-done(((f32[8,16,2,128]{3,2,0,1:T(2,128)}), f32[8,16,2,128]{3,2,0,1:T(2,128)S(1)}, u32[]{:S(2)}, u32[]{:S(2)}) %all-to-all-start) | async-done | bytes 131104 | tf_op jit(solution)/shard_map/while/body/eval_jaxpr/all_to_all | solution.py:108
  415.7 8.3 all-to-all-done.1
  427.3 5.5 convolution_add_fusion.4
  432.7 4.7 convolution_add_fusion.5
  455.5 4.5 collective-permute-done.2
  460.0 4.6 collective-permute-done.3
  465.9 13.9 %all-to-all-start = ((f32[8,16,2,128]{3,2,0,1:T(2,128)}), f32[8,16,2,128]{3,2,0,1:T(2,128)S(1)}, u32[]{:S(2)}, u32[]{:S(2)}) async-start(f32[8,16,2,128]{3,2,0,1:T(2,128)} %copy.187), calls=%async_computation | async-start | bytes 262144 | tf_op jit(solution)/shard_map/while/body/eval_jaxpr/all_to_all | solution.py:108
  479.9 10.1 %all-to-all-done = f32[8,16,2,128]{3,2,0,1:T(2,128)S(1)} async-done(((f32[8,16,2,128]{3,2,0,1:T(2,128)}), f32[8,16,2,128]{3,2,0,1:T(2,128)S(1)}, u32[]{:S(2)}, u32[]{:S(2)}) %all-to-all-start) | async-done | bytes 131104 | tf_op jit(solution)/shard_map/while/body/eval_jaxpr/all_to_all | solution.py:108
  498.3 8.3 all-to-all-done.1
  510.0 5.5 convolution_add_fusion.4
  515.4 4.7 convolution_add_fusion.5
  538.2 4.5 collective-permute-done.2
  542.7 4.6 collective-permute-done.3
  548.6 13.9 %all-to-all-start = ((f32[8,16,2,128]{3,2,0,1:T(2,128)}), f32[8,16,2,128]{3,2,0,1:T(2,128)S(1)}, u32[]{:S(2)}, u32[]{:S(2)}) async-start(f32[8,16,2,128]{3,2,0,1:T(2,128)} %copy.187), calls=%async_computation | async-start | bytes 262144 | tf_op jit(solution)/shard_map/while/body/eval_jaxpr/all_to_all | solution.py:108
  562.6 10.1 %all-to-all-done = f32[8,16,2,128]{3,2,0,1:T(2,128)S(1)} async-done(((f32[8,16,2,128]{3,2,0,1:T(2,128)}), f32[8,16,2,128]{3,2,0,1:T(2,128)S(1)}, u32[]{:S(2)}, u32[]{:S(2)}) %all-to-all-start) | async-done | bytes 131104 | tf_op jit(solution)/shard_map/while/body/eval_jaxpr/all_to_all | solution.py:108
  581.0 8.3 all-to-all-done.1
  592.6 5.4 convolution_add_fusion.4
  598.1 4.7 convolution_add_fusion.5
  620.8 4.5 collective-permute-done.2
  625.3 4.6 collective-permute-done.3
  631.3 13.9 %all-to-all-start = ((f32[8,16,2,128]{3,2,0,1:T(2,128)}), f32[8,16,2,128]{3,2,0,1:T(2,128)S(1)}, u32[]{:S(2)}, u32[]{:S(2)}) async-start(f32[8,16,2,128]{3,2,0,1:T(2,128)} %copy.187), calls=%async_computation | async-start | bytes 262144 | tf_op jit(solution)/shard_map/while/body/eval_jaxpr/all_to_all | solution.py:108
  645.3 10.1 %all-to-all-done = f32[8,16,2,128]{3,2,0,1:T(2,128)S(1)} async-done(((f32[8,16,2,128]{3,2,0,1:T(2,128)}), f32[8,16,2,128]{3,2,0,1:T(2,128)S(1)}, u32[]{:S(2)}, u32[]{:S(2)}) %all-to-all-start) | async-done | bytes 131104 | tf_op jit(solution)/shard_map/while/body/eval_jaxpr/all_to_all | solution.py:108
  663.7 8.3 all-to-all-done.1
  675.3 5.5 convolution_add_fusion.4
  680.7 4.7 convolution_add_fusion.5
  688.8 18.0 %all_to_all.83 = f32[4,2,128,2,128]{2,4,3,1,0:T(8,128)S(1)} all-to-all(f32[4,2,128,2,128]{2,4,3,1,0:T(8,128)S(1)} %copy-done.4), channel_id=1, replica_groups=mesh['section'=4,'tile'=16,'col'=4] {'section'}, dimensions={0} | all-to-all | bytes 2097152 | tf_op jit(solution)/shard_map/all_to_all | solution.py:159
  708.1 243.1 %all-reduce.3.cloned.1.call-done = (f32[4096,128]{1,0:T(8,128)}, f32[128,4096]{1,0:T(8,128)}) async-done(((f32[4096,128]{1,0:T(8,128)}, f32[128,4096]{1,0:T(8,128)}), (f32[4096,128]{1,0:T(8,128)}, f32[128,4096]{1,0:T(8,128)})) %all-reduce.3.cloned.1.call-update) | async-done | bytes 4194320 | tf_op jit(solution)/shard_map/psum | solution.py:162
  (655 shorter events, 235.1 us)
Async XLA Ops:
  7.2 2.4 copy-start
  7.2 10.4 %copy-start.8 = (s32[2,128]{1,0:T(2,128)S(1)}, s32[2,128]{1,0:T(2,128)}, u32[]{:S(2)}) copy-start(s32[2,128]{1,0:T(2,128)} %param.23) | copy-start | bytes 3076
  7.2 10.4 %copy-start.6 = (s32[2,128]{1,0:T(2,128)S(1)}, s32[2,128]{1,0:T(2,128)}, u32[]{:S(2)}) copy-start(s32[2,128]{1,0:T(2,128)} %param.24) | copy-start | bytes 3076
  9.6 16.1 %copy-start.2 = (bf16[128,4096]{1,0:T(8,128)(2,1)S(1)}, bf16[128,4096]{1,0:T(8,128)(2,1)}, u32[]{:S(2)}) copy-start(bf16[128,4096]{1,0:T(8,128)(2,1)} %param.20) | copy-start | bytes 3145732
  9.6 16.1 %copy-start.3 = (bf16[4096,128]{1,0:T(8,128)(2,1)S(1)}, bf16[4096,128]{1,0:T(8,128)(2,1)}, u32[]{:S(2)}) copy-start(bf16[4096,128]{1,0:T(8,128)(2,1)} %param.19) | copy-start | bytes 3145732
  9.6 16.1 %copy-start.7 = (f32[128]{0:T(128)S(1)}, f32[128]{0:T(128)}, u32[]{:S(2)}) copy-start(f32[128]{0:T(128)} %param.21) | copy-start | bytes 1540
  9.6 16.1 %copy-start.9 = (s32[8]{0:T(128)S(1)}, s32[8]{0:T(128)}, u32[]{:S(2)}) copy-start(s32[8]{0:T(128)} %param.25) | copy-start | bytes 100
  9.6 16.1 %copy-start.10 = (s32[5]{0:T(128)S(1)}, s32[5]{0:T(128)}, u32[]{:S(2)}) copy-start(s32[5]{0:T(128)} %constant.317.clone.3) | copy-start | bytes 64
  12.6 12.1 %all-to-all-start.2 = ((bf16[1,8,128,2,128]{4,3,2,0,1:T(2,128)(2,1)}), bf16[1,8,128,2,128]{4,3,2,0,1:T(2,128)(2,1)}, u32[]{:S(2)}, u32[]{:S(2)}) async-start(bf16[1,8,128,2,128]{4,3,2,0,1:T(2,128)(2,1)} %broadcast_select_fusion.1), calls=%async_computation.2 | async-start | bytes 1048576 | tf_op jit(solution)/shard_map/all_to_all | solution.py:136
  17.6 933.6 %all-reduce.3.cloned.1.call-start = ((), (), s32[]{:S(2)}) async-start(), calls=%async_computation.4 | async-start | bytes 8388608 | tf_op jit(solution)/shard_map/psum | solution.py:162
  29.5 9.8 %collective-permute-start = (f32[128,1,128]{2,0,1:T(8,128)S(1)}, f32[128,1,128]{2,0,1:T(8,128)S(1)}, u32[]{:S(2)}, u32[]{:S(2)}) collective-permute-start(f32[128,1,128]{2,0,1:T(8,128)S(1)} %get-tuple-element.1042), channel_id=1, source_target_pairs={{4,0},{8,4},{12,8},{16,12},{20,16},{24,20},{28,24},{32,28},{36,32}... | collective-permute-start | bytes 196616 | tf_op jit(solution)/shard_map/while/body/eval_jaxpr/ppermute | solution.py:21
  34.8 4.5 collective-permute-start.1
  39.5 9.5 collective-permute-start.2
  43.0 10.3 %collective-permute-start.3 = (f32[128,4,1]{2,0,1:T(8,128)S(1)}, f32[128,4,1]{2,0,1:T(8,128)S(1)}, u32[]{:S(2)}, u32[]{:S(2)}) collective-permute-start(f32[128,4,1]{2,0,1:T(8,128)S(1)} %get-tuple-element.1045), channel_id=1, source_target_pairs={{1,0},{2,1},{3,2},{5,4},{6,5},{7,6},{9,8},{10,9},{11,10},{13,12},{... | collective-permute-start | bytes 6152 | tf_op jit(solution)/shard_map/while/body/eval_jaxpr/ppermute | solution.py:21
  54.7 23.6 %all-to-all-start = ((f32[8,16,2,128]{3,2,0,1:T(2,128)}), f32[8,16,2,128]{3,2,0,1:T(2,128)S(1)}, u32[]{:S(2)}, u32[]{:S(2)}) async-start(f32[8,16,2,128]{3,2,0,1:T(2,128)} %copy.187), calls=%async_computation | async-start | bytes 262144 | tf_op jit(solution)/shard_map/while/body/eval_jaxpr/all_to_all | solution.py:108
  80.8 14.0 %all-to-all-start.1 = ((f32[8,1,32,128]{3,0,1,2:T(8,128)}), f32[8,1,32,128]{3,0,1,2:T(8,128)S(1)}, u32[]{:S(2)}, u32[]{:S(2)}) async-start(f32[8,1,32,128]{3,0,1,2:T(8,128)} %maximum_bitcast_fusion.2), calls=%async_computation.1 | async-start | bytes 262144 | tf_op jit(solution)/shard_map/while/body/eval_jaxpr/all_to_all | solution.py:88
  96.1 2.0 copy-start.1
  112.7 7.0 collective-permute-start
  115.4 4.3 collective-permute-start.1
  119.9 10.6 %collective-permute-start.2 = (f32[128,4,1]{2,0,1:T(8,128)S(1)}, f32[128,4,1]{2,0,1:T(8,128)S(1)}, u32[]{:S(2)}, u32[]{:S(2)}) collective-permute-start(f32[128,4,1]{2,0,1:T(8,128)S(1)} %get-tuple-element.1044), channel_id=1, source_target_pairs={{0,1},{1,2},{2,3},{4,5},{5,6},{6,7},{8,9},{9,10},{10,11},{12,13},{... | collective-permute-start | bytes 6152 | tf_op jit(solution)/shard_map/while/body/eval_jaxpr/ppermute | solution.py:18
  124.5 10.1 %collective-permute-start.3 = (f32[128,4,1]{2,0,1:T(8,128)S(1)}, f32[128,4,1]{2,0,1:T(8,128)S(1)}, u32[]{:S(2)}, u32[]{:S(2)}) collective-permute-start(f32[128,4,1]{2,0,1:T(8,128)S(1)} %get-tuple-element.1045), channel_id=1, source_target_pairs={{1,0},{2,1},{3,2},{5,4},{6,5},{7,6},{9,8},{10,9},{11,10},{13,12},{... | collective-permute-start | bytes 6152 | tf_op jit(solution)/shard_map/while/body/eval_jaxpr/ppermute | solution.py:21
  135.9 23.4 %all-to-all-start = ((f32[8,16,2,128]{3,2,0,1:T(2,128)}), f32[8,16,2,128]{3,2,0,1:T(2,128)S(1)}, u32[]{:S(2)}, u32[]{:S(2)}) async-start(f32[8,16,2,128]{3,2,0,1:T(2,128)} %copy.187), calls=%async_computation | async-start | bytes 262144 | tf_op jit(solution)/shard_map/while/body/eval_jaxpr/all_to_all | solution.py:108
  161.8 14.2 %all-to-all-start.1 = ((f32[8,1,32,128]{3,0,1,2:T(8,128)}), f32[8,1,32,128]{3,0,1,2:T(8,128)S(1)}, u32[]{:S(2)}, u32[]{:S(2)}) async-start(f32[8,1,32,128]{3,0,1,2:T(8,128)} %maximum_bitcast_fusion.2), calls=%async_computation.1 | async-start | bytes 262144 | tf_op jit(solution)/shard_map/while/body/eval_jaxpr/all_to_all | solution.py:88
  177.3 2.0 copy-start.1
  195.3 7.0 collective-permute-start
  197.8 4.4 collective-permute-start.1
  202.4 9.5 collective-permute-start.2
  205.8 10.7 %collective-permute-start.3 = (f32[128,4,1]{2,0,1:T(8,128)S(1)}, f32[128,4,1]{2,0,1:T(8,128)S(1)}, u32[]{:S(2)}, u32[]{:S(2)}) collective-permute-start(f32[128,4,1]{2,0,1:T(8,128)S(1)} %get-tuple-element.1045), channel_id=1, source_target_pairs={{1,0},{2,1},{3,2},{5,4},{6,5},{7,6},{9,8},{10,9},{11,10},{13,12},{... | collective-permute-start | bytes 6152 | tf_op jit(solution)/shard_map/while/body/eval_jaxpr/ppermute | solution.py:21
  217.9 24.1 %all-to-all-start = ((f32[8,16,2,128]{3,2,0,1:T(2,128)}), f32[8,16,2,128]{3,2,0,1:T(2,128)S(1)}, u32[]{:S(2)}, u32[]{:S(2)}) async-start(f32[8,16,2,128]{3,2,0,1:T(2,128)} %copy.187), calls=%async_computation | async-start | bytes 262144 | tf_op jit(solution)/shard_map/while/body/eval_jaxpr/all_to_all | solution.py:108
  244.5 14.2 %all-to-all-start.1 = ((f32[8,1,32,128]{3,0,1,2:T(8,128)}), f32[8,1,32,128]{3,0,1,2:T(8,128)S(1)}, u32[]{:S(2)}, u32[]{:S(2)}) async-start(f32[8,1,32,128]{3,0,1,2:T(8,128)} %maximum_bitcast_fusion.2), calls=%async_computation.1 | async-start | bytes 262144 | tf_op jit(solution)/shard_map/while/body/eval_jaxpr/all_to_all | solution.py:88
  277.9 7.0 collective-permute-start
  280.5 4.4 collective-permute-start.1
  285.1 9.6 collective-permute-start.2
  288.6 10.7 %collective-permute-start.3 = (f32[128,4,1]{2,0,1:T(8,128)S(1)}, f32[128,4,1]{2,0,1:T(8,128)S(1)}, u32[]{:S(2)}, u32[]{:S(2)}) collective-permute-start(f32[128,4,1]{2,0,1:T(8,128)S(1)} %get-tuple-element.1045), channel_id=1, source_target_pairs={{1,0},{2,1},{3,2},{5,4},{6,5},{7,6},{9,8},{10,9},{11,10},{13,12},{... | collective-permute-start | bytes 6152 | tf_op jit(solution)/shard_map/while/body/eval_jaxpr/ppermute | solution.py:21
  300.6 24.1 %all-to-all-start = ((f32[8,16,2,128]{3,2,0,1:T(2,128)}), f32[8,16,2,128]{3,2,0,1:T(2,128)S(1)}, u32[]{:S(2)}, u32[]{:S(2)}) async-start(f32[8,16,2,128]{3,2,0,1:T(2,128)} %copy.187), calls=%async_computation | async-start | bytes 262144 | tf_op jit(solution)/shard_map/while/body/eval_jaxpr/all_to_all | solution.py:108
  327.1 14.2 %all-to-all-start.1 = ((f32[8,1,32,128]{3,0,1,2:T(8,128)}), f32[8,1,32,128]{3,0,1,2:T(8,128)S(1)}, u32[]{:S(2)}, u32[]{:S(2)}) async-start(f32[8,1,32,128]{3,0,1,2:T(8,128)} %maximum_bitcast_fusion.2), calls=%async_computation.1 | async-start | bytes 262144 | tf_op jit(solution)/shard_map/while/body/eval_jaxpr/all_to_all | solution.py:88
  360.6 7.0 collective-permute-start
  363.2 4.4 collective-permute-start.1
  367.8 9.5 collective-permute-start.2
  371.2 10.7 %collective-permute-start.3 = (f32[128,4,1]{2,0,1:T(8,128)S(1)}, f32[128,4,1]{2,0,1:T(8,128)S(1)}, u32[]{:S(2)}, u32[]{:S(2)}) collective-permute-start(f32[128,4,1]{2,0,1:T(8,128)S(1)} %get-tuple-element.1045), channel_id=1, source_target_pairs={{1,0},{2,1},{3,2},{5,4},{6,5},{7,6},{9,8},{10,9},{11,10},{13,12},{... | collective-permute-start | bytes 6152 | tf_op jit(solution)/shard_map/while/body/eval_jaxpr/ppermute | solution.py:21
  383.3 24.1 %all-to-all-start = ((f32[8,16,2,128]{3,2,0,1:T(2,128)}), f32[8,16,2,128]{3,2,0,1:T(2,128)S(1)}, u32[]{:S(2)}, u32[]{:S(2)}) async-start(f32[8,16,2,128]{3,2,0,1:T(2,128)} %copy.187), calls=%async_computation | async-start | bytes 262144 | tf_op jit(solution)/shard_map/while/body/eval_jaxpr/all_to_all | solution.py:108
  409.8 14.2 %all-to-all-start.1 = ((f32[8,1,32,128]{3,0,1,2:T(8,128)}), f32[8,1,32,128]{3,0,1,2:T(8,128)S(1)}, u32[]{:S(2)}, u32[]{:S(2)}) async-start(f32[8,1,32,128]{3,0,1,2:T(8,128)} %maximum_bitcast_fusion.2), calls=%async_computation.1 | async-start | bytes 262144 | tf_op jit(solution)/shard_map/while/body/eval_jaxpr/all_to_all | solution.py:88
  425.3 2.0 copy-start.1
  443.3 7.0 collective-permute-start
  445.9 4.4 collective-permute-start.1
  450.4 9.5 collective-permute-start.2
  453.9 10.7 %collective-permute-start.3 = (f32[128,4,1]{2,0,1:T(8,128)S(1)}, f32[128,4,1]{2,0,1:T(8,128)S(1)}, u32[]{:S(2)}, u32[]{:S(2)}) collective-permute-start(f32[128,4,1]{2,0,1:T(8,128)S(1)} %get-tuple-element.1045), channel_id=1, source_target_pairs={{1,0},{2,1},{3,2},{5,4},{6,5},{7,6},{9,8},{10,9},{11,10},{13,12},{... | collective-permute-start | bytes 6152 | tf_op jit(solution)/shard_map/while/body/eval_jaxpr/ppermute | solution.py:21
  465.9 24.1 %all-to-all-start = ((f32[8,16,2,128]{3,2,0,1:T(2,128)}), f32[8,16,2,128]{3,2,0,1:T(2,128)S(1)}, u32[]{:S(2)}, u32[]{:S(2)}) async-start(f32[8,16,2,128]{3,2,0,1:T(2,128)} %copy.187), calls=%async_computation | async-start | bytes 262144 | tf_op jit(solution)/shard_map/while/body/eval_jaxpr/all_to_all | solution.py:108
  492.5 14.2 %all-to-all-start.1 = ((f32[8,1,32,128]{3,0,1,2:T(8,128)}), f32[8,1,32,128]{3,0,1,2:T(8,128)S(1)}, u32[]{:S(2)}, u32[]{:S(2)}) async-start(f32[8,1,32,128]{3,0,1,2:T(8,128)} %maximum_bitcast_fusion.2), calls=%async_computation.1 | async-start | bytes 262144 | tf_op jit(solution)/shard_map/while/body/eval_jaxpr/all_to_all | solution.py:88
  525.9 7.0 collective-permute-start
  528.5 4.4 collective-permute-start.1
  533.1 9.6 collective-permute-start.2
  536.6 10.7 %collective-permute-start.3 = (f32[128,4,1]{2,0,1:T(8,128)S(1)}, f32[128,4,1]{2,0,1:T(8,128)S(1)}, u32[]{:S(2)}, u32[]{:S(2)}) collective-permute-start(f32[128,4,1]{2,0,1:T(8,128)S(1)} %get-tuple-element.1045), channel_id=1, source_target_pairs={{1,0},{2,1},{3,2},{5,4},{6,5},{7,6},{9,8},{10,9},{11,10},{13,12},{... | collective-permute-start | bytes 6152 | tf_op jit(solution)/shard_map/while/body/eval_jaxpr/ppermute | solution.py:21
  548.6 24.1 %all-to-all-start = ((f32[8,16,2,128]{3,2,0,1:T(2,128)}), f32[8,16,2,128]{3,2,0,1:T(2,128)S(1)}, u32[]{:S(2)}, u32[]{:S(2)}) async-start(f32[8,16,2,128]{3,2,0,1:T(2,128)} %copy.187), calls=%async_computation | async-start | bytes 262144 | tf_op jit(solution)/shard_map/while/body/eval_jaxpr/all_to_all | solution.py:108
  575.1 14.2 %all-to-all-start.1 = ((f32[8,1,32,128]{3,0,1,2:T(8,128)}), f32[8,1,32,128]{3,0,1,2:T(8,128)S(1)}, u32[]{:S(2)}, u32[]{:S(2)}) async-start(f32[8,1,32,128]{3,0,1,2:T(8,128)} %maximum_bitcast_fusion.2), calls=%async_computation.1 | async-start | bytes 262144 | tf_op jit(solution)/shard_map/while/body/eval_jaxpr/all_to_all | solution.py:88
  590.7 2.0 copy-start.1
  608.6 7.0 collective-permute-start
  611.2 4.4 collective-permute-start.1
  615.8 9.5 collective-permute-start.2
  619.2 10.7 %collective-permute-start.3 = (f32[128,4,1]{2,0,1:T(8,128)S(1)}, f32[128,4,1]{2,0,1:T(8,128)S(1)}, u32[]{:S(2)}, u32[]{:S(2)}) collective-permute-start(f32[128,4,1]{2,0,1:T(8,128)S(1)} %get-tuple-element.1045), channel_id=1, source_target_pairs={{1,0},{2,1},{3,2},{5,4},{6,5},{7,6},{9,8},{10,9},{11,10},{13,12},{... | collective-permute-start | bytes 6152 | tf_op jit(solution)/shard_map/while/body/eval_jaxpr/ppermute | solution.py:21
  631.3 24.1 %all-to-all-start = ((f32[8,16,2,128]{3,2,0,1:T(2,128)}), f32[8,16,2,128]{3,2,0,1:T(2,128)S(1)}, u32[]{:S(2)}, u32[]{:S(2)}) async-start(f32[8,16,2,128]{3,2,0,1:T(2,128)} %copy.187), calls=%async_computation | async-start | bytes 262144 | tf_op jit(solution)/shard_map/while/body/eval_jaxpr/all_to_all | solution.py:108
  657.8 14.2 %all-to-all-start.1 = ((f32[8,1,32,128]{3,0,1,2:T(8,128)}), f32[8,1,32,128]{3,0,1,2:T(8,128)S(1)}, u32[]{:S(2)}, u32[]{:S(2)}) async-start(f32[8,1,32,128]{3,0,1,2:T(8,128)} %maximum_bitcast_fusion.2), calls=%async_computation.1 | async-start | bytes 262144 | tf_op jit(solution)/shard_map/while/body/eval_jaxpr/all_to_all | solution.py:88
  673.3 2.0 copy-start.1
  951.2 3.2 copy-start.5
  (4 other events, 7.1 us)
Sparse Core Ops, SparseCore 0:
  687.8 263.4 all-reduce.2
where the time goes:
time: 967 us; the launch traced here: 963 us
  waiting for transfers between devices  469 us (49%)
  starting transfers between devices  233 us (24%)
  matrix products  98.2 us (10%)
  other arithmetic  60.1 us (6%)
  local copies, waits for them, and re-layouts  52.1 us (5%)
  blocking collectives  18 us (2%)
  loops' own time  17.6 us (2%)
  between operations  14.2 us (1%)
    psum x1, waiting for transfers between devices, local(): lax.psum((grad_in, grad_out), ('section', 'tile', 'col'))  243 us
    all_to_all x8, starting transfers between devices, dynamics(): lax.all_to_all(modal_fields, 'tile', split_axis=1, concat_axis=2, tiled=T...  110 us
    all_to_all x8, waiting for transfers between devices, dynamics(): lax.all_to_all(modal_fields, 'tile', split_axis=1, concat_axis=2, tiled=T...  80.7 us
    dot_general x16, matrix products, contract_rows(): lax.dot_general(left_operand, right_operand, (((1,), (1,)), ((), ())), pr...  79.6 us
    all_to_all x8, waiting for transfers between devices, solve_items(): lax.all_to_all(solved.reshape(modal_piece.shape), 'tile', split_axis=2, c...  66.3 us
    ppermute x16, starting transfers between devices, with_halo(): lax.ppermute(lax.slice_in_dim(block, block.shape[dim] - width, None, axis...  52.5 us
    ppermute x16, waiting for transfers between devices, with_halo(): lax.ppermute(lax.slice_in_dim(block, 0, width, axis=dim), axis, backward)  36 us
    ppermute x16, waiting for transfers between devices, with_halo(): lax.ppermute(lax.slice_in_dim(block, block.shape[dim] - width, None, axis...  35.9 us
  transfers between devices with their start and end apart: 50, of which 34 were waited for; matrix products, arithmetic and copies ran while one was open for 3% of the time, Pallas kernels for 0%

commit v1 on v0

v1 whole, which is shorter than its diff:
```python
import math

import jax
import jax.numpy as jnp
import numpy as np
from jax import lax
from jax.experimental import pallas as pl
from jax.experimental.pallas import tpu as pltpu
from jax.sharding import Mesh, PartitionSpec as P

V = 8
L = 16
H = 4096
F = 128
STEPS = 4
MB = 8
NX = 32
NY = 512
CHUNK = 16
HALO = STEPS
SLAB = CHUNK + 2 * HALO
MSG = 48
CODE = 32000.0
UNIT = 32768.0 / CODE
OWN = NX * CHUNK
COLS = STEPS * OWN
HB1 = 512
HB2 = 256
HALF = H // 2
GRAD_SCALE = 1.0 / math.sqrt(MB * STEPS * NX * NY)
TILE = ("zh", "cx", "core")
COL = ("c1", "c0")
SPREAD = ("sec", "cx", "c0")
PARTS = 32
ROWS = H // 2 // PARTS


def mode_block():
    order = np.arange(L)
    angles = np.pi * (order[None, :] + 0.5) * order[:, None] / L
    weights = np.where(order[:, None] == 0, math.sqrt(1.0 / L), math.sqrt(2.0 / L))
    return np.kron(np.eye(V), np.cos(angles) * weights).astype(np.float32)


def params(semantics=None, mib=60):
    return pltpu.CompilerParams(dimension_semantics=semantics, vmem_limit_bytes=mib * 2**20)


def exponent(largest):
    return jnp.ceil(jnp.log(jnp.maximum(largest, 1e-30)) * (1.0 / math.log(2.0)) + 0.01)


def encode(value, power):
    scaled = value * (jnp.exp2(15.0 - power) * (1.0 / UNIT))
    return jnp.round(jnp.clip(scaled, -32767.0, 32767.0))


def to_int16(value):
    return value.astype(jnp.int32).astype(jnp.int16)


def to_float(code):
    return code.astype(jnp.int32).astype(jnp.float32)


def decode(value, power):
    return value * (jnp.exp2(power - 15.0) * UNIT)


def init_kernel(meta_ref, plan_ref, state_ref, land_ref, levels_ref, msg_ref):
    power = exponent(jnp.max(jnp.abs(state_ref[0]), keepdims=True))
    code = [encode(state_ref[0, pl.ds(x, F, stride=2), :], power).T for x in range(2)]
    depth = jnp.where(land_ref[...] == 1, levels_ref[...], 0).astype(jnp.float32)
    extra = jnp.concatenate(
        [depth, jnp.broadcast_to(power, (1, 128)), jnp.zeros((5, 128), jnp.float32)], axis=0
    )
    for j in range(8):
        y = CHUNK * j
        first = [c[y : y + HALO] for c in code]
        middle = [c[y + HALO : y + CHUNK - HALO] for c in code]
        last = [c[y + CHUNK - HALO : y + CHUNK] for c in code]
        msg_ref[j] = to_int16(jnp.concatenate(first + [extra] + middle + last + [extra], axis=0))


def init_slabs(meta, plan, states, land_mask, wet_levels):
    whole = lambda i, meta, plan: (0, 0)
    return pl.pallas_call(
        init_kernel,
        grid_spec=pltpu.PrefetchScalarGridSpec(
            num_scalar_prefetch=2,
            grid=(2,),
            in_specs=[
                pl.BlockSpec((1, 2 * F, 128), lambda i, meta, plan: (plan[2 * meta[0] + i], 0, 0)),
                pl.BlockSpec((2, 128), whole),
                pl.BlockSpec((2, 128), whole),
            ],
            out_specs=pl.BlockSpec((8, MSG, F), lambda i, meta, plan: (i, 0, 0)),
        ),
        out_shape=jax.ShapeDtypeStruct((16, MSG, F), jnp.int16),
        compiler_params=params(("arbitrary",)),
        name="init_slabs",
    )(meta, plan, states, land_mask, wet_levels)


def levels():
    return (lax.broadcasted_iota(jnp.int32, (1, F), 1) % L).astype(jnp.float32)


def rollout_kernel(
    meta_ref, msg_ref, left_ref, right_ref, w_in_t, w_out_t, mode_ref, mode_t, diff_ref, stiff_ref,
    traj_ref, inputs_ref, tend_ref, own_wet_ref,
    state, wet, modal, acc, x_scr, gain, pull, depth, depth_t,
):
    for t in range(16):
        for n, (ref, base) in enumerate(
            ((msg_ref, 0), (msg_ref, 16), (msg_ref, 32), (right_ref, 0), (left_ref, 0))
        ):
            piece = to_float(ref[t, base : base + 16])
            if n != 1:
                scale = decode(1.0, piece[10:11])
            rows = 8 if n == 1 else HALO
            at = (0, HALO, CHUNK - HALO, CHUNK, CHUNK + HALO)[n]
            for x in range(2):
                state[2 * t + x, at : at + rows] = piece[x * rows : (x + 1) * rows] * scale
            if n in (0, 3, 4):
                depth[n // 2 if n else 0, 2 * t : 2 * t + 2] = piece[8:10]
    for n in range(3):
        depth_t[n] = depth[n].T
    mine = meta_ref[1]
    y_own = pl.multiple_of(mine * CHUNK, CHUNK)
    y_right = pl.multiple_of(lax.rem(mine + 1, 8) * CHUNK, CHUNK)
    y_left = pl.multiple_of(lax.rem(mine + 7, 8) * CHUNK + 8, 8)
    here = jnp.concatenate(
        [
            depth_t[0, pl.ds(y_own, CHUNK)],
            depth_t[1, pl.ds(y_right, 8)][:HALO],
            depth_t[2, pl.ds(y_left, 8)][8 - HALO :],
        ],
        axis=0,
    )
    level = levels()
    for x in range(NX):
        wet[x] = jnp.where(level < here[:, x : x + 1], 1.0, 0.0)
    own_wet_ref[...] = wet[:, :CHUNK]

    a = stiff_ref[...]
    u = 1.0 + a
    for i in range(NX):
        r = 1.0 / (a + u)
        gain[pl.ds(i, 1), :] = r
        pull[pl.ds(i, 1), :] = a * r
        u = 1.0 + a * (u * r)
    diff = diff_ref[...].reshape(1, 1, F)
    edge = jnp.zeros((1, SLAB, F), jnp.float32)
    for step in range(STEPS):
        now = state[...]
        around = (
            jnp.concatenate([edge, now[:-1]], axis=0)
            + jnp.concatenate([now[1:], edge], axis=0)
            + pltpu.roll(now, 1, 1)
            + pltpu.roll(now, SLAB - 1, 1)
            - 4.0 * now
        )
        smoothed = wet[...] * (now + diff * around)
        modal[...] = jnp.dot(
            smoothed.reshape(NX * SLAB, F),
            mode_t[...],
            precision=lax.Precision.HIGHEST,
            preferred_element_type=jnp.float32,
        ).reshape(NX, SLAB, F)
        part = modal[0] * gain[pl.ds(0, 1), :]
        modal[0] = part
        for i in range(1, NX):
            part = modal[i] * gain[pl.ds(i, 1), :] + pull[pl.ds(i, 1), :] * part
            modal[i] = part
        for i in range(NX - 2, -1, -1):
            part = modal[i] + pull[pl.ds(i, 1), :] * part
            modal[i] = part
        after = wet[...] * jnp.dot(
            modal[...].reshape(NX * SLAB, F),
            mode_ref[...],
            precision=lax.Precision.HIGHEST,
            preferred_element_type=jnp.float32,
        ).reshape(NX, SLAB, F)
        rows = SLAB if step < STEPS - 1 else CHUNK
        after = after[:, :rows]
        state[:, :rows] = after
        x_scr[0 : NX * rows] = after.reshape(NX * rows, F).astype(jnp.bfloat16)
        inputs_ref[step] = after[:, :CHUNK].astype(jnp.bfloat16)
        acc[0 : NX * rows] = jnp.zeros((NX * rows, F), jnp.float32)

        def block(b, carry, rows=rows):
            at = pl.multiple_of(b * HB1, HB1)
            hidden = jnp.tanh(
                jnp.dot(
                    x_scr[0 : NX * rows],
                    w_in_t[:, pl.ds(at, HB1)],
                    preferred_element_type=jnp.float32,
                )
            ).astype(jnp.bfloat16)
            acc[0 : NX * rows] += jnp.dot(
                hidden, w_out_t[pl.ds(at, HB1), :], preferred_element_type=jnp.float32
            )
            return carry

        lax.fori_loop(0, H // HB1, block, 0, unroll=2)
        tendency = acc[0 : NX * rows].reshape(NX, rows, F)
        result = wet[:, :rows] * (state[:, :rows] + tendency)
        state[:, :rows] = result
        traj_ref[step] = result[:, :CHUNK].astype(jnp.bfloat16)
        tend_ref[step] = tendency[:, :CHUNK]


def rollout(meta, msg, left, right, w_in_t, w_out_t, diffusivity, stiffness):
    block = mode_block()
    vmem = pl.BlockSpec(memory_space=pltpu.VMEM)
    return pl.pallas_call(
        rollout_kernel,
        out_shape=[
            jax.ShapeDtypeStruct((STEPS, NX, CHUNK, F), jnp.bfloat16),
            jax.ShapeDtypeStruct((STEPS, NX, CHUNK, F), jnp.bfloat16),
            jax.ShapeDtypeStruct((STEPS, NX, CHUNK, F), jnp.float32),
            jax.ShapeDtypeStruct((NX, CHUNK, F), jnp.float32),
        ],
        in_specs=[pl.BlockSpec(memory_space=pltpu.SMEM)] + [vmem] * 9,
        out_specs=[vmem] * 4,
        scratch_shapes=[
            pltpu.VMEM((NX, SLAB, F), jnp.float32),
            pltpu.VMEM((NX, SLAB, F), jnp.float32),
            pltpu.VMEM((NX, SLAB, F), jnp.float32),
            pltpu.VMEM((NX * SLAB, F), jnp.float32),
            pltpu.VMEM((NX * SLAB, F), jnp.bfloat16),
            pltpu.VMEM((NX, F), jnp.float32),
            pltpu.VMEM((NX, F), jnp.float32),
            pltpu.VMEM((3, NX, 128), jnp.float32),
            pltpu.VMEM((3, 128, NX), jnp.float32),
        ],
        compiler_params=params(),
        cost_estimate=pl.CostEstimate(
            flops=4 * 2816 * F * H, bytes_accessed=6 * 2**20, transcendentals=2816 * H
        ),
        name="rollout",
    )(
        meta,
        msg,
        left,
        right,
        w_in_t,
        w_out_t,
        jnp.asarray(block),
        jnp.asarray(np.ascontiguousarray(block.T)),
        diffusivity.reshape(1, F),
        stiffness.reshape(1, F),
    )


def prepare_kernel(plan_ref, target_ref, w_in_ref, w_out_ref, out_ref, w_in_t, w_out_t, wide):
    wide[...] = target_ref[0].astype(jnp.float32)
    for x in range(2):
        t = wide[pl.ds(x, F, stride=2), :].T
        out_ref[0, :, x] = t.reshape(8, CHUNK, F).astype(jnp.bfloat16)
    w_in_t[...] = w_in_ref[...].T
    w_out_t[...] = w_out_ref[...].T


def prepare(targets, w_in, w_out, plan):
    part = H // MB
    down = lambda i, plan: (i, 0)
    along = lambda i, plan: (0, i)
    return pl.pallas_call(
        prepare_kernel,
        grid_spec=pltpu.PrefetchScalarGridSpec(
            num_scalar_prefetch=1,
            grid=(MB,),
            in_specs=[
                pl.BlockSpec((1, 2 * F, 128), lambda i, plan: (plan[i], 0, 0)),
                pl.BlockSpec((part, F), down),
                pl.BlockSpec((F, part), along),
            ],
            out_specs=[
                pl.BlockSpec((1, 8, 2, CHUNK, F), lambda i, plan: (i, 0, 0, 0, 0)),
                pl.BlockSpec((F, part), along),
                pl.BlockSpec((part, F), down),
            ],
            scratch_shapes=[pltpu.VMEM((2 * F, 128), jnp.float32)],
        ),
        out_shape=[
            jax.ShapeDtypeStruct((MB, 8, 2, CHUNK, F), jnp.bfloat16),
            jax.ShapeDtypeStruct((F, H), jnp.bfloat16),
            jax.ShapeDtypeStruct((H, F), jnp.bfloat16),
        ],
        compiler_params=params(),
        cost_estimate=pl.CostEstimate(flops=0, bytes_accessed=6 * 2**20, transcendentals=0),
        name="prepare",
    )(plan, targets, w_in, w_out)


def spread_kernel(in_ref, out_ref):
    for x in range(2):
        block = in_ref[0, :, x].astype(jnp.float32).reshape(128, F)
        out_ref[0, pl.ds(x, F, stride=2), :] = block.T


def spread_trajectory(arrived):
    return pl.pallas_call(
        spread_kernel,
        grid=(MB,),
        in_specs=[pl.BlockSpec((1, 8, 2, CHUNK, F), lambda i: (i, 0, 0, 0, 0))],
        out_specs=pl.BlockSpec((1, 2 * F, 128), lambda i: (i, 0, 0)),
        out_shape=jax.ShapeDtypeStruct((MB, 2 * F, 128), jnp.float32),
        compiler_params=params(),
        name="spread_trajectory",
    )(arrived)


def grad_block(x_ref, x_t, misfit, misfit_t, w_in_ref, w_out_ref):
    width = w_in_ref.shape[1]
    grad_in = jnp.zeros((F, width), jnp.float32)
    grad_out = jnp.zeros((F, width), jnp.float32)
    for part in range(STEPS):
        at = slice(part * OWN, (part + 1) * OWN)
        hidden = jnp.tanh(jnp.dot(x_ref[at], w_in_ref[...], preferred_element_type=jnp.float32))
        grad_out += jnp.dot(
            misfit_t[:, at], hidden.astype(jnp.bfloat16), preferred_element_type=jnp.float32
        )
        back = jnp.dot(misfit[at], w_out_ref[...], preferred_element_type=jnp.float32)
        back = (back * (1.0 - hidden * hidden)).astype(jnp.bfloat16)
        grad_in += jnp.dot(x_t[:, at], back, preferred_element_type=jnp.float32)
    shape = (width // ROWS, ROWS, F)
    return grad_in.T.reshape(shape), grad_out.T.reshape(shape)


def first_kernel(
    half_ref, x_ref, tend_ref, target_ref, wet_ref, w_in_ref, w_out_ref, out_ref, x_t, misfit, misfit_t
):
    @pl.when(pl.program_id(0) == 0)
    def _():
        for step in range(STEPS):
            at = slice(step * OWN, (step + 1) * OWN)
            gap = wet_ref[...] * (tend_ref[at] - target_ref[at].astype(jnp.float32))
            gap = (gap * GRAD_SCALE).astype(jnp.bfloat16)
            misfit[at] = gap
            misfit_t[:, at] = gap.T
            x_t[:, at] = x_ref[at].T

    grad_in, grad_out = grad_block(x_ref, x_t, misfit, misfit_t, w_in_ref, w_out_ref)
    out_ref[:, 0] = grad_in
    out_ref[:, 1] = grad_out


def second_kernel(half_ref, x_ref, x_t, misfit, misfit_t, w_in_ref, w_out_ref, add_ref, out_ref):
    grad_in, grad_out = grad_block(x_ref, x_t, misfit, misfit_t, w_in_ref, w_out_ref)
    out_ref[:, 0] = (grad_in + add_ref[:, 0]).astype(jnp.bfloat16)
    out_ref[:, 1] = (grad_out + add_ref[:, 1]).astype(jnp.bfloat16)


def half_grads(half, columns, w_in_t, w_out, add=None):
    first = add is None
    width = 512 if first else 256
    blocks = HALF // width
    whole = lambda i, half: (0, 0)
    weight = lambda i, half: (0, half[0] * blocks + i)
    rows = pl.BlockSpec((width // ROWS, 2, ROWS, F), lambda i, half: (i, 0, 0, 0))
    in_specs = [pl.BlockSpec(c.shape, whole) for c in columns] + [pl.BlockSpec((F, width), weight)] * 2
    out_specs = [rows]
    out_shape = [jax.ShapeDtypeStruct((PARTS, 2, ROWS, F), jnp.float32 if first else jnp.bfloat16)]
    if first:
        for shape in ((F, COLS), (COLS, F), (F, COLS)):
            out_specs.append(pl.BlockSpec(shape, whole))
            out_shape.append(jax.ShapeDtypeStruct(shape, jnp.bfloat16))
    return pl.pallas_call(
        first_kernel if first else second_kernel,
        grid_spec=pltpu.PrefetchScalarGridSpec(
            num_scalar_prefetch=1,
            grid=(blocks,),
            in_specs=in_specs if first else in_specs + [rows],
            out_specs=out_specs,
        ),
        out_shape=out_shape,
        compiler_params=params(("arbitrary",)),
        cost_estimate=pl.CostEstimate(
            flops=8 * COLS * F * HALF, bytes_accessed=5 * 2**20, transcendentals=COLS * HALF
        ),
        name="first_grads" if first else "second_grads",
    )(half, *columns, w_in_t, w_out, *(() if first else (add,)))


def plane_kernel(in_ref, out_ref):
    total = in_ref[0].astype(jnp.float32)
    for n in range(1, PARTS):
        total += in_ref[n].astype(jnp.float32)
    total = total.astype(jnp.bfloat16)
    for n in range(4):
        out_ref[n] = total


def plane_copies(parts):
    vmem = pl.BlockSpec(memory_space=pltpu.VMEM)
    return pl.pallas_call(
        plane_kernel,
        out_shape=jax.ShapeDtypeStruct((4, 2, ROWS, F), jnp.bfloat16),
        in_specs=[vmem],
        out_specs=vmem,
        compiler_params=params(mib=32),
        name="plane_copies",
    )(parts)


def column_kernel(in_ref, out_ref):
    powers = []
    for g in range(2):
        total = in_ref[0, g].astype(jnp.float32)
        for n in range(1, 4):
            total += in_ref[n, g].astype(jnp.float32)
        power = exponent(jnp.max(jnp.abs(total), axis=0, keepdims=True))
        powers.append(power)
        code = to_int16(encode(total, power))
        for n in range(PARTS):
            out_ref[n, g * ROWS : (g + 1) * ROWS] = code
    tail = to_int16(jnp.concatenate(powers + [jnp.zeros((14, F), jnp.float32)], axis=0))
    for n in range(PARTS):
        out_ref[n, 2 * ROWS : 2 * ROWS + 16] = tail


def column_copies(planes):
    vmem = pl.BlockSpec(memory_space=pltpu.VMEM)
    return pl.pallas_call(
        column_kernel,
        out_shape=jax.ShapeDtypeStruct((PARTS, 2 * ROWS + 16, F), jnp.int16),
        in_specs=[vmem],
        out_specs=vmem,
        compiler_params=params(mib=32),
        name="column_copies",
    )(planes)


def finish_kernel(half_ref, code_ref, *refs):
    grad_in_ref, grad_out_ref = refs[-2:]
    for n in range(0, code_ref.shape[0], 2):
        at = slice(n * ROWS, (n + 2) * ROWS)
        both = []
        for m in (n, n + 1):
            code = to_float(code_ref[m])
            grad_in_ref[m * ROWS : (m + 1) * ROWS] = decode(
                code[0:ROWS], code[2 * ROWS : 2 * ROWS + 1]
            )
            both.append(decode(code[ROWS : 2 * ROWS], code[2 * ROWS + 1 : 2 * ROWS + 2]))
        grad_out_ref[:, at] = jnp.concatenate(both, axis=0).T


def finish_half(half, code, before=()):
    return pl.pallas_call(
        finish_kernel,
        grid_spec=pltpu.PrefetchScalarGridSpec(
            num_scalar_prefetch=1,
            grid=(2,),
            in_specs=[pl.BlockSpec((PARTS // 2, 2 * ROWS + 16, F), lambda i, half: (i, 0, 0))]
            + [pl.BlockSpec(memory_space=pl.ANY)] * len(before),
            out_specs=[
                pl.BlockSpec((1024, F), lambda i, half: (half[0] * 2 + i, 0)),
                pl.BlockSpec((F, 1024), lambda i, half: (0, half[0] * 2 + i)),
            ],
        ),
        out_shape=[
            jax.ShapeDtypeStruct((H, F), jnp.float32),
            jax.ShapeDtypeStruct((F, H), jnp.float32),
        ],
        input_output_aliases={2: 0, 3: 1} if before else {},
        compiler_params=params(("arbitrary",), 32),
        name="finish_half",
    )(half, code, *before)


def swap(value, axes):
    return lax.all_to_all(value, axes, split_axis=0, concat_axis=0, tiled=True)


def local(initial_states, targets, w_in, w_out, diffusivity, stiffness, land_mask, wet_levels, plan):
    core = lax.axis_index("core").astype(jnp.int32).reshape(1)
    meta = jnp.stack([lax.axis_index("sec"), lax.axis_index(TILE) % 8]).astype(jnp.int32)

    states = initial_states.reshape(MB, 2 * F, 128)
    msg = swap(init_slabs(meta, plan, states, land_mask, wet_levels), TILE)
    place = lambda half, chunk, col: (half * 8 + chunk) * 4 + col
    forward = [
        (place(h, j, c), place(h, (j + 1) % 8, c + (j + 1) // 8))
        for h in range(2)
        for j in range(8)
        for c in range(4)
        if c + (j + 1) // 8 < 4
    ]
    left = lax.ppermute(msg[:, 32:48], TILE + COL, forward)
    right = lax.ppermute(msg[:, 0:16], TILE + COL, [(b, a) for a, b in forward])

    target, w_in_t, w_out_t = prepare(targets.reshape(MB, 2 * F, 128), w_in, w_out, plan)
    target = swap(target.reshape(64, 2, CHUNK, F), ("sec",) + TILE).reshape(COLS, F)

    traj, inputs, tend, wet = rollout(meta, msg, left, right, w_in_t, w_out_t, diffusivity, stiffness)
    arrived = swap(traj.reshape(64, 2, CHUNK, F), ("sec",) + TILE)

    inputs = inputs.reshape(COLS, F)
    columns = (inputs, tend.reshape(COLS, F), target, wet.reshape(OWN, F))
    other, *columns = half_grads(1 - core, columns, w_in_t, w_out)
    swapped = lax.ppermute(other, "core", [(0, 1), (1, 0)])
    (pair,) = half_grads(core, (inputs, *columns), w_in_t, w_out, swapped)
    pair, arrived = lax.optimization_barrier((pair, arrived))

    planes = swap(plane_copies(swap(pair, SPREAD)), ("zh", "c1"))
    code = swap(column_copies(planes), SPREAD)
    across = lax.ppermute(code, "core", [(0, 1), (1, 0)])
    grad_in, grad_out = finish_half(1 - core, across, finish_half(core, code))
    trajectory = spread_trajectory(arrived.reshape(MB, 8, 2, CHUNK, F))
    return (trajectory.reshape(1, MB, F, 2, 128), grad_in, grad_out)


def solution(mesh):
    fine = Mesh(mesh.devices.reshape(4, 2, 4, 2, 2, 2), ("sec", "zh", "cx", "core", "c1", "c0"))
    in_specs = (
        P(None, None, TILE, COL),
        P("sec", None, None, TILE, COL),
        P(),
        P(),
        P(),
        P(),
        P(TILE, COL),
        P(TILE, COL),
        P(),
    )
    out_specs = (P("sec", None, None, TILE, COL), P(), P())
    return jax.shard_map(local, mesh=fine, in_specs=in_specs, out_specs=out_specs, check_vma=False)
```

time: 967 us -> 190 us (0.20)
  waiting for transfers between devices: 469 us -> 11.2 us
  starting transfers between devices: 233 us -> 46.1 us
  matrix products: 98.2 us -> 0 us
  Pallas kernels: 0 us -> 71.8 us
  other arithmetic: 60.1 us -> 0.64 us
  local copies, waits for them, and re-layouts: 52.1 us -> 2.73 us
  blocking collectives: 18 us -> 55.8 us
  loops' own time: 17.6 us -> 0 us
  between operations: 14.2 us -> 0.77 us
    psum x1 -> x0, waiting for transfers between devices: 243 us -> none  [local(): lax.psum((grad_in, grad_out), ('section', 'tile', 'col'))]
    all_to_all x17 -> x3, waiting for transfers between devices: 154 us -> 6.42 us  [swap(): return lax.all_to_all(value, axes, split_axis=0, concat_axis=0, tiled=True)]
    all_to_all x17 -> x3, starting transfers between devices: 147 us -> 37.4 us  [swap(): return lax.all_to_all(value, axes, split_axis=0, concat_axis=0, tiled=True)]
    dot_general x48 -> x0, matrix products: 98.2 us -> none  [the longest x16 79.6 us: contract_rows(): lax.dot_general(left_operand, right_operand, (((1,), (1,)), ((), ())), pr...]
    ppermute x32 -> x4, starting transfers between devices: 86.5 us -> 8.69 us  [the longest x1 3.54 us: local(): left = lax.ppermute(msg[:, 32:48], TILE + COL, forward)]
    pallas_call x0 -> x10, Pallas kernels: none -> 71.8 us  [the longest x2 27.4 us: half_grads(): pl.pallas_call(first_kernel if first else second_kernel, grid_spec=pltpu....]
    ppermute x32 -> x4, waiting for transfers between devices: 71.9 us -> 4.79 us  [the longest x1 4.79 us: local(): right = lax.ppermute(msg[:, 0:16], TILE + COL, [(b, a) for a, b in forward])]
    all_to_all x1 -> x3, blocking collectives: 18 us -> 55.8 us  [swap(): return lax.all_to_all(value, axes, split_axis=0, concat_axis=0, tiled=True)]
  transfers between devices with their start and end apart: 50 -> 7, of which waited for: 34 -> 3; matrix products, arithmetic and copies ran while one was open for 3% -> 0% of each run, Pallas kernels for 0% -> 28%
where the time goes in v1:
time: 190 us; the launch traced here: 189 us
  Pallas kernels  71.8 us (38%)
  blocking collectives  55.8 us (29%)
  starting transfers between devices  46.1 us (24%)
  waiting for transfers between devices  11.2 us (6%)
  local copies, waits for them, and re-layouts  2.73 us (1%)
    all_to_all x3, blocking collectives, swap(): return lax.all_to_all(value, axes, split_axis=0, concat_axis=0, tiled=True)  55.8 us
    all_to_all x3, starting transfers between devices, swap(): return lax.all_to_all(value, axes, split_axis=0, concat_axis=0, tiled=True)  37.4 us
    pallas_call x2, Pallas kernels, half_grads(): pl.pallas_call(first_kernel if first else second_kernel, grid_spec=pltpu....  27.4 us
    pallas_call x1, Pallas kernels, rollout(): pl.pallas_call(rollout_kernel, out_shape=[jax.ShapeDtypeStruct((STEPS, NX...  26.3 us
    pallas_call x1, Pallas kernels, prepare(): pl.pallas_call(prepare_kernel, grid_spec=pltpu.PrefetchScalarGridSpec(num...  6.89 us
    all_to_all x3, waiting for transfers between devices, swap(): return lax.all_to_all(value, axes, split_axis=0, concat_axis=0, tiled=True)  6.42 us
    pallas_call x1, Pallas kernels, spread_trajectory(): pl.pallas_call(spread_kernel, grid=(MB,), in_specs=[pl.BlockSpec((1, 8, 2...  5.23 us
    ppermute x1, waiting for transfers between devices, local(): right = lax.ppermute(msg[:, 0:16], TILE + COL, [(b, a) for a, b in forward])  4.79 us
  transfers between devices with their start and end apart: 7, of which 3 were waited for; matrix products, arithmetic and copies ran while one was open for 0% of the time, Pallas kernels for 28%

profile of v1, /device:TPU:1, one launch (start us, length us, event | category | flops | bytes accessed | tf_op | source)
XLA Modules:
  0.0 189.0 jit_solution(1686612959582789486)
XLA Ops:
  0.7 0.6 pad_add_fusion.meta_ref
  1.3 2.8 %init_slabs.1 = s16[16,48,128]{2,1,0:T(8,128)(2,1)} custom-call(s32[2]{0:T(128)} %pad_add_fusion.meta_ref, s32[8]{0:T(128)} %plan_ref.3, f32[8,256,128]{2,1,0:T(8,128)} %bitcast.17, s32[2,128]{1,0:T(2,128)} %land_ref.1, s32[2,128]{1,0:T(2,128)} %levels_ref.1), custom_call_target="tpu_custom_call" | custom-call | tf_op jit(solution)/shard_map/init_slabs/pallas_call | solution.py:87
  4.1 12.4 %all-to-all-start = ((s16[16,48,128]{2,1,0:T(8,128)(2,1)}), s16[16,48,128]{2,1,0:T(8,128)(2,1)S(1)}, u32[]{:S(2)}, u32[]{:S(2)}) async-start(s16[16,48,128]{2,1,0:T(8,128)(2,1)} %init_slabs.1), calls=%async_computation | async-start | bytes 393216 | tf_op jit(solution)/shard_map/all_to_all | solution.py:475
  16.5 6.9 %prepare.1 = (bf16[8,8,2,16,128]{4,3,2,1,0:T(8,128)(2,1)}, bf16[128,4096]{1,0:T(8,128)(2,1)}, bf16[4096,128]{1,0:T(8,128)(2,1)}) custom-call(s32[8]{0:T(128)} %plan_ref.3, bf16[8,256,128]{2,1,0:T(8,128)(2,1)} %bitcast.20, bf16[4096,128]{1,0:T(8,128)(2,1)} %w_in_ref.1, bf16[128,4096]{1,0:T(8,128)(2,1)} %w_out_ref.5), custom_call_target="tpu_custom_call" | custom-call | bytes 6291456 | tf_op jit(solution)/shard_map/prepare/pallas_call | solution.py:270
  23.4 3.8 %all-to-all-done.msg_ref = s16[16,48,128]{2,1,0:T(8,128)(2,1)S(1)} async-done(((s16[16,48,128]{2,1,0:T(8,128)(2,1)}), s16[16,48,128]{2,1,0:T(8,128)(2,1)S(1)}, u32[]{:S(2)}, u32[]{:S(2)}) %all-to-all-start) | async-done | bytes 196640 | tf_op jit(solution)/shard_map/all_to_all | solution.py:475
  27.1 0.0 copy-start.1
  27.1 9.1 %all-to-all-start.1 = ((bf16[64,2,16,128]{3,2,1,0:T(8,128)(2,1)}), bf16[64,2,16,128]{3,2,1,0:T(8,128)(2,1)S(1)}, u32[]{:S(2)}, u32[]{:S(2)}) async-start(bf16[64,2,16,128]{3,2,1,0:T(8,128)(2,1)} %bitcast.19), calls=%async_computation.1 | async-start | bytes 1048576 | tf_op jit(solution)/shard_map/all_to_all | solution.py:475
  36.2 3.5 %collective-permute-start = (s16[16,16,128]{2,1,0:T(8,128)(2,1)S(1)}, s16[16,16,128]{2,1,0:T(8,128)(2,1)S(1)}, u32[]{:S(2)}, u32[]{:S(2)}) collective-permute-start(s16[16,16,128]{2,1,0:T(8,128)(2,1)S(1)} %get-tuple-element.38), channel_id=1, source_target_pairs={{0,4},{1,5},{2,6},{3,7},{4,8},{5,9},{6,10},{7,11},{8,12},{9,13},{1... | collective-permute-start | bytes 196616 | tf_op jit(solution)/shard_map/ppermute | solution.py:492
  39.8 1.9 %collective-permute-start.1 = (s16[16,16,128]{2,1,0:T(8,128)(2,1)S(1)}, s16[16,16,128]{2,1,0:T(8,128)(2,1)S(1)}, u32[]{:S(2)}, u32[]{:S(2)}) collective-permute-start(s16[16,16,128]{2,1,0:T(8,128)(2,1)S(1)} %get-tuple-element.37), channel_id=1, source_target_pairs={{4,0},{5,1},{6,2},{7,3},{8,4},{9,5},{10,6},{11,7},{12,8},{13,9},{1... | collective-permute-start | bytes 196616 | tf_op jit(solution)/shard_map/ppermute | solution.py:493
  41.7 0.0 collective-permute-done.left_ref
  41.7 0.0 copy-start.4
  41.7 4.8 %collective-permute-done.1.right_ref = s16[16,16,128]{2,1,0:T(8,128)(2,1)S(1)} collective-permute-done((s16[16,16,128]{2,1,0:T(8,128)(2,1)S(1)}, s16[16,16,128]{2,1,0:T(8,128)(2,1)S(1)}, u32[]{:S(2)}, u32[]{:S(2)}) %collective-permute-start.1) | collective-permute-done | bytes 65568 | tf_op jit(solution)/shard_map/ppermute | solution.py:493
  46.5 0.0 copy-start.5
  46.5 0.0 copy-done.1
  46.5 0.0 copy-done.4
  46.5 0.6 copy-done.5
  47.1 26.3 %rollout.1 = (bf16[4,32,16,128]{3,2,1,0:T(8,128)(2,1)}, bf16[4,32,16,128]{3,2,1,0:T(8,128)(2,1)}, f32[4,32,16,128]{3,2,1,0:T(8,128)}, f32[32,16,128]{2,1,0:T(8,128)}) custom-call(s32[2]{0:T(128)} %pad_add_fusion.meta_ref, s16[16,48,128]{2,1,0:T(8,128)(2,1)} %copy-done.1, s16[16,16,128]{2,1,0:T(8,128)(2,1)} %copy-done.4, s16[16,16,128]{2,1,0:T(8,128)(2,1)} %copy-done.5, ...), custom_call_target="tpu_custom_call" | custom-call | flops 5905580032 | bytes 6291456 | tf_op jit(solution)/shard_map/rollout/pallas_call | solution.py:217
  73.5 0.0 all-to-all-done.1
  73.5 0.0 copy-start.2
  73.5 0.8 copy-done.2
  74.3 13.6 %first_grads.1 = (f32[32,2,64,128]{3,2,1,0:T(8,128)}, bf16[128,2048]{1,0:T(8,128)(2,1)}, bf16[2048,128]{1,0:T(8,128)(2,1)}, bf16[128,2048]{1,0:T(8,128)(2,1)}) custom-call(s32[1]{0:T(128)S(6)} %sub.4.half_ref, bf16[2048,128]{1,0:T(8,128)(2,1)} %bitcast.24, f32[2048,128]{1,0:T(8,128)} %bitcast.23, bf16[2048,128]{1,0:T(8,128)(2,1)} %bitcast.18, ...), custom_call_target="tpu_custom_call" | custom-call | flops 4294967296 | bytes 5242880 | tf_op jit(solution)/shard_map/first_grads/pallas_call | solution.py:371
  87.9 0.0 collective-permute-start.2
  87.9 15.9 %all-to-all-start.2 = ((bf16[64,2,16,128]{3,2,1,0:T(8,128)(2,1)}), bf16[64,2,16,128]{3,2,1,0:T(8,128)(2,1)S(1)}, u32[]{:S(2)}, u32[]{:S(2)}) async-start(bf16[64,2,16,128]{3,2,1,0:T(8,128)(2,1)} %bitcast.12), calls=%async_computation.2 | async-start | bytes 1048576 | tf_op jit(solution)/shard_map/all_to_all | solution.py:475
  103.8 0.0 collective-permute-done.2.add_ref
  103.8 0.0 copy-start.3
  103.9 1.3 copy-done.3
  105.2 13.8 %second_grads.1 = bf16[32,2,64,128]{3,2,1,0:T(8,128)(2,1)} custom-call(s32[1]{0:T(128)} %bitcast.half_ref, bf16[2048,128]{1,0:T(8,128)(2,1)} %bitcast.25, bf16[128,2048]{1,0:T(8,128)(2,1)} %get-tuple-element.26.x_t, bf16[2048,128]{1,0:T(8,128)(2,1)} %get-tuple-element.27.misfit, bf16[128,2048]{1,0:T(8,128)(2,1)} %get-tuple-element.28.misfit_t, ...), custom_call_target="tpu_custom_call" | custom-call | flops 4294967296 | bytes 5242880 | tf_op jit(solution)/shard_map/second_grads/pallas_call | solution.py:371
  118.9 2.7 %all-to-all-done.2 = bf16[64,2,16,128]{3,2,1,0:T(8,128)(2,1)S(1)} async-done(((bf16[64,2,16,128]{3,2,1,0:T(8,128)(2,1)}), bf16[64,2,16,128]{3,2,1,0:T(8,128)(2,1)S(1)}, u32[]{:S(2)}, u32[]{:S(2)}) %all-to-all-start.2) | async-done | bytes 524320 | tf_op jit(solution)/shard_map/all_to_all | solution.py:475
  121.6 0.0 copy-start
  121.6 23.8 %all_to_all.30.in_ref = bf16[32,2,64,128]{3,2,1,0:T(8,128)(2,1)S(1)} all-to-all(bf16[32,2,64,128]{3,2,1,0:T(8,128)(2,1)} %second_grads.1), channel_id=1, replica_groups=mesh['sec'=4,'zh'=2,'cx'=4,'core'=2,'c1'=2,'c0'=2] {'sec','cx','c0'}, dimensions={0} | all-to-all | bytes 2097152 | tf_op jit(solution)/shard_map/all_to_all | solution.py:475
  145.4 0.1 plane_copies.1
  145.6 11.3 %all_to_all.31.in_ref = bf16[4,2,64,128]{3,2,1,0:T(8,128)(2,1)S(1)} all-to-all(bf16[4,2,64,128]{3,2,1,0:T(8,128)(2,1)S(1)} %plane_copies.1), channel_id=1, replica_groups=mesh['sec'=4,'zh'=2,'cx'=4,'core'=2,'c1'=2,'c0'=2] {'zh','c1'}, dimensions={0} | all-to-all | bytes 262144 | tf_op jit(solution)/shard_map/all_to_all | solution.py:475
  156.9 0.2 column_copies.1
  157.1 0.0 copy-done
  157.1 20.7 %all_to_all.32.code_ref = s16[32,144,128]{2,1,0:T(8,128)(2,1)S(1)} all-to-all(s16[32,144,128]{2,1,0:T(8,128)(2,1)S(1)} %column_copies.1), channel_id=1, replica_groups=mesh['sec'=4,'zh'=2,'cx'=4,'core'=2,'c1'=2,'c0'=2] {'sec','cx','c0'}, dimensions={0} | all-to-all | bytes 2359296 | tf_op jit(solution)/shard_map/all_to_all | solution.py:475
  177.7 3.2 %collective-permute-start.3 = (s16[32,144,128]{2,1,0:T(8,128)(2,1)S(1)}, s16[32,144,128]{2,1,0:T(8,128)(2,1)S(1)}, u32[]{:S(2)}, u32[]{:S(2)}) collective-permute-start(s16[32,144,128]{2,1,0:T(8,128)(2,1)S(1)} %all_to_all.32.code_ref), channel_id=1, source_target_pairs={{0,4},{4,0},{1,5},{5,1},{2,6},{6,2},{3,7},{7,3},{8,12},{12,8},{9,1... | collective-permute-start | bytes 3538952 | tf_op jit(solution)/shard_map/ppermute | solution.py:510
  181.0 5.2 %spread_trajectory.1 = f32[8,256,128]{2,1,0:T(8,128)} custom-call(bf16[8,8,2,16,128]{4,3,2,1,0:T(8,128)(2,1)} %bitcast.15), custom_call_target="tpu_custom_call" | custom-call | tf_op jit(solution)/shard_map/spread_trajectory/pallas_call | solution.py:305
  186.2 1.4 finish_half.2
  187.6 0.0 collective-permute-done.3.code_ref
  187.6 1.4 finish_half.3
  (1 shorter events, 0.0 us)
Async XLA Ops:
  4.1 23.1 %all-to-all-start = ((s16[16,48,128]{2,1,0:T(8,128)(2,1)}), s16[16,48,128]{2,1,0:T(8,128)(2,1)S(1)}, u32[]{:S(2)}, u32[]{:S(2)}) async-start(s16[16,48,128]{2,1,0:T(8,128)(2,1)} %init_slabs.1), calls=%async_computation | async-start | bytes 393216 | tf_op jit(solution)/shard_map/all_to_all | solution.py:475
  27.1 19.4 %copy-start.1 = (s16[16,48,128]{2,1,0:T(8,128)(2,1)}, s16[16,48,128]{2,1,0:T(8,128)(2,1)S(1)}, u32[]{:S(2)}) copy-start(s16[16,48,128]{2,1,0:T(8,128)(2,1)S(1)} %all-to-all-done.msg_ref) | copy-start | bytes 589828
  27.1 46.3 %all-to-all-start.1 = ((bf16[64,2,16,128]{3,2,1,0:T(8,128)(2,1)}), bf16[64,2,16,128]{3,2,1,0:T(8,128)(2,1)S(1)}, u32[]{:S(2)}, u32[]{:S(2)}) async-start(bf16[64,2,16,128]{3,2,1,0:T(8,128)(2,1)} %bitcast.19), calls=%async_computation.1 | async-start | bytes 1048576 | tf_op jit(solution)/shard_map/all_to_all | solution.py:475
  36.2 5.5 %collective-permute-start = (s16[16,16,128]{2,1,0:T(8,128)(2,1)S(1)}, s16[16,16,128]{2,1,0:T(8,128)(2,1)S(1)}, u32[]{:S(2)}, u32[]{:S(2)}) collective-permute-start(s16[16,16,128]{2,1,0:T(8,128)(2,1)S(1)} %get-tuple-element.38), channel_id=1, source_target_pairs={{0,4},{1,5},{2,6},{3,7},{4,8},{5,9},{6,10},{7,11},{8,12},{9,13},{1... | collective-permute-start | bytes 196616 | tf_op jit(solution)/shard_map/ppermute | solution.py:492
  39.8 6.7 %collective-permute-start.1 = (s16[16,16,128]{2,1,0:T(8,128)(2,1)S(1)}, s16[16,16,128]{2,1,0:T(8,128)(2,1)S(1)}, u32[]{:S(2)}, u32[]{:S(2)}) collective-permute-start(s16[16,16,128]{2,1,0:T(8,128)(2,1)S(1)} %get-tuple-element.37), channel_id=1, source_target_pairs={{4,0},{5,1},{6,2},{7,3},{8,4},{9,5},{10,6},{11,7},{12,8},{13,9},{1... | collective-permute-start | bytes 196616 | tf_op jit(solution)/shard_map/ppermute | solution.py:493
  41.7 4.8 %copy-start.4 = (s16[16,16,128]{2,1,0:T(8,128)(2,1)}, s16[16,16,128]{2,1,0:T(8,128)(2,1)S(1)}, u32[]{:S(2)}) copy-start(s16[16,16,128]{2,1,0:T(8,128)(2,1)S(1)} %collective-permute-done.left_ref) | copy-start | bytes 196612
  46.5 0.6 copy-start.5
  73.5 0.8 copy-start.2
  87.9 15.9 %collective-permute-start.2 = (f32[32,2,64,128]{3,2,1,0:T(8,128)}, f32[32,2,64,128]{3,2,1,0:T(8,128)S(1)}, u32[]{:S(2)}, u32[]{:S(2)}) collective-permute-start(f32[32,2,64,128]{3,2,1,0:T(8,128)} %get-tuple-element.29), channel_id=1, source_target_pairs={{0,4},{4,0},{1,5},{5,1},{2,6},{6,2},{3,7},{7,3},{8,12},{12,8},{9,1... | collective-permute-start | bytes 6291464 | tf_op jit(solution)/shard_map/ppermute | solution.py:504
  87.9 33.7 %all-to-all-start.2 = ((bf16[64,2,16,128]{3,2,1,0:T(8,128)(2,1)}), bf16[64,2,16,128]{3,2,1,0:T(8,128)(2,1)S(1)}, u32[]{:S(2)}, u32[]{:S(2)}) async-start(bf16[64,2,16,128]{3,2,1,0:T(8,128)(2,1)} %bitcast.12), calls=%async_computation.2 | async-start | bytes 1048576 | tf_op jit(solution)/shard_map/all_to_all | solution.py:475
  103.8 1.3 copy-start.3
  121.6 35.5 %copy-start = (bf16[64,2,16,128]{3,2,1,0:T(8,128)(2,1)}, bf16[64,2,16,128]{3,2,1,0:T(8,128)(2,1)S(1)}, u32[]{:S(2)}) copy-start(bf16[64,2,16,128]{3,2,1,0:T(8,128)(2,1)S(1)} %all-to-all-done.2) | copy-start | bytes 1572868
  177.7 9.9 %collective-permute-start.3 = (s16[32,144,128]{2,1,0:T(8,128)(2,1)S(1)}, s16[32,144,128]{2,1,0:T(8,128)(2,1)S(1)}, u32[]{:S(2)}, u32[]{:S(2)}) collective-permute-start(s16[32,144,128]{2,1,0:T(8,128)(2,1)S(1)} %all_to_all.32.code_ref), channel_id=1, source_target_pairs={{0,4},{4,0},{1,5},{5,1},{2,6},{6,2},{3,7},{7,3},{8,12},{12,8},{9,1... | collective-permute-start | bytes 3538952 | tf_op jit(solution)/shard_map/ppermute | solution.py:510

commit v2 on v1

--- a/solution.py
+++ b/solution.py
@@ -24,8 +24,10 @@
 UNIT = 32768.0 / CODE
 OWN = NX * CHUNK
 COLS = STEPS * OWN
-HB1 = 512
-HB2 = 256
+HB1 = 2048
+HB2 = 1024
+WIDE = 512
+STRIP = 32
 HALF = H // 2
 GRAD_SCALE = 1.0 / math.sqrt(MB * STEPS * NX * NY)
 TILE = ("zh", "cx", "core")
@@ -39,7 +41,13 @@
     order = np.arange(L)
     angles = np.pi * (order[None, :] + 0.5) * order[:, None] / L
     weights = np.where(order[:, None] == 0, math.sqrt(1.0 / L), math.sqrt(2.0 / L))
-    return np.kron(np.eye(V), np.cos(angles) * weights).astype(np.float32)
+    return np.kron(np.eye(V), np.cos(angles) * weights)
+
+
+def split_table(matrix):
+    high = matrix.astype(jnp.bfloat16)
+    low = (matrix - high.astype(np.float64)).astype(jnp.bfloat16)
+    return np.concatenate([high, high, low], axis=0)
 
 
 def params(semantics=None, mib=60):
@@ -106,10 +114,19 @@
     return (lax.broadcasted_iota(jnp.int32, (1, F), 1) % L).astype(jnp.float32)
 
 
+def split_dot(value, table):
+    high = value.astype(jnp.bfloat16)
+    low = (value - high.astype(jnp.float32)).astype(jnp.bfloat16)
+    both = jnp.concatenate([high, low], axis=1)
+    return jnp.dot(both, table[0 : 2 * F], preferred_element_type=jnp.float32) + jnp.dot(
+        high, table[2 * F :], preferred_element_type=jnp.float32
+    )
+
+
 def rollout_kernel(
     meta_ref, msg_ref, left_ref, right_ref, w_in_t, w_out_t, mode_ref, mode_t, diff_ref, stiff_ref,
     traj_ref, inputs_ref, tend_ref, own_wet_ref,
-    state, wet, modal, acc, x_scr, gain, pull, depth, depth_t,
+    state, wet, modal, acc, x_scr, gain, pull, depth, depth_t, before, hidden,
 ):
     for t in range(16):
         for n, (ref, base) in enumerate(
@@ -162,12 +179,7 @@
             - 4.0 * now
         )
         smoothed = wet[...] * (now + diff * around)
-        modal[...] = jnp.dot(
-            smoothed.reshape(NX * SLAB, F),
-            mode_t[...],
-            precision=lax.Precision.HIGHEST,
-            preferred_element_type=jnp.float32,
-        ).reshape(NX, SLAB, F)
+        modal[...] = split_dot(smoothed.reshape(NX * SLAB, F), mode_t).reshape(NX, SLAB, F)
         part = modal[0] * gain[pl.ds(0, 1), :]
         modal[0] = part
         for i in range(1, NX):
@@ -176,12 +188,8 @@
         for i in range(NX - 2, -1, -1):
             part = modal[i] + pull[pl.ds(i, 1), :] * part
             modal[i] = part
-        after = wet[...] * jnp.dot(
-            modal[...].reshape(NX * SLAB, F),
-            mode_ref[...],
-            precision=lax.Precision.HIGHEST,
-            preferred_element_type=jnp.float32,
-        ).reshape(NX, SLAB, F)
+        after = split_dot(modal[...].reshape(NX * SLAB, F), mode_ref).reshape(NX, SLAB, F)
+        after = wet[...] * after
         rows = SLAB if step < STEPS - 1 else CHUNK
         after = after[:, :rows]
         state[:, :rows] = after
@@ -189,21 +197,29 @@
         inputs_ref[step] = after[:, :CHUNK].astype(jnp.bfloat16)
         acc[0 : NX * rows] = jnp.zeros((NX * rows, F), jnp.float32)
 
-        def block(b, carry, rows=rows):
-            at = pl.multiple_of(b * HB1, HB1)
-            hidden = jnp.tanh(
-                jnp.dot(
-                    x_scr[0 : NX * rows],
-                    w_in_t[:, pl.ds(at, HB1)],
+        def block(b, carry, n=NX * rows):
+            def front(i):
+                at = pl.multiple_of(b * HB1 + i * WIDE, WIDE)
+                before[i % 2, 0:n] = jnp.dot(
+                    x_scr[0:n], w_in_t[:, pl.ds(at, WIDE)], preferred_element_type=jnp.float32
+                )
+                return at
+
+            at = front(0)
+            for i in range(HB1 // WIDE):
+                following = front(i + 1) if i + 1 < HB1 // WIDE else None
+                for r in range(0, n, STRIP):
+                    strip = jnp.tanh(before[i % 2, r : r + STRIP])
+                    hidden[i % 2, r : r + STRIP] = strip.astype(jnp.bfloat16)
+                acc[0:n] += jnp.dot(
+                    hidden[i % 2, 0:n],
+                    w_out_t[pl.ds(at, WIDE), :],
                     preferred_element_type=jnp.float32,
                 )
-            ).astype(jnp.bfloat16)
-            acc[0 : NX * rows] += jnp.dot(
-                hidden, w_out_t[pl.ds(at, HB1), :], preferred_element_type=jnp.float32
-            )
+                at = following
             return carry
 
-        lax.fori_loop(0, H // HB1, block, 0, unroll=2)
+        lax.fori_loop(0, H // HB1, block, 0)
         tendency = acc[0 : NX * rows].reshape(NX, rows, F)
         result = wet[:, :rows] * (state[:, :rows] + tendency)
         state[:, :rows] = result
@@ -234,6 +250,8 @@
             pltpu.VMEM((NX, F), jnp.float32),
             pltpu.VMEM((3, NX, 128), jnp.float32),
             pltpu.VMEM((3, 128, NX), jnp.float32),
+            pltpu.VMEM((2, NX * SLAB, WIDE), jnp.float32),
+            pltpu.VMEM((2, NX * SLAB, WIDE), jnp.bfloat16),
         ],
         compiler_params=params(),
         cost_estimate=pl.CostEstimate(
@@ -247,8 +265,8 @@
         right,
         w_in_t,
         w_out_t,
-        jnp.asarray(block),
-        jnp.asarray(np.ascontiguousarray(block.T)),
+        jnp.asarray(split_table(block)),
+        jnp.asarray(split_table(block.T)),
         diffusivity.reshape(1, F),
         stiffness.reshape(1, F),
     )
@@ -313,25 +331,40 @@
     )(arrived)
 
 
-def grad_block(x_ref, x_t, misfit, misfit_t, w_in_ref, w_out_ref):
-    width = w_in_ref.shape[1]
-    grad_in = jnp.zeros((F, width), jnp.float32)
-    grad_out = jnp.zeros((F, width), jnp.float32)
-    for part in range(STEPS):
-        at = slice(part * OWN, (part + 1) * OWN)
-        hidden = jnp.tanh(jnp.dot(x_ref[at], w_in_ref[...], preferred_element_type=jnp.float32))
-        grad_out += jnp.dot(
-            misfit_t[:, at], hidden.astype(jnp.bfloat16), preferred_element_type=jnp.float32
+def grad_block(x_ref, x_t, misfit, misfit_t, w_in_ref, w_out_t_ref, out_ref, scratch):
+    before, back, hidden, change = scratch
+    rows = w_in_ref.shape[0]
+
+    def front(part):
+        at = slice(part * WIDE, (part + 1) * WIDE)
+        before[part % 2] = jnp.dot(w_in_ref[...], x_t[:, at], preferred_element_type=jnp.float32)
+        back[part % 2] = jnp.dot(
+            w_out_t_ref[...], misfit_t[:, at], preferred_element_type=jnp.float32
         )
-        back = jnp.dot(misfit[at], w_out_ref[...], preferred_element_type=jnp.float32)
-        back = (back * (1.0 - hidden * hidden)).astype(jnp.bfloat16)
-        grad_in += jnp.dot(x_t[:, at], back, preferred_element_type=jnp.float32)
-    shape = (width // ROWS, ROWS, F)
-    return grad_in.T.reshape(shape), grad_out.T.reshape(shape)
+        return at
+
+    grad_in = jnp.zeros((rows, F), jnp.float32)
+    grad_out = jnp.zeros((rows, F), jnp.float32)
+    at = front(0)
+    for part in range(COLS // WIDE):
+        following = front(part + 1) if part + 1 < COLS // WIDE else None
+        n = part % 2
+        for r in range(0, rows, STRIP):
+            strip = jnp.tanh(before[n, r : r + STRIP])
+            hidden[n, r : r + STRIP] = strip.astype(jnp.bfloat16)
+            strip = back[n, r : r + STRIP] * (1.0 - strip * strip)
+            change[n, r : r + STRIP] = strip.astype(jnp.bfloat16)
+        grad_out += jnp.dot(hidden[n], misfit[at], preferred_element_type=jnp.float32)
+        grad_in += jnp.dot(change[n], x_ref[at], preferred_element_type=jnp.float32)
+        at = following
+    out_ref[:, 0] = grad_in.reshape(rows // ROWS, ROWS, F)
+    out_ref[:, 1] = grad_out.reshape(rows // ROWS, ROWS, F)
 
 
 def first_kernel(
-    half_ref, x_ref, tend_ref, target_ref, wet_ref, w_in_ref, w_out_ref, out_ref, x_t, misfit, misfit_t
+    half_ref, x_ref, tend_ref, target_ref, wet_ref, w_in_ref, w_out_ref,
+    out_ref, x_t, misfit, misfit_t,
+    *scratch,
 ):
     @pl.when(pl.program_id(0) == 0)
     def _():
@@ -343,27 +376,21 @@
             misfit_t[:, at] = gap.T
             x_t[:, at] = x_ref[at].T
 
-    grad_in, grad_out = grad_block(x_ref, x_t, misfit, misfit_t, w_in_ref, w_out_ref)
-    out_ref[:, 0] = grad_in
-    out_ref[:, 1] = grad_out
-
-
-def second_kernel(half_ref, x_ref, x_t, misfit, misfit_t, w_in_ref, w_out_ref, add_ref, out_ref):
-    grad_in, grad_out = grad_block(x_ref, x_t, misfit, misfit_t, w_in_ref, w_out_ref)
-    out_ref[:, 0] = (grad_in + add_ref[:, 0]).astype(jnp.bfloat16)
-    out_ref[:, 1] = (grad_out + add_ref[:, 1]).astype(jnp.bfloat16)
-
-
-def half_grads(half, columns, w_in_t, w_out, add=None):
-    first = add is None
-    width = 512 if first else 256
-    blocks = HALF // width
+    grad_block(x_ref, x_t, misfit, misfit_t, w_in_ref, w_out_ref, out_ref, scratch)
+
+
+def second_kernel(
+    half_ref, x_ref, x_t, misfit, misfit_t, w_in_ref, w_out_ref, out_ref, *scratch
+):
+    grad_block(x_ref, x_t, misfit, misfit_t, w_in_ref, w_out_ref, out_ref, scratch)
+
+
+def half_grads(half, columns, w_in, w_out_t, first):
+    blocks = HALF // HB2
     whole = lambda i, half: (0, 0)
-    weight = lambda i, half: (0, half[0] * blocks + i)
-    rows = pl.BlockSpec((width // ROWS, 2, ROWS, F), lambda i, half: (i, 0, 0, 0))
-    in_specs = [pl.BlockSpec(c.shape, whole) for c in columns] + [pl.BlockSpec((F, width), weight)] * 2
-    out_specs = [rows]
-    out_shape = [jax.ShapeDtypeStruct((PARTS, 2, ROWS, F), jnp.float32 if first else jnp.bfloat16)]
+    weight = lambda i, half: (half[0] * blocks + i, 0)
+    out_specs = [pl.BlockSpec((HB2 // ROWS, 2, ROWS, F), lambda i, half: (i, 0, 0, 0))]
+    out_shape = [jax.ShapeDtypeStruct((PARTS, 2, ROWS, F), jnp.float32)]
     if first:
         for shape in ((F, COLS), (COLS, F), (F, COLS)):
             out_specs.append(pl.BlockSpec(shape, whole))
@@ -373,45 +400,62 @@
         grid_spec=pltpu.PrefetchScalarGridSpec(
             num_scalar_prefetch=1,
             grid=(blocks,),
-            in_specs=in_specs if first else in_specs + [rows],
+            in_specs=[pl.BlockSpec(c.shape, whole) for c in columns]
+            + [pl.BlockSpec((HB2, F), weight)] * 2,
             out_specs=out_specs,
+            scratch_shapes=[pltpu.VMEM((2, HB2, WIDE), jnp.float32)] * 2
+            + [pltpu.VMEM((2, HB2, WIDE), jnp.bfloat16)] * 2,
         ),
         out_shape=out_shape,
         compiler_params=params(("arbitrary",)),
-        cost_estimate=pl.CostEstimate(
-            flops=8 * COLS * F * HALF, bytes_accessed=5 * 2**20, transcendentals=COLS * HALF
-        ),
+        cost_estimate=pl.CostEstimate(flops=10**8, bytes_accessed=2**20, transcendentals=0),
         name="first_grads" if first else "second_grads",
-    )(half, *columns, w_in_t, w_out, *(() if first else (add,)))
+    )(half, *columns, w_in, w_out_t)
+
+
+def pair_kernel(mine_ref, other_ref, out_ref):
+    out_ref[...] = (mine_ref[...] + other_ref[...]).astype(jnp.bfloat16)
+
+
+def pair_sum(mine, other):
+    block = pl.BlockSpec((PARTS // 4, 2, ROWS, F), lambda i: (i, 0, 0, 0))
+    return pl.pallas_call(
+        pair_kernel,
+        grid=(4,),
+        in_specs=[block] * 2,
+        out_specs=block,
+        out_shape=jax.ShapeDtypeStruct((PARTS, 2, ROWS, F), jnp.bfloat16),
+        compiler_params=params(("arbitrary",)),
+        name="pair_sum",
+    )(mine, other)
 
 
 def plane_kernel(in_ref, out_ref):
     total = in_ref[0].astype(jnp.float32)
     for n in range(1, PARTS):
         total += in_ref[n].astype(jnp.float32)
-    total = total.astype(jnp.bfloat16)
-    for n in range(4):
-        out_ref[n] = total
-
-
-def plane_copies(parts):
+    out_ref[...] = total.astype(jnp.bfloat16)
+
+
+def plane_sum(parts):
     vmem = pl.BlockSpec(memory_space=pltpu.VMEM)
     return pl.pallas_call(
         plane_kernel,
-        out_shape=jax.ShapeDtypeStruct((4, 2, ROWS, F), jnp.bfloat16),
+        out_shape=jax.ShapeDtypeStruct((2, ROWS, F), jnp.bfloat16),
         in_specs=[vmem],
         out_specs=vmem,
         compiler_params=params(mib=32),
-        name="plane_copies",
+        name="plane_sum",
     )(parts)
 
 
-def column_kernel(in_ref, out_ref):
+def column_kernel(own_ref, near_ref, far_ref, both_ref, out_ref):
     powers = []
     for g in range(2):
-        total = in_ref[0, g].astype(jnp.float32)
-        for n in range(1, 4):
-            total += in_ref[n, g].astype(jnp.float32)
+        own, near, far, both = (
+            ref[g].astype(jnp.float32) for ref in (own_ref, near_ref, far_ref, both_ref)
+        )
+        total = (own + near) + (far + both)
         power = exponent(jnp.max(jnp.abs(total), axis=0, keepdims=True))
         powers.append(power)
         code = to_int16(encode(total, power))
@@ -422,16 +466,16 @@
         out_ref[n, 2 * ROWS : 2 * ROWS + 16] = tail
 
 
-def column_copies(planes):
+def column_copies(*planes):
     vmem = pl.BlockSpec(memory_space=pltpu.VMEM)
     return pl.pallas_call(
         column_kernel,
         out_shape=jax.ShapeDtypeStruct((PARTS, 2 * ROWS + 16, F), jnp.int16),
-        in_specs=[vmem],
+        in_specs=[vmem] * 4,
         out_specs=vmem,
         compiler_params=params(mib=32),
         name="column_copies",
-    )(planes)
+    )(*planes)
 
 
 def finish_kernel(half_ref, code_ref, *refs):
@@ -500,16 +544,21 @@
 
     inputs = inputs.reshape(COLS, F)
     columns = (inputs, tend.reshape(COLS, F), target, wet.reshape(OWN, F))
-    other, *columns = half_grads(1 - core, columns, w_in_t, w_out)
+    other, *columns = half_grads(1 - core, columns, w_in, w_out_t, True)
     swapped = lax.ppermute(other, "core", [(0, 1), (1, 0)])
-    (pair,) = half_grads(core, (inputs, *columns), w_in_t, w_out, swapped)
-    pair, arrived = lax.optimization_barrier((pair, arrived))
-
-    planes = swap(plane_copies(swap(pair, SPREAD)), ("zh", "c1"))
-    code = swap(column_copies(planes), SPREAD)
+    (mine,) = half_grads(core, (inputs, *columns), w_in, w_out_t, False)
+    mine, arrived = lax.optimization_barrier((mine, arrived))
+    pair = pair_sum(mine, swapped)
+
+    trajectory = spread_trajectory(arrived.reshape(MB, 8, 2, CHUNK, F))
+    plane = plane_sum(swap(pair, SPREAD))
+    plane, trajectory = lax.optimization_barrier((plane, trajectory))
+    others = [
+        lax.ppermute(plane, ("zh", "c1"), [(i, i ^ n) for i in range(4)]) for n in range(1, 4)
+    ]
+    code = swap(column_copies(plane, *others), SPREAD)
     across = lax.ppermute(code, "core", [(0, 1), (1, 0)])
     grad_in, grad_out = finish_half(1 - core, across, finish_half(core, code))
-    trajectory = spread_trajectory(arrived.reshape(MB, 8, 2, CHUNK, F))
     return (trajectory.reshape(1, MB, F, 2, 128), grad_in, grad_out)
 
 

time: 190 us -> 182 us (0.958)
  blocking collectives: 55.8 us -> 20.4 us
  waiting for transfers between devices: 11.2 us -> 27.8 us
  starting transfers between devices: 46.1 us -> 62.5 us
  Pallas kernels: 71.8 us -> 67.5 us
    all_to_all x3 -> x1, blocking collectives: 55.8 us -> 20.4 us  [swap(): return lax.all_to_all(value, axes, split_axis=0, concat_axis=0, tiled=True)]
    all_to_all x3 -> x4, waiting for transfers between devices: 6.42 us -> 20.9 us  [swap(): return lax.all_to_all(value, axes, split_axis=0, concat_axis=0, tiled=True)]
    all_to_all x3 -> x4, starting transfers between devices: 37.4 us -> 47.8 us  [swap(): return lax.all_to_all(value, axes, split_axis=0, concat_axis=0, tiled=True)]
    ppermute x0 -> x3, starting transfers between devices: none -> 5.96 us  [local(): lax.ppermute(plane, ('zh', 'c1'), [(i, i ^ n) for i in range(4)])]
    pallas_call x1, Pallas kernels: 26.3 us -> 21.4 us  [rollout(): pl.pallas_call(rollout_kernel, out_shape=[jax.ShapeDtypeStruct((STEPS, NX...]
    ppermute x1, waiting for transfers between devices: 4.79 us -> 0.39 us  [local(): right = lax.ppermute(msg[:, 0:16], TILE + COL, [(b, a) for a, b in forward])]
    pallas_call x1 -> x2, Pallas kernels: 0.15 us -> 4.32 us  [the longest x1 4.17 us: pair_sum(): pl.pallas_call(pair_kernel, grid=(4,), in_specs=[block] * 2, out_specs=bl...]
    ppermute x0 -> x3, waiting for transfers between devices: none -> 4.12 us  [local(): lax.ppermute(plane, ('zh', 'c1'), [(i, i ^ n) for i in range(4)])]
  transfers between devices with their start and end apart: 7 -> 11, of which waited for: 3 -> 8; matrix products, arithmetic and copies ran while one was open for 0% -> 0% of each run, Pallas kernels for 28% -> 26%
where the time goes in v2:
time: 182 us; the launch traced here: 181 us
  Pallas kernels  67.5 us (37%)
  starting transfers between devices  62.5 us (34%)
  waiting for transfers between devices  27.8 us (15%)
  blocking collectives  20.4 us (11%)
    all_to_all x4, starting transfers between devices, swap(): return lax.all_to_all(value, axes, split_axis=0, concat_axis=0, tiled=True)  47.8 us
    pallas_call x2, Pallas kernels, half_grads(): pl.pallas_call(first_kernel if first else second_kernel, grid_spec=pltpu....  23.8 us
    pallas_call x1, Pallas kernels, rollout(): pl.pallas_call(rollout_kernel, out_shape=[jax.ShapeDtypeStruct((STEPS, NX...  21.4 us
    all_to_all x4, waiting for transfers between devices, swap(): return lax.all_to_all(value, axes, split_axis=0, concat_axis=0, tiled=True)  20.9 us
    all_to_all x1, blocking collectives, swap(): return lax.all_to_all(value, axes, split_axis=0, concat_axis=0, tiled=True)  20.4 us
    pallas_call x1, Pallas kernels, prepare(): pl.pallas_call(prepare_kernel, grid_spec=pltpu.PrefetchScalarGridSpec(num...  6.9 us
    ppermute x3, starting transfers between devices, local(): lax.ppermute(plane, ('zh', 'c1'), [(i, i ^ n) for i in range(4)])  5.96 us
    pallas_call x1, Pallas kernels, spread_trajectory(): pl.pallas_call(spread_kernel, grid=(MB,), in_specs=[pl.BlockSpec((1, 8, 2...  5.24 us
  transfers between devices with their start and end apart: 11, of which 8 were waited for; matrix products, arithmetic and copies ran while one was open for 0% of the time, Pallas kernels for 26%

profile of v2, /device:TPU:1, one launch (start us, length us, event | category | flops | bytes accessed | tf_op | source)
XLA Modules:
  0.0 180.9 jit_solution(7597215319474122908)
XLA Ops:
  0.6 0.6 pad_add_fusion.meta_ref
  1.2 2.8 %init_slabs.1 = s16[16,48,128]{2,1,0:T(8,128)(2,1)} custom-call(s32[2]{0:T(128)} %pad_add_fusion.meta_ref, s32[8]{0:T(128)} %plan_ref.3, f32[8,256,128]{2,1,0:T(8,128)} %bitcast.21, s32[2,128]{1,0:T(2,128)} %land_ref.1, s32[2,128]{1,0:T(2,128)} %levels_ref.1), custom_call_target="tpu_custom_call" | custom-call | tf_op jit(solution)/shard_map/init_slabs/pallas_call | solution.py:95
  4.0 12.4 %all-to-all-start = ((s16[16,48,128]{2,1,0:T(8,128)(2,1)}), s16[16,48,128]{2,1,0:T(8,128)(2,1)S(1)}, u32[]{:S(2)}, u32[]{:S(2)}) async-start(s16[16,48,128]{2,1,0:T(8,128)(2,1)} %init_slabs.1), calls=%async_computation | async-start | bytes 393216 | tf_op jit(solution)/shard_map/all_to_all | solution.py:519
  16.4 6.9 %prepare.1 = (bf16[8,8,2,16,128]{4,3,2,1,0:T(8,128)(2,1)}, bf16[128,4096]{1,0:T(8,128)(2,1)}, bf16[4096,128]{1,0:T(8,128)(2,1)}) custom-call(s32[8]{0:T(128)} %plan_ref.3, bf16[8,256,128]{2,1,0:T(8,128)(2,1)} %bitcast.23, bf16[4096,128]{1,0:T(8,128)(2,1)} %w_in_ref.5, bf16[128,4096]{1,0:T(8,128)(2,1)} %w_out_ref.1), custom_call_target="tpu_custom_call" | custom-call | bytes 6291456 | tf_op jit(solution)/shard_map/prepare/pallas_call | solution.py:288
  23.3 3.7 %all-to-all-done.msg_ref = s16[16,48,128]{2,1,0:T(8,128)(2,1)S(1)} async-done(((s16[16,48,128]{2,1,0:T(8,128)(2,1)}), s16[16,48,128]{2,1,0:T(8,128)(2,1)S(1)}, u32[]{:S(2)}, u32[]{:S(2)}) %all-to-all-start) | async-done | bytes 196640 | tf_op jit(solution)/shard_map/all_to_all | solution.py:519
  27.1 0.0 copy-start.2
  27.1 9.1 %all-to-all-start.1 = ((bf16[64,2,16,128]{3,2,1,0:T(8,128)(2,1)}), bf16[64,2,16,128]{3,2,1,0:T(8,128)(2,1)S(1)}, u32[]{:S(2)}, u32[]{:S(2)}) async-start(bf16[64,2,16,128]{3,2,1,0:T(8,128)(2,1)} %bitcast.22), calls=%async_computation.1 | async-start | bytes 1048576 | tf_op jit(solution)/shard_map/all_to_all | solution.py:519
  36.2 2.4 %collective-permute-start.1 = (s16[16,16,128]{2,1,0:T(8,128)(2,1)S(1)}, s16[16,16,128]{2,1,0:T(8,128)(2,1)S(1)}, u32[]{:S(2)}, u32[]{:S(2)}) collective-permute-start(s16[16,16,128]{2,1,0:T(8,128)(2,1)S(1)} %get-tuple-element.41), channel_id=1, source_target_pairs={{4,0},{5,1},{6,2},{7,3},{8,4},{9,5},{10,6},{11,7},{12,8},{13,9},{1... | collective-permute-start | bytes 196616 | tf_op jit(solution)/shard_map/ppermute | solution.py:537
  38.6 3.2 %collective-permute-start = (s16[16,16,128]{2,1,0:T(8,128)(2,1)S(1)}, s16[16,16,128]{2,1,0:T(8,128)(2,1)S(1)}, u32[]{:S(2)}, u32[]{:S(2)}) collective-permute-start(s16[16,16,128]{2,1,0:T(8,128)(2,1)S(1)} %get-tuple-element.42), channel_id=1, source_target_pairs={{0,4},{1,5},{2,6},{3,7},{4,8},{5,9},{6,10},{7,11},{8,12},{9,13},{1... | collective-permute-start | bytes 196616 | tf_op jit(solution)/shard_map/ppermute | solution.py:536
  41.8 0.4 collective-permute-done.1.right_ref
  42.2 0.0 copy-start.3
  42.2 1.3 collective-permute-done.left_ref
  43.5 0.0 copy-start.4
  43.5 0.0 copy-done.2
  43.5 0.0 copy-done.3
  43.5 0.6 copy-done.4
  44.1 21.4 %rollout.1 = (bf16[4,32,16,128]{3,2,1,0:T(8,128)(2,1)}, bf16[4,32,16,128]{3,2,1,0:T(8,128)(2,1)}, f32[4,32,16,128]{3,2,1,0:T(8,128)}, f32[32,16,128]{2,1,0:T(8,128)}) custom-call(s32[2]{0:T(128)} %pad_add_fusion.meta_ref, s16[16,48,128]{2,1,0:T(8,128)(2,1)} %copy-done.2, s16[16,16,128]{2,1,0:T(8,128)(2,1)} %copy-done.4, s16[16,16,128]{2,1,0:T(8,128)(2,1)} %copy-done.3, ...), custom_call_target="tpu_custom_call" | custom-call | flops 5905580032 | bytes 6291456 | tf_op jit(solution)/shard_map/rollout/pallas_call | solution.py:233
  65.5 0.0 all-to-all-done.1
  65.5 0.0 copy-start
  65.6 0.8 copy-done
  66.3 12.1 %first_grads.1 = (f32[32,2,64,128]{3,2,1,0:T(8,128)}, bf16[128,2048]{1,0:T(8,128)(2,1)}, bf16[2048,128]{1,0:T(8,128)(2,1)}, bf16[128,2048]{1,0:T(8,128)(2,1)}) custom-call(s32[1]{0:T(128)S(6)} %sub.4.half_ref, bf16[2048,128]{1,0:T(8,128)(2,1)} %bitcast.15, f32[2048,128]{1,0:T(8,128)} %bitcast.19, bf16[2048,128]{1,0:T(8,128)(2,1)} %bitcast.17, ...), custom_call_target="tpu_custom_call" | custom-call | flops 100000000 | bytes 1048576 | tf_op jit(solution)/shard_map/first_grads/pallas_call | solution.py:398
  78.4 0.0 collective-permute-start.2
  78.4 18.8 %all-to-all-start.2 = ((bf16[64,2,16,128]{3,2,1,0:T(8,128)(2,1)}), bf16[64,2,16,128]{3,2,1,0:T(8,128)(2,1)S(1)}, u32[]{:S(2)}, u32[]{:S(2)}) async-start(bf16[64,2,16,128]{3,2,1,0:T(8,128)(2,1)} %bitcast.12), calls=%async_computation.2 | async-start | bytes 1048576 | tf_op jit(solution)/shard_map/all_to_all | solution.py:519
  97.2 11.7 %second_grads.1.mine_ref = f32[32,2,64,128]{3,2,1,0:T(8,128)} custom-call(s32[1]{0:T(128)} %bitcast.half_ref, bf16[2048,128]{1,0:T(8,128)(2,1)} %bitcast.16, bf16[128,2048]{1,0:T(8,128)(2,1)} %get-tuple-element.28.x_t, bf16[2048,128]{1,0:T(8,128)(2,1)} %get-tuple-element.29.misfit, bf16[128,2048]{1,0:T(8,128)(2,1)} %get-tuple-element.30.misfit_t, ...), custom_call_target="tpu_custom_call" | custom-call | flops 100000000 | bytes 1048576 | tf_op jit(solution)/shard_map/second_grads/pallas_call | solution.py:398
  108.9 6.1 %all-to-all-done.2 = bf16[64,2,16,128]{3,2,1,0:T(8,128)(2,1)S(1)} async-done(((bf16[64,2,16,128]{3,2,1,0:T(8,128)(2,1)}), bf16[64,2,16,128]{3,2,1,0:T(8,128)(2,1)S(1)}, u32[]{:S(2)}, u32[]{:S(2)}) %all-to-all-start.2) | async-done | bytes 524320 | tf_op jit(solution)/shard_map/all_to_all | solution.py:519
  115.0 0.0 copy-start.1
  115.0 0.0 collective-permute-done.2.other_ref
  115.0 4.2 %pair_sum.1 = bf16[32,2,64,128]{3,2,1,0:T(8,128)(2,1)} custom-call(f32[32,2,64,128]{3,2,1,0:T(8,128)} %second_grads.1.mine_ref, f32[32,2,64,128]{3,2,1,0:T(8,128)} %collective-permute-done.2.other_ref), custom_call_target="tpu_custom_call" | custom-call | tf_op jit(solution)/shard_map/pair_sum/pallas_call | solution.py:422
  119.2 0.0 copy-done.1
  119.2 7.5 %all-to-all-start.3 = ((bf16[32,2,64,128]{3,2,1,0:T(8,128)(2,1)}), bf16[32,2,64,128]{3,2,1,0:T(8,128)(2,1)S(1)}, u32[]{:S(2)}, u32[]{:S(2)}) async-start(bf16[32,2,64,128]{3,2,1,0:T(8,128)(2,1)} %pair_sum.1), calls=%async_computation.3 | async-start | bytes 2097152 | tf_op jit(solution)/shard_map/all_to_all | solution.py:519
  126.6 5.2 %spread_trajectory.1 = f32[8,256,128]{2,1,0:T(8,128)} custom-call(bf16[8,8,2,16,128]{4,3,2,1,0:T(8,128)(2,1)} %bitcast.18), custom_call_target="tpu_custom_call" | custom-call | tf_op jit(solution)/shard_map/spread_trajectory/pallas_call | solution.py:323
  131.9 11.1 %all-to-all-done.3.in_ref = bf16[32,2,64,128]{3,2,1,0:T(8,128)(2,1)S(1)} async-done(((bf16[32,2,64,128]{3,2,1,0:T(8,128)(2,1)}), bf16[32,2,64,128]{3,2,1,0:T(8,128)(2,1)S(1)}, u32[]{:S(2)}, u32[]{:S(2)}) %all-to-all-start.3) | async-done | bytes 1048608 | tf_op jit(solution)/shard_map/all_to_all | solution.py:519
  143.0 0.1 plane_sum.1.own_ref
  143.1 0.8 collective-permute-start.5
  143.9 5.2 %collective-permute-start.4 = (bf16[2,64,128]{2,1,0:T(8,128)(2,1)S(1)}, bf16[2,64,128]{2,1,0:T(8,128)(2,1)S(1)}, u32[]{:S(2)}, u32[]{:S(2)}) collective-permute-start(bf16[2,64,128]{2,1,0:T(8,128)(2,1)S(1)} %plane_sum.1.own_ref), channel_id=1, source_target_pairs={{0,32},{2,34},{32,0},{34,2},{1,33},{3,35},{33,1},{35,3},{4,36},{6,... | collective-permute-start | bytes 98312 | tf_op jit(solution)/shard_map/ppermute | solution.py:557
  149.1 0.0 collective-permute-start.3
  149.1 0.0 collective-permute-done.5.both_ref
  149.1 1.6 collective-permute-done.4.far_ref
  150.7 2.5 %collective-permute-done.3.near_ref = bf16[2,64,128]{2,1,0:T(8,128)(2,1)S(1)} collective-permute-done((bf16[2,64,128]{2,1,0:T(8,128)(2,1)S(1)}, bf16[2,64,128]{2,1,0:T(8,128)(2,1)S(1)}, u32[]{:S(2)}, u32[]{:S(2)}) %collective-permute-start.3) | collective-permute-done | bytes 32800 | tf_op jit(solution)/shard_map/ppermute | solution.py:557
  153.2 0.2 column_copies.1
  153.4 20.4 %all_to_all.25.code_ref = s16[32,144,128]{2,1,0:T(8,128)(2,1)S(1)} all-to-all(s16[32,144,128]{2,1,0:T(8,128)(2,1)S(1)} %column_copies.1), channel_id=1, replica_groups=mesh['sec'=4,'zh'=2,'cx'=4,'core'=2,'c1'=2,'c0'=2] {'sec','cx','c0'}, dimensions={0} | all-to-all | bytes 2359296 | tf_op jit(solution)/shard_map/all_to_all | solution.py:519
  173.8 3.2 %collective-permute-start.6 = (s16[32,144,128]{2,1,0:T(8,128)(2,1)S(1)}, s16[32,144,128]{2,1,0:T(8,128)(2,1)S(1)}, u32[]{:S(2)}, u32[]{:S(2)}) collective-permute-start(s16[32,144,128]{2,1,0:T(8,128)(2,1)S(1)} %all_to_all.25.code_ref), channel_id=1, source_target_pairs={{0,4},{4,0},{1,5},{5,1},{2,6},{6,2},{3,7},{7,3},{8,12},{12,8},{9,1... | collective-permute-start | bytes 3538952 | tf_op jit(solution)/shard_map/ppermute | solution.py:560
  177.0 1.4 finish_half.2
  178.4 1.0 collective-permute-done.6.code_ref
  179.5 1.4 finish_half.3
  (1 shorter events, 0.0 us)
Async XLA Ops:
  4.0 23.1 %all-to-all-start = ((s16[16,48,128]{2,1,0:T(8,128)(2,1)}), s16[16,48,128]{2,1,0:T(8,128)(2,1)S(1)}, u32[]{:S(2)}, u32[]{:S(2)}) async-start(s16[16,48,128]{2,1,0:T(8,128)(2,1)} %init_slabs.1), calls=%async_computation | async-start | bytes 393216 | tf_op jit(solution)/shard_map/all_to_all | solution.py:519
  27.1 16.4 %copy-start.2 = (s16[16,48,128]{2,1,0:T(8,128)(2,1)}, s16[16,48,128]{2,1,0:T(8,128)(2,1)S(1)}, u32[]{:S(2)}) copy-start(s16[16,48,128]{2,1,0:T(8,128)(2,1)S(1)} %all-to-all-done.msg_ref) | copy-start | bytes 589828
  27.1 38.4 %all-to-all-start.1 = ((bf16[64,2,16,128]{3,2,1,0:T(8,128)(2,1)}), bf16[64,2,16,128]{3,2,1,0:T(8,128)(2,1)S(1)}, u32[]{:S(2)}, u32[]{:S(2)}) async-start(bf16[64,2,16,128]{3,2,1,0:T(8,128)(2,1)} %bitcast.22), calls=%async_computation.1 | async-start | bytes 1048576 | tf_op jit(solution)/shard_map/all_to_all | solution.py:519
  36.2 6.0 %collective-permute-start.1 = (s16[16,16,128]{2,1,0:T(8,128)(2,1)S(1)}, s16[16,16,128]{2,1,0:T(8,128)(2,1)S(1)}, u32[]{:S(2)}, u32[]{:S(2)}) collective-permute-start(s16[16,16,128]{2,1,0:T(8,128)(2,1)S(1)} %get-tuple-element.41), channel_id=1, source_target_pairs={{4,0},{5,1},{6,2},{7,3},{8,4},{9,5},{10,6},{11,7},{12,8},{13,9},{1... | collective-permute-start | bytes 196616 | tf_op jit(solution)/shard_map/ppermute | solution.py:537
  38.6 4.9 %collective-permute-start = (s16[16,16,128]{2,1,0:T(8,128)(2,1)S(1)}, s16[16,16,128]{2,1,0:T(8,128)(2,1)S(1)}, u32[]{:S(2)}, u32[]{:S(2)}) collective-permute-start(s16[16,16,128]{2,1,0:T(8,128)(2,1)S(1)} %get-tuple-element.42), channel_id=1, source_target_pairs={{0,4},{1,5},{2,6},{3,7},{4,8},{5,9},{6,10},{7,11},{8,12},{9,13},{1... | collective-permute-start | bytes 196616 | tf_op jit(solution)/shard_map/ppermute | solution.py:536
  42.2 1.3 copy-start.3
  43.5 0.6 copy-start.4
  65.5 0.8 copy-start
  78.4 36.6 %collective-permute-start.2 = (f32[32,2,64,128]{3,2,1,0:T(8,128)}, f32[32,2,64,128]{3,2,1,0:T(8,128)}, u32[]{:S(2)}, u32[]{:S(2)}) collective-permute-start(f32[32,2,64,128]{3,2,1,0:T(8,128)} %get-tuple-element.33), channel_id=1, source_target_pairs={{0,4},{4,0},{1,5},{5,1},{2,6},{6,2},{3,7},{7,3},{8,12},{12,8},{9,1... | collective-permute-start | bytes 6291464 | tf_op jit(solution)/shard_map/ppermute | solution.py:548
  78.4 36.5 %all-to-all-start.2 = ((bf16[64,2,16,128]{3,2,1,0:T(8,128)(2,1)}), bf16[64,2,16,128]{3,2,1,0:T(8,128)(2,1)S(1)}, u32[]{:S(2)}, u32[]{:S(2)}) async-start(bf16[64,2,16,128]{3,2,1,0:T(8,128)(2,1)} %bitcast.12), calls=%async_computation.2 | async-start | bytes 1048576 | tf_op jit(solution)/shard_map/all_to_all | solution.py:519
  115.0 4.2 %copy-start.1 = (bf16[64,2,16,128]{3,2,1,0:T(8,128)(2,1)}, bf16[64,2,16,128]{3,2,1,0:T(8,128)(2,1)S(1)}, u32[]{:S(2)}) copy-start(bf16[64,2,16,128]{3,2,1,0:T(8,128)(2,1)S(1)} %all-to-all-done.2) | copy-start | bytes 1572868
  119.2 23.8 %all-to-all-start.3 = ((bf16[32,2,64,128]{3,2,1,0:T(8,128)(2,1)}), bf16[32,2,64,128]{3,2,1,0:T(8,128)(2,1)S(1)}, u32[]{:S(2)}, u32[]{:S(2)}) async-start(bf16[32,2,64,128]{3,2,1,0:T(8,128)(2,1)} %pair_sum.1), calls=%async_computation.3 | async-start | bytes 2097152 | tf_op jit(solution)/shard_map/all_to_all | solution.py:519
  143.1 6.0 %collective-permute-start.5 = (bf16[2,64,128]{2,1,0:T(8,128)(2,1)S(1)}, bf16[2,64,128]{2,1,0:T(8,128)(2,1)S(1)}, u32[]{:S(2)}, u32[]{:S(2)}) collective-permute-start(bf16[2,64,128]{2,1,0:T(8,128)(2,1)S(1)} %plane_sum.1.own_ref), channel_id=1, source_target_pairs={{0,34},{2,32},{32,2},{34,0},{1,35},{3,33},{33,3},{35,1},{4,38},{6,... | collective-permute-start | bytes 98312 | tf_op jit(solution)/shard_map/ppermute | solution.py:557
  143.9 6.8 %collective-permute-start.4 = (bf16[2,64,128]{2,1,0:T(8,128)(2,1)S(1)}, bf16[2,64,128]{2,1,0:T(8,128)(2,1)S(1)}, u32[]{:S(2)}, u32[]{:S(2)}) collective-permute-start(bf16[2,64,128]{2,1,0:T(8,128)(2,1)S(1)} %plane_sum.1.own_ref), channel_id=1, source_target_pairs={{0,32},{2,34},{32,0},{34,2},{1,33},{3,35},{33,1},{35,3},{4,36},{6,... | collective-permute-start | bytes 98312 | tf_op jit(solution)/shard_map/ppermute | solution.py:557
  149.1 4.1 %collective-permute-start.3 = (bf16[2,64,128]{2,1,0:T(8,128)(2,1)S(1)}, bf16[2,64,128]{2,1,0:T(8,128)(2,1)S(1)}, u32[]{:S(2)}, u32[]{:S(2)}) collective-permute-start(bf16[2,64,128]{2,1,0:T(8,128)(2,1)S(1)} %plane_sum.1.own_ref), channel_id=1, source_target_pairs={{0,2},{2,0},{32,34},{34,32},{1,3},{3,1},{33,35},{35,33},{4,6},{6,4... | collective-permute-start | bytes 98312 | tf_op jit(solution)/shard_map/ppermute | solution.py:557
  173.8 5.7 %collective-permute-start.6 = (s16[32,144,128]{2,1,0:T(8,128)(2,1)S(1)}, s16[32,144,128]{2,1,0:T(8,128)(2,1)S(1)}, u32[]{:S(2)}, u32[]{:S(2)}) collective-permute-start(s16[32,144,128]{2,1,0:T(8,128)(2,1)S(1)} %all_to_all.25.code_ref), channel_id=1, source_target_pairs={{0,4},{4,0},{1,5},{5,1},{2,6},{6,2},{3,7},{7,3},{8,12},{12,8},{9,1... | collective-permute-start | bytes 3538952 | tf_op jit(solution)/shard_map/ppermute | solution.py:560

commit v3 on v2

--- a/solution.py
+++ b/solution.py
@@ -112,6 +112,28 @@
 
 def levels():
     return (lax.broadcasted_iota(jnp.int32, (1, F), 1) % L).astype(jnp.float32)
+
+
+def pack_halo(halo, step):
+    if step == STEPS - 1:
+        return jnp.zeros((0, F), jnp.float32)
+    share = (1, 2, 4)[step]
+    halo = halo.reshape(NX // share, share, 8, F)
+    packed = halo[:, 0]
+    row = lax.broadcasted_iota(jnp.int32, packed.shape, 1)
+    for n in range(1, share):
+        shift = n * 8 // share
+        keep = STEPS - 1 - step
+        place = (row + (8 - shift) + keep) % 8 < 2 * keep
+        packed = jnp.where(place, pltpu.roll(halo[:, n], shift, 1), packed)
+    return packed.reshape(NX // share * 8, F)
+
+
+def unpack_halo(packed, step):
+    share = (1, 2, 4)[step]
+    packed = packed.reshape(NX // share, 8, F)
+    parts = [packed] + [pltpu.roll(packed, 8 - n * 8 // share, 1) for n in range(1, share)]
+    return jnp.stack(parts, axis=1).reshape(NX, 8, F)
 
 
 def split_dot(value, table):
@@ -190,14 +212,16 @@
             modal[i] = part
         after = split_dot(modal[...].reshape(NX * SLAB, F), mode_ref).reshape(NX, SLAB, F)
         after = wet[...] * after
-        rows = SLAB if step < STEPS - 1 else CHUNK
-        after = after[:, :rows]
-        state[:, :rows] = after
-        x_scr[0 : NX * rows] = after.reshape(NX * rows, F).astype(jnp.bfloat16)
         inputs_ref[step] = after[:, :CHUNK].astype(jnp.bfloat16)
-        acc[0 : NX * rows] = jnp.zeros((NX * rows, F), jnp.float32)
-
-        def block(b, carry, n=NX * rows):
+        extra = pack_halo(after[:, CHUNK:], step)
+        count = OWN + extra.shape[0]
+        state[...] = after
+        x_scr[0:OWN] = after[:, :CHUNK].reshape(OWN, F).astype(jnp.bfloat16)
+        if step < STEPS - 1:
+            x_scr[OWN:count] = extra.astype(jnp.bfloat16)
+        acc[0:count] = jnp.zeros((count, F), jnp.float32)
+
+        def block(b, carry, n=count):
             def front(i):
                 at = pl.multiple_of(b * HB1 + i * WIDE, WIDE)
                 before[i % 2, 0:n] = jnp.dot(
@@ -220,11 +244,14 @@
             return carry
 
         lax.fori_loop(0, H // HB1, block, 0)
-        tendency = acc[0 : NX * rows].reshape(NX, rows, F)
-        result = wet[:, :rows] * (state[:, :rows] + tendency)
-        state[:, :rows] = result
-        traj_ref[step] = result[:, :CHUNK].astype(jnp.bfloat16)
-        tend_ref[step] = tendency[:, :CHUNK]
+        tendency = acc[0:OWN].reshape(NX, CHUNK, F)
+        result = wet[:, :CHUNK] * (state[:, :CHUNK] + tendency)
+        traj_ref[step] = result.astype(jnp.bfloat16)
+        tend_ref[step] = tendency
+        if step < STEPS - 1:
+            beside = unpack_halo(acc[OWN:count], step)
+            state[:, CHUNK:] = wet[:, CHUNK:] * (state[:, CHUNK:] + beside)
+            state[:, :CHUNK] = result
 
 
 def rollout(meta, msg, left, right, w_in_t, w_out_t, diffusivity, stiffness):
@@ -331,7 +358,7 @@
     )(arrived)
 
 
-def grad_block(x_ref, x_t, misfit, misfit_t, w_in_ref, w_out_t_ref, out_ref, scratch):
+def grad_block(x_ref, x_t, misfit, misfit_t, w_in_ref, w_out_t_ref, scratch):
     before, back, hidden, change = scratch
     rows = w_in_ref.shape[0]
 
@@ -357,77 +384,78 @@
         grad_out += jnp.dot(hidden[n], misfit[at], preferred_element_type=jnp.float32)
         grad_in += jnp.dot(change[n], x_ref[at], preferred_element_type=jnp.float32)
         at = following
-    out_ref[:, 0] = grad_in.reshape(rows // ROWS, ROWS, F)
-    out_ref[:, 1] = grad_out.reshape(rows // ROWS, ROWS, F)
-
-
-def first_kernel(
-    half_ref, x_ref, tend_ref, target_ref, wet_ref, w_in_ref, w_out_ref,
-    out_ref, x_t, misfit, misfit_t,
-    *scratch,
-):
+    shape = (rows // ROWS, ROWS, F)
+    return grad_in.reshape(shape), grad_out.reshape(shape)
+
+
+def columns_kernel(x_ref, tend_ref, target_ref, wet_ref, out_ref):
+    gap = wet_ref[...] * (tend_ref[...] - target_ref[...].astype(jnp.float32)) * GRAD_SCALE
+    out_ref[0] = x_ref[...]
+    out_ref[1] = gap.astype(jnp.bfloat16)
+
+
+def own_columns(inputs, tend, target, wet):
+    rows = pl.BlockSpec((OWN, F), lambda i: (i, 0))
+    return pl.pallas_call(
+        columns_kernel,
+        grid=(STEPS,),
+        in_specs=[rows] * 3 + [pl.BlockSpec((OWN, F), lambda i: (0, 0))],
+        out_specs=pl.BlockSpec((2, OWN, F), lambda i: (0, i, 0)),
+        out_shape=jax.ShapeDtypeStruct((2, COLS, F), jnp.bfloat16),
+        compiler_params=params(("arbitrary",)),
+        name="own_columns",
+    )(inputs, tend, target, wet)
+
+
+def grad_kernel(half_ref, columns_ref, w_in_ref, w_out_ref, *refs):
+    *add_ref, out_ref, x_t, misfit_t, before, back, hidden, change = refs
+
     @pl.when(pl.program_id(0) == 0)
     def _():
-        for step in range(STEPS):
-            at = slice(step * OWN, (step + 1) * OWN)
-            gap = wet_ref[...] * (tend_ref[at] - target_ref[at].astype(jnp.float32))
-            gap = (gap * GRAD_SCALE).astype(jnp.bfloat16)
-            misfit[at] = gap
-            misfit_t[:, at] = gap.T
-            x_t[:, at] = x_ref[at].T
-
-    grad_block(x_ref, x_t, misfit, misfit_t, w_in_ref, w_out_ref, out_ref, scratch)
-
-
-def second_kernel(
-    half_ref, x_ref, x_t, misfit, misfit_t, w_in_ref, w_out_ref, out_ref, *scratch
-):
-    grad_block(x_ref, x_t, misfit, misfit_t, w_in_ref, w_out_ref, out_ref, scratch)
-
-
-def half_grads(half, columns, w_in, w_out_t, first):
+        for part in range(STEPS):
+            at = slice(part * OWN, (part + 1) * OWN)
+            x_t[:, at] = columns_ref[0, at].T
+            misfit_t[:, at] = columns_ref[1, at].T
+
+    grads = grad_block(
+        columns_ref.at[0],
+        x_t,
+        columns_ref.at[1],
+        misfit_t,
+        w_in_ref,
+        w_out_ref,
+        (before, back, hidden, change),
+    )
+    for n, grad in enumerate(grads):
+        if add_ref:
+            grad = grad + add_ref[0][:, n]
+        out_ref[:, n] = grad.astype(out_ref.dtype)
+
+
+def half_grads(half, columns, w_in, w_out_t, add=None):
     blocks = HALF // HB2
-    whole = lambda i, half: (0, 0)
-    weight = lambda i, half: (half[0] * blocks + i, 0)
-    out_specs = [pl.BlockSpec((HB2 // ROWS, 2, ROWS, F), lambda i, half: (i, 0, 0, 0))]
-    out_shape = [jax.ShapeDtypeStruct((PARTS, 2, ROWS, F), jnp.float32)]
-    if first:
-        for shape in ((F, COLS), (COLS, F), (F, COLS)):
-            out_specs.append(pl.BlockSpec(shape, whole))
-            out_shape.append(jax.ShapeDtypeStruct(shape, jnp.bfloat16))
-    return pl.pallas_call(
-        first_kernel if first else second_kernel,
+    weight = pl.BlockSpec((HB2, F), lambda i, half: (half[0] * blocks + i, 0))
+    rows = pl.BlockSpec((HB2 // ROWS, 2, ROWS, F), lambda i, half: (i, 0, 0, 0))
+    first = add is None
+    return pl.pallas_call(
+        grad_kernel,
         grid_spec=pltpu.PrefetchScalarGridSpec(
             num_scalar_prefetch=1,
             grid=(blocks,),
-            in_specs=[pl.BlockSpec(c.shape, whole) for c in columns]
-            + [pl.BlockSpec((HB2, F), weight)] * 2,
-            out_specs=out_specs,
-            scratch_shapes=[pltpu.VMEM((2, HB2, WIDE), jnp.float32)] * 2
+            in_specs=[pl.BlockSpec((2, COLS, F), lambda i, half: (0, 0, 0)), weight, weight]
+            + ([] if first else [rows]),
+            out_specs=rows,
+            scratch_shapes=[pltpu.VMEM((F, COLS), jnp.bfloat16)] * 2
+            + [pltpu.VMEM((2, HB2, WIDE), jnp.float32)] * 2
             + [pltpu.VMEM((2, HB2, WIDE), jnp.bfloat16)] * 2,
         ),
-        out_shape=out_shape,
+        out_shape=jax.ShapeDtypeStruct(
+            (PARTS, 2, ROWS, F), jnp.float32 if first else jnp.bfloat16
+        ),
         compiler_params=params(("arbitrary",)),
         cost_estimate=pl.CostEstimate(flops=10**8, bytes_accessed=2**20, transcendentals=0),
         name="first_grads" if first else "second_grads",
-    )(half, *columns, w_in, w_out_t)
-
-
-def pair_kernel(mine_ref, other_ref, out_ref):
-    out_ref[...] = (mine_ref[...] + other_ref[...]).astype(jnp.bfloat16)
-
-
-def pair_sum(mine, other):
-    block = pl.BlockSpec((PARTS // 4, 2, ROWS, F), lambda i: (i, 0, 0, 0))
-    return pl.pallas_call(
-        pair_kernel,
-        grid=(4,),
-        in_specs=[block] * 2,
-        out_specs=block,
-        out_shape=jax.ShapeDtypeStruct((PARTS, 2, ROWS, F), jnp.bfloat16),
-        compiler_params=params(("arbitrary",)),
-        name="pair_sum",
-    )(mine, other)
+    )(half, columns, w_in, w_out_t, *(() if first else (add,)))
 
 
 def plane_kernel(in_ref, out_ref):
@@ -542,13 +570,12 @@
     traj, inputs, tend, wet = rollout(meta, msg, left, right, w_in_t, w_out_t, diffusivity, stiffness)
     arrived = swap(traj.reshape(64, 2, CHUNK, F), ("sec",) + TILE)
 
-    inputs = inputs.reshape(COLS, F)
-    columns = (inputs, tend.reshape(COLS, F), target, wet.reshape(OWN, F))
-    other, *columns = half_grads(1 - core, columns, w_in, w_out_t, True)
-    swapped = lax.ppermute(other, "core", [(0, 1), (1, 0)])
-    (mine,) = half_grads(core, (inputs, *columns), w_in, w_out_t, False)
-    mine, arrived = lax.optimization_barrier((mine, arrived))
-    pair = pair_sum(mine, swapped)
+    own = own_columns(
+        inputs.reshape(COLS, F), tend.reshape(COLS, F), target, wet.reshape(OWN, F)
+    )
+    theirs = lax.ppermute(own, "core", [(0, 1), (1, 0)])
+    pair = half_grads(core, theirs, w_in, w_out_t, half_grads(core, own, w_in, w_out_t))
+    pair, arrived = lax.optimization_barrier((pair, arrived))
 
     trajectory = spread_trajectory(arrived.reshape(MB, 8, 2, CHUNK, F))
     plane = plane_sum(swap(pair, SPREAD))

time: 182 us -> 178 us (0.978)
  waiting for transfers between devices: 27.8 us -> 23 us
    all_to_all x4, waiting for transfers between devices: 20.9 us -> 15.5 us  [swap(): return lax.all_to_all(value, axes, split_axis=0, concat_axis=0, tiled=True)]
  transfers between devices with their start and end apart: 11 -> 11, of which waited for: 8 -> 6; matrix products, arithmetic and copies ran while one was open for 0% -> 0% of each run, Pallas kernels for 26% -> 33%
where the time goes in v3:
time: 178 us; the launch traced here: 176 us
  Pallas kernels  65.8 us (37%)
  starting transfers between devices  63.7 us (36%)
  waiting for transfers between devices  23 us (13%)
  blocking collectives  20.2 us (11%)
  local copies, waits for them, and re-layouts  2.4 us (1%)
    all_to_all x4, starting transfers between devices, swap(): return lax.all_to_all(value, axes, split_axis=0, concat_axis=0, tiled=True)  47.6 us
    pallas_call x2, Pallas kernels, half_grads(): pl.pallas_call(grad_kernel, grid_spec=pltpu.PrefetchScalarGridSpec(num_sc...  23.7 us
    all_to_all x1, blocking collectives, swap(): return lax.all_to_all(value, axes, split_axis=0, concat_axis=0, tiled=True)  20.2 us
    pallas_call x1, Pallas kernels, rollout(): pl.pallas_call(rollout_kernel, out_shape=[jax.ShapeDtypeStruct((STEPS, NX...  20.1 us
    all_to_all x4, waiting for transfers between devices, swap(): return lax.all_to_all(value, axes, split_axis=0, concat_axis=0, tiled=True)  15.5 us
    ppermute x3, starting transfers between devices, local(): lax.ppermute(plane, ('zh', 'c1'), [(i, i ^ n) for i in range(4)])  7.26 us
    pallas_call x1, Pallas kernels, prepare(): pl.pallas_call(prepare_kernel, grid_spec=pltpu.PrefetchScalarGridSpec(num...  6.89 us
    pallas_call x1, Pallas kernels, spread_trajectory(): pl.pallas_call(spread_kernel, grid=(MB,), in_specs=[pl.BlockSpec((1, 8, 2...  5.24 us
  transfers between devices with their start and end apart: 11, of which 6 were waited for; matrix products, arithmetic and copies ran while one was open for 0% of the time, Pallas kernels for 33%

profile of v3, /device:TPU:1, one launch (start us, length us, event | category | flops | bytes accessed | tf_op | source)
XLA Modules:
  0.0 176.4 jit_solution(4500402125720143020)
XLA Ops:
  0.6 0.7 pad_add_fusion.meta_ref
  1.3 2.8 %init_slabs.1 = s16[16,48,128]{2,1,0:T(8,128)(2,1)} custom-call(s32[2]{0:T(128)} %pad_add_fusion.meta_ref, s32[8]{0:T(128)} %plan_ref.3, f32[8,256,128]{2,1,0:T(8,128)} %bitcast.18, s32[2,128]{1,0:T(2,128)} %land_ref.1, s32[2,128]{1,0:T(2,128)} %levels_ref.1), custom_call_target="tpu_custom_call" | custom-call | tf_op jit(solution)/shard_map/init_slabs/pallas_call | solution.py:95
  4.1 12.4 %all-to-all-start = ((s16[16,48,128]{2,1,0:T(8,128)(2,1)}), s16[16,48,128]{2,1,0:T(8,128)(2,1)S(1)}, u32[]{:S(2)}, u32[]{:S(2)}) async-start(s16[16,48,128]{2,1,0:T(8,128)(2,1)} %init_slabs.1), calls=%async_computation | async-start | bytes 393216 | tf_op jit(solution)/shard_map/all_to_all | solution.py:547
  16.5 6.9 %prepare.1 = (bf16[8,8,2,16,128]{4,3,2,1,0:T(8,128)(2,1)}, bf16[128,4096]{1,0:T(8,128)(2,1)}, bf16[4096,128]{1,0:T(8,128)(2,1)}) custom-call(s32[8]{0:T(128)} %plan_ref.3, bf16[8,256,128]{2,1,0:T(8,128)(2,1)} %bitcast.21, bf16[4096,128]{1,0:T(8,128)(2,1)} %w_in_ref.5, bf16[128,4096]{1,0:T(8,128)(2,1)} %w_out_ref.1), custom_call_target="tpu_custom_call" | custom-call | bytes 6291456 | tf_op jit(solution)/shard_map/prepare/pallas_call | solution.py:315
  23.4 3.8 %all-to-all-done.msg_ref = s16[16,48,128]{2,1,0:T(8,128)(2,1)S(1)} async-done(((s16[16,48,128]{2,1,0:T(8,128)(2,1)}), s16[16,48,128]{2,1,0:T(8,128)(2,1)S(1)}, u32[]{:S(2)}, u32[]{:S(2)}) %all-to-all-start) | async-done | bytes 196640 | tf_op jit(solution)/shard_map/all_to_all | solution.py:547
  27.2 0.0 copy-start.3
  27.2 9.1 %all-to-all-start.1 = ((bf16[64,2,16,128]{3,2,1,0:T(8,128)(2,1)}), bf16[64,2,16,128]{3,2,1,0:T(8,128)(2,1)S(1)}, u32[]{:S(2)}, u32[]{:S(2)}) async-start(bf16[64,2,16,128]{3,2,1,0:T(8,128)(2,1)} %bitcast.20), calls=%async_computation.1 | async-start | bytes 1048576 | tf_op jit(solution)/shard_map/all_to_all | solution.py:547
  36.3 2.4 %collective-permute-start.1 = (s16[16,16,128]{2,1,0:T(8,128)(2,1)S(1)}, s16[16,16,128]{2,1,0:T(8,128)(2,1)S(1)}, u32[]{:S(2)}, u32[]{:S(2)}) collective-permute-start(s16[16,16,128]{2,1,0:T(8,128)(2,1)S(1)} %get-tuple-element.33), channel_id=1, source_target_pairs={{4,0},{5,1},{6,2},{7,3},{8,4},{9,5},{10,6},{11,7},{12,8},{13,9},{1... | collective-permute-start | bytes 196616 | tf_op jit(solution)/shard_map/ppermute | solution.py:565
  38.6 3.2 %collective-permute-start = (s16[16,16,128]{2,1,0:T(8,128)(2,1)S(1)}, s16[16,16,128]{2,1,0:T(8,128)(2,1)S(1)}, u32[]{:S(2)}, u32[]{:S(2)}) collective-permute-start(s16[16,16,128]{2,1,0:T(8,128)(2,1)S(1)} %get-tuple-element.34), channel_id=1, source_target_pairs={{0,4},{1,5},{2,6},{3,7},{4,8},{5,9},{6,10},{7,11},{8,12},{9,13},{1... | collective-permute-start | bytes 196616 | tf_op jit(solution)/shard_map/ppermute | solution.py:564
  41.8 0.4 collective-permute-done.1.right_ref
  42.2 0.0 copy-start.4
  42.2 1.3 collective-permute-done.left_ref
  43.5 0.0 copy-start.5
  43.6 0.0 copy-done.3
  43.6 0.0 copy-done.4
  43.6 0.6 copy-done.5
  44.2 20.1 %rollout.1 = (bf16[4,32,16,128]{3,2,1,0:T(8,128)(2,1)}, bf16[4,32,16,128]{3,2,1,0:T(8,128)(2,1)}, f32[4,32,16,128]{3,2,1,0:T(8,128)}, f32[32,16,128]{2,1,0:T(8,128)}) custom-call(s32[2]{0:T(128)} %pad_add_fusion.meta_ref, s16[16,48,128]{2,1,0:T(8,128)(2,1)} %copy-done.3, s16[16,16,128]{2,1,0:T(8,128)(2,1)} %copy-done.5, s16[16,16,128]{2,1,0:T(8,128)(2,1)} %copy-done.4, ...), custom_call_target="tpu_custom_call" | custom-call | flops 5905580032 | bytes 6291456 | tf_op jit(solution)/shard_map/rollout/pallas_call | solution.py:260
  64.3 0.0 all-to-all-done.1
  64.3 0.0 copy-start.1
  64.3 0.8 copy-done.1
  65.1 3.9 %own_columns.1.columns_ref = bf16[2,2048,128]{2,1,0:T(8,128)(2,1)} custom-call(bf16[2048,128]{1,0:T(8,128)(2,1)} %bitcast.22, f32[2048,128]{1,0:T(8,128)} %bitcast.19, bf16[2048,128]{1,0:T(8,128)(2,1)} %bitcast.16, f32[512,128]{1,0:T(8,128)} %bitcast.23), custom_call_target="tpu_custom_call" | custom-call | tf_op jit(solution)/shard_map/own_columns/pallas_call | solution.py:399
  68.9 0.0 collective-permute-start.2
  68.9 18.8 %all-to-all-start.2 = ((bf16[64,2,16,128]{3,2,1,0:T(8,128)(2,1)}), bf16[64,2,16,128]{3,2,1,0:T(8,128)(2,1)S(1)}, u32[]{:S(2)}, u32[]{:S(2)}) async-start(bf16[64,2,16,128]{3,2,1,0:T(8,128)(2,1)} %bitcast.12), calls=%async_computation.2 | async-start | bytes 1048576 | tf_op jit(solution)/shard_map/all_to_all | solution.py:547
  87.7 11.7 %first_grads.1.refs_0_ = f32[32,2,64,128]{3,2,1,0:T(8,128)} custom-call(s32[1]{0:T(128)} %bitcast.half_ref, bf16[2,2048,128]{2,1,0:T(8,128)(2,1)} %own_columns.1.columns_ref, bf16[4096,128]{1,0:T(8,128)(2,1)} %w_in_ref.5, bf16[4096,128]{1,0:T(8,128)(2,1)} %get-tuple-element.19.w_out_t.w_out_ref), custom_call_target="tpu_custom_call" | custom-call | flops 100000000 | bytes 1048576 | tf_op jit(solution)/shard_map/first_grads/pallas_call | solution.py:440
  99.4 0.0 collective-permute-done.2.columns_ref
  99.5 0.0 copy-start.2
  99.5 1.0 copy-done.2
  100.4 12.0 %second_grads.1 = bf16[32,2,64,128]{3,2,1,0:T(8,128)(2,1)} custom-call(s32[1]{0:T(128)} %bitcast.half_ref, bf16[2,2048,128]{2,1,0:T(8,128)(2,1)} %copy-done.2, bf16[4096,128]{1,0:T(8,128)(2,1)} %w_in_ref.5, bf16[4096,128]{1,0:T(8,128)(2,1)} %get-tuple-element.19.w_out_t.w_out_ref, f32[32,2,64,128]{3,2,1,0:T(8,128)} %first_grads.1.refs_0_), custom_call_target="tpu_custom_call" | custom-call | flops 100000000 | bytes 1048576 | tf_op jit(solution)/shard_map/second_grads/pallas_call | solution.py:440
  112.4 0.0 all-to-all-done.2
  112.4 0.0 copy-start
  112.4 7.3 %all-to-all-start.3 = ((bf16[32,2,64,128]{3,2,1,0:T(8,128)(2,1)}), bf16[32,2,64,128]{3,2,1,0:T(8,128)(2,1)S(1)}, u32[]{:S(2)}, u32[]{:S(2)}) async-start(bf16[32,2,64,128]{3,2,1,0:T(8,128)(2,1)} %second_grads.1), calls=%async_computation.3 | async-start | bytes 2097152 | tf_op jit(solution)/shard_map/all_to_all | solution.py:547
  119.8 0.0 copy-done
  119.8 5.2 %spread_trajectory.1 = f32[8,256,128]{2,1,0:T(8,128)} custom-call(bf16[8,8,2,16,128]{4,3,2,1,0:T(8,128)(2,1)} %bitcast.15), custom_call_target="tpu_custom_call" | custom-call | tf_op jit(solution)/shard_map/spread_trajectory/pallas_call | solution.py:350
  125.0 11.7 %all-to-all-done.3.in_ref = bf16[32,2,64,128]{3,2,1,0:T(8,128)(2,1)S(1)} async-done(((bf16[32,2,64,128]{3,2,1,0:T(8,128)(2,1)}), bf16[32,2,64,128]{3,2,1,0:T(8,128)(2,1)S(1)}, u32[]{:S(2)}, u32[]{:S(2)}) %all-to-all-start.3) | async-done | bytes 1048608 | tf_op jit(solution)/shard_map/all_to_all | solution.py:547
  136.7 0.1 plane_sum.1.own_ref
  136.9 4.9 %collective-permute-start.5 = (bf16[2,64,128]{2,1,0:T(8,128)(2,1)S(1)}, bf16[2,64,128]{2,1,0:T(8,128)(2,1)S(1)}, u32[]{:S(2)}, u32[]{:S(2)}) collective-permute-start(bf16[2,64,128]{2,1,0:T(8,128)(2,1)S(1)} %plane_sum.1.own_ref), channel_id=1, source_target_pairs={{0,34},{2,32},{32,2},{34,0},{1,35},{3,33},{33,3},{35,1},{4,38},{6,... | collective-permute-start | bytes 98312 | tf_op jit(solution)/shard_map/ppermute | solution.py:584
  141.8 0.7 collective-permute-start.4
  142.4 1.7 collective-permute-start.3
  144.2 0.0 collective-permute-done.5.both_ref
  144.2 4.7 %collective-permute-done.4.far_ref = bf16[2,64,128]{2,1,0:T(8,128)(2,1)S(1)} collective-permute-done((bf16[2,64,128]{2,1,0:T(8,128)(2,1)S(1)}, bf16[2,64,128]{2,1,0:T(8,128)(2,1)S(1)}, u32[]{:S(2)}, u32[]{:S(2)}) %collective-permute-start.4) | collective-permute-done | bytes 32800 | tf_op jit(solution)/shard_map/ppermute | solution.py:584
  148.9 0.0 collective-permute-done.3.near_ref
  148.9 0.2 column_copies.1
  149.1 20.2 %all_to_all.25.code_ref = s16[32,144,128]{2,1,0:T(8,128)(2,1)S(1)} all-to-all(s16[32,144,128]{2,1,0:T(8,128)(2,1)S(1)} %column_copies.1), channel_id=1, replica_groups=mesh['sec'=4,'zh'=2,'cx'=4,'core'=2,'c1'=2,'c0'=2] {'sec','cx','c0'}, dimensions={0} | all-to-all | bytes 2359296 | tf_op jit(solution)/shard_map/all_to_all | solution.py:547
  169.2 3.2 %collective-permute-start.6 = (s16[32,144,128]{2,1,0:T(8,128)(2,1)S(1)}, s16[32,144,128]{2,1,0:T(8,128)(2,1)S(1)}, u32[]{:S(2)}, u32[]{:S(2)}) collective-permute-start(s16[32,144,128]{2,1,0:T(8,128)(2,1)S(1)} %all_to_all.25.code_ref), channel_id=1, source_target_pairs={{0,4},{4,0},{1,5},{5,1},{2,6},{6,2},{3,7},{7,3},{8,12},{12,8},{9,1... | collective-permute-start | bytes 3538952 | tf_op jit(solution)/shard_map/ppermute | solution.py:587
  172.5 1.4 finish_half.2
  173.9 1.0 collective-permute-done.6.code_ref
  174.9 1.4 finish_half.3
  (1 shorter events, 0.0 us)
Async XLA Ops:
  4.1 23.1 %all-to-all-start = ((s16[16,48,128]{2,1,0:T(8,128)(2,1)}), s16[16,48,128]{2,1,0:T(8,128)(2,1)S(1)}, u32[]{:S(2)}, u32[]{:S(2)}) async-start(s16[16,48,128]{2,1,0:T(8,128)(2,1)} %init_slabs.1), calls=%async_computation | async-start | bytes 393216 | tf_op jit(solution)/shard_map/all_to_all | solution.py:547
  27.2 16.4 %copy-start.3 = (s16[16,48,128]{2,1,0:T(8,128)(2,1)}, s16[16,48,128]{2,1,0:T(8,128)(2,1)S(1)}, u32[]{:S(2)}) copy-start(s16[16,48,128]{2,1,0:T(8,128)(2,1)S(1)} %all-to-all-done.msg_ref) | copy-start | bytes 589828
  27.2 37.1 %all-to-all-start.1 = ((bf16[64,2,16,128]{3,2,1,0:T(8,128)(2,1)}), bf16[64,2,16,128]{3,2,1,0:T(8,128)(2,1)S(1)}, u32[]{:S(2)}, u32[]{:S(2)}) async-start(bf16[64,2,16,128]{3,2,1,0:T(8,128)(2,1)} %bitcast.20), calls=%async_computation.1 | async-start | bytes 1048576 | tf_op jit(solution)/shard_map/all_to_all | solution.py:547
  36.3 6.0 %collective-permute-start.1 = (s16[16,16,128]{2,1,0:T(8,128)(2,1)S(1)}, s16[16,16,128]{2,1,0:T(8,128)(2,1)S(1)}, u32[]{:S(2)}, u32[]{:S(2)}) collective-permute-start(s16[16,16,128]{2,1,0:T(8,128)(2,1)S(1)} %get-tuple-element.33), channel_id=1, source_target_pairs={{4,0},{5,1},{6,2},{7,3},{8,4},{9,5},{10,6},{11,7},{12,8},{13,9},{1... | collective-permute-start | bytes 196616 | tf_op jit(solution)/shard_map/ppermute | solution.py:565
  38.6 4.9 %collective-permute-start = (s16[16,16,128]{2,1,0:T(8,128)(2,1)S(1)}, s16[16,16,128]{2,1,0:T(8,128)(2,1)S(1)}, u32[]{:S(2)}, u32[]{:S(2)}) collective-permute-start(s16[16,16,128]{2,1,0:T(8,128)(2,1)S(1)} %get-tuple-element.34), channel_id=1, source_target_pairs={{0,4},{1,5},{2,6},{3,7},{4,8},{5,9},{6,10},{7,11},{8,12},{9,13},{1... | collective-permute-start | bytes 196616 | tf_op jit(solution)/shard_map/ppermute | solution.py:564
  42.2 1.3 copy-start.4
  43.5 0.6 copy-start.5
  64.3 0.8 copy-start.1
  68.9 30.5 %collective-permute-start.2 = (bf16[2,2048,128]{2,1,0:T(8,128)(2,1)}, bf16[2,2048,128]{2,1,0:T(8,128)(2,1)S(1)}, u32[]{:S(2)}, u32[]{:S(2)}) collective-permute-start(bf16[2,2048,128]{2,1,0:T(8,128)(2,1)} %own_columns.1.columns_ref), channel_id=1, source_target_pairs={{0,4},{4,0},{1,5},{5,1},{2,6},{6,2},{3,7},{7,3},{8,12},{12,8},{9,1... | collective-permute-start | bytes 3145736 | tf_op jit(solution)/shard_map/ppermute | solution.py:576
  68.9 43.5 %all-to-all-start.2 = ((bf16[64,2,16,128]{3,2,1,0:T(8,128)(2,1)}), bf16[64,2,16,128]{3,2,1,0:T(8,128)(2,1)S(1)}, u32[]{:S(2)}, u32[]{:S(2)}) async-start(bf16[64,2,16,128]{3,2,1,0:T(8,128)(2,1)} %bitcast.12), calls=%async_computation.2 | async-start | bytes 1048576 | tf_op jit(solution)/shard_map/all_to_all | solution.py:547
  99.5 1.0 copy-start.2
  112.4 7.4 %copy-start = (bf16[64,2,16,128]{3,2,1,0:T(8,128)(2,1)}, bf16[64,2,16,128]{3,2,1,0:T(8,128)(2,1)S(1)}, u32[]{:S(2)}) copy-start(bf16[64,2,16,128]{3,2,1,0:T(8,128)(2,1)S(1)} %all-to-all-done.2) | copy-start | bytes 1572868
  112.4 24.3 %all-to-all-start.3 = ((bf16[32,2,64,128]{3,2,1,0:T(8,128)(2,1)}), bf16[32,2,64,128]{3,2,1,0:T(8,128)(2,1)S(1)}, u32[]{:S(2)}, u32[]{:S(2)}) async-start(bf16[32,2,64,128]{3,2,1,0:T(8,128)(2,1)} %second_grads.1), calls=%async_computation.3 | async-start | bytes 2097152 | tf_op jit(solution)/shard_map/all_to_all | solution.py:547
  136.9 7.3 %collective-permute-start.5 = (bf16[2,64,128]{2,1,0:T(8,128)(2,1)S(1)}, bf16[2,64,128]{2,1,0:T(8,128)(2,1)S(1)}, u32[]{:S(2)}, u32[]{:S(2)}) collective-permute-start(bf16[2,64,128]{2,1,0:T(8,128)(2,1)S(1)} %plane_sum.1.own_ref), channel_id=1, source_target_pairs={{0,34},{2,32},{32,2},{34,0},{1,35},{3,33},{33,3},{35,1},{4,38},{6,... | collective-permute-start | bytes 98312 | tf_op jit(solution)/shard_map/ppermute | solution.py:584
  141.8 7.1 %collective-permute-start.4 = (bf16[2,64,128]{2,1,0:T(8,128)(2,1)S(1)}, bf16[2,64,128]{2,1,0:T(8,128)(2,1)S(1)}, u32[]{:S(2)}, u32[]{:S(2)}) collective-permute-start(bf16[2,64,128]{2,1,0:T(8,128)(2,1)S(1)} %plane_sum.1.own_ref), channel_id=1, source_target_pairs={{0,32},{2,34},{32,0},{34,2},{1,33},{3,35},{33,1},{35,3},{4,36},{6,... | collective-permute-start | bytes 98312 | tf_op jit(solution)/shard_map/ppermute | solution.py:584
  142.4 6.4 %collective-permute-start.3 = (bf16[2,64,128]{2,1,0:T(8,128)(2,1)S(1)}, bf16[2,64,128]{2,1,0:T(8,128)(2,1)S(1)}, u32[]{:S(2)}, u32[]{:S(2)}) collective-permute-start(bf16[2,64,128]{2,1,0:T(8,128)(2,1)S(1)} %plane_sum.1.own_ref), channel_id=1, source_target_pairs={{0,2},{2,0},{32,34},{34,32},{1,3},{3,1},{33,35},{35,33},{4,6},{6,4... | collective-permute-start | bytes 98312 | tf_op jit(solution)/shard_map/ppermute | solution.py:584
  169.2 5.7 %collective-permute-start.6 = (s16[32,144,128]{2,1,0:T(8,128)(2,1)S(1)}, s16[32,144,128]{2,1,0:T(8,128)(2,1)S(1)}, u32[]{:S(2)}, u32[]{:S(2)}) collective-permute-start(s16[32,144,128]{2,1,0:T(8,128)(2,1)S(1)} %all_to_all.25.code_ref), channel_id=1, source_target_pairs={{0,4},{4,0},{1,5},{5,1},{2,6},{6,2},{3,7},{7,3},{8,12},{12,8},{9,1... | collective-permute-start | bytes 3538952 | tf_op jit(solution)/shard_map/ppermute | solution.py:587

commit v4 on v3

--- a/solution.py
+++ b/solution.py
@@ -136,19 +136,10 @@
     return jnp.stack(parts, axis=1).reshape(NX, 8, F)
 
 
-def split_dot(value, table):
-    high = value.astype(jnp.bfloat16)
-    low = (value - high.astype(jnp.float32)).astype(jnp.bfloat16)
-    both = jnp.concatenate([high, low], axis=1)
-    return jnp.dot(both, table[0 : 2 * F], preferred_element_type=jnp.float32) + jnp.dot(
-        high, table[2 * F :], preferred_element_type=jnp.float32
-    )
-
-
 def rollout_kernel(
     meta_ref, msg_ref, left_ref, right_ref, w_in_t, w_out_t, mode_ref, mode_t, diff_ref, stiff_ref,
     traj_ref, inputs_ref, tend_ref, own_wet_ref,
-    state, wet, modal, acc, x_scr, gain, pull, depth, depth_t, before, hidden,
+    state, wet, modal, acc, x_scr, gain, pull, depth, depth_t, before, hidden, split,
 ):
     for t in range(16):
         for n, (ref, base) in enumerate(
@@ -189,29 +180,43 @@
         gain[pl.ds(i, 1), :] = r
         pull[pl.ds(i, 1), :] = a * r
         u = 1.0 + a * (u * r)
-    diff = diff_ref[...].reshape(1, 1, F)
-    edge = jnp.zeros((1, SLAB, F), jnp.float32)
+    diff = diff_ref[...]
+
+    def put_split(x, value):
+        at = slice(x * SLAB, (x + 2) * SLAB)
+        high = value.astype(jnp.bfloat16)
+        split[at, 0:F] = high
+        split[at, F : 2 * F] = (value - high.astype(jnp.float32)).astype(jnp.bfloat16)
+
+    def transform(table):
+        return jnp.dot(
+            split[...], table[0 : 2 * F], preferred_element_type=jnp.float32
+        ) + jnp.dot(split[:, 0:F], table[2 * F :], preferred_element_type=jnp.float32)
+
     for step in range(STEPS):
-        now = state[...]
-        around = (
-            jnp.concatenate([edge, now[:-1]], axis=0)
-            + jnp.concatenate([now[1:], edge], axis=0)
-            + pltpu.roll(now, 1, 1)
-            + pltpu.roll(now, SLAB - 1, 1)
-            - 4.0 * now
-        )
-        smoothed = wet[...] * (now + diff * around)
-        modal[...] = split_dot(smoothed.reshape(NX * SLAB, F), mode_t).reshape(NX, SLAB, F)
+        for x in range(0, NX, 2):
+            pieces = []
+            for at in (x, x + 1):
+                here = state[at]
+                around = pltpu.roll(here, 1, 0) + pltpu.roll(here, SLAB - 1, 0) - 4.0 * here
+                if at > 0:
+                    around += state[at - 1]
+                if at < NX - 1:
+                    around += state[at + 1]
+                pieces.append(wet[at] * (here + diff * around))
+            put_split(x, jnp.concatenate(pieces, axis=0))
+        modal[...] = transform(mode_t).reshape(NX, SLAB, F)
         part = modal[0] * gain[pl.ds(0, 1), :]
         modal[0] = part
         for i in range(1, NX):
             part = modal[i] * gain[pl.ds(i, 1), :] + pull[pl.ds(i, 1), :] * part
             modal[i] = part
         for i in range(NX - 2, -1, -1):
+            behind = part
             part = modal[i] + pull[pl.ds(i, 1), :] * part
-            modal[i] = part
-        after = split_dot(modal[...].reshape(NX * SLAB, F), mode_ref).reshape(NX, SLAB, F)
-        after = wet[...] * after
+            if i % 2 == 0:
+                put_split(i, jnp.concatenate([part, behind], axis=0))
+        after = wet[...] * transform(mode_ref).reshape(NX, SLAB, F)
         inputs_ref[step] = after[:, :CHUNK].astype(jnp.bfloat16)
         extra = pack_halo(after[:, CHUNK:], step)
         count = OWN + extra.shape[0]
@@ -279,6 +284,7 @@
             pltpu.VMEM((3, 128, NX), jnp.float32),
             pltpu.VMEM((2, NX * SLAB, WIDE), jnp.float32),
             pltpu.VMEM((2, NX * SLAB, WIDE), jnp.bfloat16),
+            pltpu.VMEM((NX * SLAB, 2 * F), jnp.bfloat16),
         ],
         compiler_params=params(),
         cost_estimate=pl.CostEstimate(
@@ -389,20 +395,21 @@
 
 
 def columns_kernel(x_ref, tend_ref, target_ref, wet_ref, out_ref):
-    gap = wet_ref[...] * (tend_ref[...] - target_ref[...].astype(jnp.float32)) * GRAD_SCALE
-    out_ref[0] = x_ref[...]
-    out_ref[1] = gap.astype(jnp.bfloat16)
+    for r in range(0, COLS, 64):
+        at = slice(r, r + 64)
+        gap = tend_ref[at] - target_ref[at].astype(jnp.float32)
+        gap = wet_ref[r % OWN : r % OWN + 64] * gap * GRAD_SCALE
+        out_ref[0, at] = x_ref[at]
+        out_ref[1, at] = gap.astype(jnp.bfloat16)
 
 
 def own_columns(inputs, tend, target, wet):
-    rows = pl.BlockSpec((OWN, F), lambda i: (i, 0))
     return pl.pallas_call(
         columns_kernel,
-        grid=(STEPS,),
-        in_specs=[rows] * 3 + [pl.BlockSpec((OWN, F), lambda i: (0, 0))],
-        out_specs=pl.BlockSpec((2, OWN, F), lambda i: (0, i, 0)),
         out_shape=jax.ShapeDtypeStruct((2, COLS, F), jnp.bfloat16),
-        compiler_params=params(("arbitrary",)),
+        in_specs=[pl.BlockSpec(memory_space=pltpu.VMEM)] * 4,
+        out_specs=pl.BlockSpec(memory_space=pltpu.VMEM),
+        compiler_params=params(),
         name="own_columns",
     )(inputs, tend, target, wet)
 
@@ -561,10 +568,11 @@
         for c in range(4)
         if c + (j + 1) // 8 < 4
     ]
-    left = lax.ppermute(msg[:, 32:48], TILE + COL, forward)
-    right = lax.ppermute(msg[:, 0:16], TILE + COL, [(b, a) for a, b in forward])
-
     target, w_in_t, w_out_t = prepare(targets.reshape(MB, 2 * F, 128), w_in, w_out, plan)
+    last, first, target = lax.optimization_barrier((msg[:, 32:48], msg[:, 0:16], target))
+    left = lax.ppermute(last, TILE + COL, forward)
+    right = lax.ppermute(first, TILE + COL, [(b, a) for a, b in forward])
+    left, right, target = lax.optimization_barrier((left, right, target))
     target = swap(target.reshape(64, 2, CHUNK, F), ("sec",) + TILE).reshape(COLS, F)
 
     traj, inputs, tend, wet = rollout(meta, msg, left, right, w_in_t, w_out_t, diffusivity, stiffness)

time: 178 us -> 172 us (0.966)
  starting transfers between devices: 63.7 us -> 58.9 us
    all_to_all x4, starting transfers between devices: 47.6 us -> 45.2 us  [swap(): return lax.all_to_all(value, axes, split_axis=0, concat_axis=0, tiled=True)]
  transfers between devices with their start and end apart: 11 -> 11, of which waited for: 6 -> 6; matrix products, arithmetic and copies ran while one was open for 0% -> 0% of each run, Pallas kernels for 33% -> 34%
where the time goes in v4:
time: 172 us; the launch traced here: 171 us
  Pallas kernels  65 us (38%)
  starting transfers between devices  58.9 us (34%)
  waiting for transfers between devices  24.1 us (14%)
  blocking collectives  20 us (12%)
  local copies, waits for them, and re-layouts  1.79 us (1%)
    all_to_all x4, starting transfers between devices, swap(): return lax.all_to_all(value, axes, split_axis=0, concat_axis=0, tiled=True)  45.2 us
    pallas_call x2, Pallas kernels, half_grads(): pl.pallas_call(grad_kernel, grid_spec=pltpu.PrefetchScalarGridSpec(num_sc...  23.7 us
    pallas_call x1, Pallas kernels, rollout(): pl.pallas_call(rollout_kernel, out_shape=[jax.ShapeDtypeStruct((STEPS, NX...  20.4 us
    all_to_all x1, blocking collectives, swap(): return lax.all_to_all(value, axes, split_axis=0, concat_axis=0, tiled=True)  20 us
    all_to_all x4, waiting for transfers between devices, swap(): return lax.all_to_all(value, axes, split_axis=0, concat_axis=0, tiled=True)  15.5 us
    pallas_call x1, Pallas kernels, prepare(): pl.pallas_call(prepare_kernel, grid_spec=pltpu.PrefetchScalarGridSpec(num...  6.89 us
    ppermute x3, starting transfers between devices, local(): lax.ppermute(plane, ('zh', 'c1'), [(i, i ^ n) for i in range(4)])  5.74 us
    pallas_call x1, Pallas kernels, spread_trajectory(): pl.pallas_call(spread_kernel, grid=(MB,), in_specs=[pl.BlockSpec((1, 8, 2...  5.24 us
  transfers between devices with their start and end apart: 11, of which 6 were waited for; matrix products, arithmetic and copies ran while one was open for 0% of the time, Pallas kernels for 34%

profile of v4, /device:TPU:1, one launch (start us, length us, event | category | flops | bytes accessed | tf_op | source)
XLA Modules:
  0.0 171.2 jit_solution(5856151437884110563)
XLA Ops:
  0.6 0.7 pad_add_fusion.meta_ref
  1.3 2.8 %init_slabs.1 = s16[16,48,128]{2,1,0:T(8,128)(2,1)} custom-call(s32[2]{0:T(128)} %pad_add_fusion.meta_ref, s32[8]{0:T(128)} %plan_ref.3, f32[8,256,128]{2,1,0:T(8,128)} %bitcast.18, s32[2,128]{1,0:T(2,128)} %land_ref.1, s32[2,128]{1,0:T(2,128)} %levels_ref.1), custom_call_target="tpu_custom_call" | custom-call | tf_op jit(solution)/shard_map/init_slabs/pallas_call | solution.py:95
  4.1 12.4 %all-to-all-start = ((s16[16,48,128]{2,1,0:T(8,128)(2,1)}), s16[16,48,128]{2,1,0:T(8,128)(2,1)S(1)}, u32[]{:S(2)}, u32[]{:S(2)}) async-start(s16[16,48,128]{2,1,0:T(8,128)(2,1)} %init_slabs.1), calls=%async_computation | async-start | bytes 393216 | tf_op jit(solution)/shard_map/all_to_all | solution.py:554
  16.5 6.9 %prepare.1 = (bf16[8,8,2,16,128]{4,3,2,1,0:T(8,128)(2,1)}, bf16[128,4096]{1,0:T(8,128)(2,1)}, bf16[4096,128]{1,0:T(8,128)(2,1)}) custom-call(s32[8]{0:T(128)} %plan_ref.3, bf16[8,256,128]{2,1,0:T(8,128)(2,1)} %bitcast.21, bf16[4096,128]{1,0:T(8,128)(2,1)} %w_in_ref.5, bf16[128,4096]{1,0:T(8,128)(2,1)} %w_out_ref.1), custom_call_target="tpu_custom_call" | custom-call | bytes 6291456 | tf_op jit(solution)/shard_map/prepare/pallas_call | solution.py:321
  23.4 3.8 %all-to-all-done.msg_ref = s16[16,48,128]{2,1,0:T(8,128)(2,1)S(1)} async-done(((s16[16,48,128]{2,1,0:T(8,128)(2,1)}), s16[16,48,128]{2,1,0:T(8,128)(2,1)S(1)}, u32[]{:S(2)}, u32[]{:S(2)}) %all-to-all-start) | async-done | bytes 196640 | tf_op jit(solution)/shard_map/all_to_all | solution.py:554
  27.2 0.0 copy-start.3
  27.2 2.0 %collective-permute-start = (s16[16,16,128]{2,1,0:T(8,128)(2,1)S(1)}, s16[16,16,128]{2,1,0:T(8,128)(2,1)S(1)}, u32[]{:S(2)}, u32[]{:S(2)}) collective-permute-start(s16[16,16,128]{2,1,0:T(8,128)(2,1)S(1)} %get-tuple-element.25), channel_id=1, source_target_pairs={{0,4},{1,5},{2,6},{3,7},{4,8},{5,9},{6,10},{7,11},{8,12},{9,13},{1... | collective-permute-start | bytes 196616 | tf_op jit(solution)/shard_map/ppermute | solution.py:573
  29.2 2.3 %collective-permute-start.1 = (s16[16,16,128]{2,1,0:T(8,128)(2,1)S(1)}, s16[16,16,128]{2,1,0:T(8,128)(2,1)S(1)}, u32[]{:S(2)}, u32[]{:S(2)}) collective-permute-start(s16[16,16,128]{2,1,0:T(8,128)(2,1)S(1)} %get-tuple-element.26), channel_id=1, source_target_pairs={{4,0},{5,1},{6,2},{7,3},{8,4},{9,5},{10,6},{11,7},{12,8},{13,9},{1... | collective-permute-start | bytes 196616 | tf_op jit(solution)/shard_map/ppermute | solution.py:574
  31.5 0.0 collective-permute-done.left_ref
  31.5 0.0 copy-start.4
  31.5 3.2 %collective-permute-done.1.right_ref = s16[16,16,128]{2,1,0:T(8,128)(2,1)S(1)} collective-permute-done((s16[16,16,128]{2,1,0:T(8,128)(2,1)S(1)}, s16[16,16,128]{2,1,0:T(8,128)(2,1)S(1)}, u32[]{:S(2)}, u32[]{:S(2)}) %collective-permute-start.1) | collective-permute-done | bytes 65568 | tf_op jit(solution)/shard_map/ppermute | solution.py:574
  34.8 0.0 copy-start.5
  34.8 12.7 %all-to-all-start.1 = ((bf16[64,2,16,128]{3,2,1,0:T(8,128)(2,1)}), bf16[64,2,16,128]{3,2,1,0:T(8,128)(2,1)S(1)}, u32[]{:S(2)}, u32[]{:S(2)}) async-start(bf16[64,2,16,128]{3,2,1,0:T(8,128)(2,1)} %bitcast.20), calls=%async_computation.1 | async-start | bytes 1048576 | tf_op jit(solution)/shard_map/all_to_all | solution.py:554
  47.5 0.0 copy-done.3
  47.5 0.0 copy-done.4
  47.5 0.0 copy-done.5
  47.6 20.4 %rollout.1 = (bf16[4,32,16,128]{3,2,1,0:T(8,128)(2,1)}, bf16[4,32,16,128]{3,2,1,0:T(8,128)(2,1)}, f32[4,32,16,128]{3,2,1,0:T(8,128)}, f32[32,16,128]{2,1,0:T(8,128)}) custom-call(s32[2]{0:T(128)} %pad_add_fusion.meta_ref, s16[16,48,128]{2,1,0:T(8,128)(2,1)} %copy-done.3, s16[16,16,128]{2,1,0:T(8,128)(2,1)} %copy-done.4, s16[16,16,128]{2,1,0:T(8,128)(2,1)} %copy-done.5, ...), custom_call_target="tpu_custom_call" | custom-call | flops 5905580032 | bytes 6291456 | tf_op jit(solution)/shard_map/rollout/pallas_call | solution.py:265
  68.0 0.0 all-to-all-done.1
  68.0 0.0 copy-start.1
  68.0 0.8 copy-done.1
  68.8 2.7 %own_columns.1.columns_ref = bf16[2,2048,128]{2,1,0:T(8,128)(2,1)} custom-call(bf16[2048,128]{1,0:T(8,128)(2,1)} %bitcast.22, f32[2048,128]{1,0:T(8,128)} %bitcast.19, bf16[2048,128]{1,0:T(8,128)(2,1)} %bitcast.16, f32[512,128]{1,0:T(8,128)} %bitcast.23), custom_call_target="tpu_custom_call" | custom-call | tf_op jit(solution)/shard_map/own_columns/pallas_call | solution.py:407
  71.5 0.5 collective-permute-start.2
  72.0 12.5 %all-to-all-start.2 = ((bf16[64,2,16,128]{3,2,1,0:T(8,128)(2,1)}), bf16[64,2,16,128]{3,2,1,0:T(8,128)(2,1)S(1)}, u32[]{:S(2)}, u32[]{:S(2)}) async-start(bf16[64,2,16,128]{3,2,1,0:T(8,128)(2,1)} %bitcast.12), calls=%async_computation.2 | async-start | bytes 1048576 | tf_op jit(solution)/shard_map/all_to_all | solution.py:554
  84.5 11.7 %first_grads.1.refs_0_ = f32[32,2,64,128]{3,2,1,0:T(8,128)} custom-call(s32[1]{0:T(128)} %bitcast.half_ref, bf16[2,2048,128]{2,1,0:T(8,128)(2,1)} %own_columns.1.columns_ref, bf16[4096,128]{1,0:T(8,128)(2,1)} %w_in_ref.5, bf16[4096,128]{1,0:T(8,128)(2,1)} %get-tuple-element.31.w_out_t.w_out_ref), custom_call_target="tpu_custom_call" | custom-call | flops 100000000 | bytes 1048576 | tf_op jit(solution)/shard_map/first_grads/pallas_call | solution.py:447
  96.2 0.0 collective-permute-done.2.columns_ref
  96.2 0.0 copy-start.2
  96.2 1.0 copy-done.2
  97.2 12.0 %second_grads.1 = bf16[32,2,64,128]{3,2,1,0:T(8,128)(2,1)} custom-call(s32[1]{0:T(128)} %bitcast.half_ref, bf16[2,2048,128]{2,1,0:T(8,128)(2,1)} %copy-done.2, bf16[4096,128]{1,0:T(8,128)(2,1)} %w_in_ref.5, bf16[4096,128]{1,0:T(8,128)(2,1)} %get-tuple-element.31.w_out_t.w_out_ref, f32[32,2,64,128]{3,2,1,0:T(8,128)} %first_grads.1.refs_0_), custom_call_target="tpu_custom_call" | custom-call | flops 100000000 | bytes 1048576 | tf_op jit(solution)/shard_map/second_grads/pallas_call | solution.py:447
  109.2 0.0 all-to-all-done.2
  109.2 0.0 copy-start
  109.2 7.6 %all-to-all-start.3 = ((bf16[32,2,64,128]{3,2,1,0:T(8,128)(2,1)}), bf16[32,2,64,128]{3,2,1,0:T(8,128)(2,1)S(1)}, u32[]{:S(2)}, u32[]{:S(2)}) async-start(bf16[32,2,64,128]{3,2,1,0:T(8,128)(2,1)} %second_grads.1), calls=%async_computation.3 | async-start | bytes 2097152 | tf_op jit(solution)/shard_map/all_to_all | solution.py:554
  116.7 0.0 copy-done
  116.7 5.2 %spread_trajectory.1 = f32[8,256,128]{2,1,0:T(8,128)} custom-call(bf16[8,8,2,16,128]{4,3,2,1,0:T(8,128)(2,1)} %bitcast.15), custom_call_target="tpu_custom_call" | custom-call | tf_op jit(solution)/shard_map/spread_trajectory/pallas_call | solution.py:356
  122.0 11.7 %all-to-all-done.3.in_ref = bf16[32,2,64,128]{3,2,1,0:T(8,128)(2,1)S(1)} async-done(((bf16[32,2,64,128]{3,2,1,0:T(8,128)(2,1)}), bf16[32,2,64,128]{3,2,1,0:T(8,128)(2,1)S(1)}, u32[]{:S(2)}, u32[]{:S(2)}) %all-to-all-start.3) | async-done | bytes 1048608 | tf_op jit(solution)/shard_map/all_to_all | solution.py:554
  133.7 0.1 plane_sum.1.own_ref
  133.9 2.7 %collective-permute-start.5 = (bf16[2,64,128]{2,1,0:T(8,128)(2,1)S(1)}, bf16[2,64,128]{2,1,0:T(8,128)(2,1)S(1)}, u32[]{:S(2)}, u32[]{:S(2)}) collective-permute-start(bf16[2,64,128]{2,1,0:T(8,128)(2,1)S(1)} %plane_sum.1.own_ref), channel_id=1, source_target_pairs={{0,34},{2,32},{32,2},{34,0},{1,35},{3,33},{33,3},{35,1},{4,38},{6,... | collective-permute-start | bytes 98312 | tf_op jit(solution)/shard_map/ppermute | solution.py:592
  136.5 2.7 %collective-permute-start.4 = (bf16[2,64,128]{2,1,0:T(8,128)(2,1)S(1)}, bf16[2,64,128]{2,1,0:T(8,128)(2,1)S(1)}, u32[]{:S(2)}, u32[]{:S(2)}) collective-permute-start(bf16[2,64,128]{2,1,0:T(8,128)(2,1)S(1)} %plane_sum.1.own_ref), channel_id=1, source_target_pairs={{0,32},{2,34},{32,0},{34,2},{1,33},{3,35},{33,1},{35,3},{4,36},{6,... | collective-permute-start | bytes 98312 | tf_op jit(solution)/shard_map/ppermute | solution.py:592
  139.2 0.4 collective-permute-start.3
  139.6 0.0 collective-permute-done.5.both_ref
  139.6 3.6 %collective-permute-done.4.far_ref = bf16[2,64,128]{2,1,0:T(8,128)(2,1)S(1)} collective-permute-done((bf16[2,64,128]{2,1,0:T(8,128)(2,1)S(1)}, bf16[2,64,128]{2,1,0:T(8,128)(2,1)S(1)}, u32[]{:S(2)}, u32[]{:S(2)}) %collective-permute-start.4) | collective-permute-done | bytes 32800 | tf_op jit(solution)/shard_map/ppermute | solution.py:592
  143.2 0.7 collective-permute-done.3.near_ref
  143.9 0.2 column_copies.1
  144.1 20.0 %all_to_all.25.code_ref = s16[32,144,128]{2,1,0:T(8,128)(2,1)S(1)} all-to-all(s16[32,144,128]{2,1,0:T(8,128)(2,1)S(1)} %column_copies.1), channel_id=1, replica_groups=mesh['sec'=4,'zh'=2,'cx'=4,'core'=2,'c1'=2,'c0'=2] {'sec','cx','c0'}, dimensions={0} | all-to-all | bytes 2359296 | tf_op jit(solution)/shard_map/all_to_all | solution.py:554
  164.1 3.2 %collective-permute-start.6 = (s16[32,144,128]{2,1,0:T(8,128)(2,1)S(1)}, s16[32,144,128]{2,1,0:T(8,128)(2,1)S(1)}, u32[]{:S(2)}, u32[]{:S(2)}) collective-permute-start(s16[32,144,128]{2,1,0:T(8,128)(2,1)S(1)} %all_to_all.25.code_ref), channel_id=1, source_target_pairs={{0,4},{4,0},{1,5},{5,1},{2,6},{6,2},{3,7},{7,3},{8,12},{12,8},{9,1... | collective-permute-start | bytes 3538952 | tf_op jit(solution)/shard_map/ppermute | solution.py:595
  167.3 1.4 finish_half.2
  168.7 1.0 collective-permute-done.6.code_ref
  169.8 1.4 finish_half.3
  (1 shorter events, 0.0 us)
Async XLA Ops:
  4.1 23.1 %all-to-all-start = ((s16[16,48,128]{2,1,0:T(8,128)(2,1)}), s16[16,48,128]{2,1,0:T(8,128)(2,1)S(1)}, u32[]{:S(2)}, u32[]{:S(2)}) async-start(s16[16,48,128]{2,1,0:T(8,128)(2,1)} %init_slabs.1), calls=%async_computation | async-start | bytes 393216 | tf_op jit(solution)/shard_map/all_to_all | solution.py:554
  27.2 20.4 %copy-start.3 = (s16[16,48,128]{2,1,0:T(8,128)(2,1)}, s16[16,48,128]{2,1,0:T(8,128)(2,1)S(1)}, u32[]{:S(2)}) copy-start(s16[16,48,128]{2,1,0:T(8,128)(2,1)S(1)} %all-to-all-done.msg_ref) | copy-start | bytes 589828
  27.2 4.3 %collective-permute-start = (s16[16,16,128]{2,1,0:T(8,128)(2,1)S(1)}, s16[16,16,128]{2,1,0:T(8,128)(2,1)S(1)}, u32[]{:S(2)}, u32[]{:S(2)}) collective-permute-start(s16[16,16,128]{2,1,0:T(8,128)(2,1)S(1)} %get-tuple-element.25), channel_id=1, source_target_pairs={{0,4},{1,5},{2,6},{3,7},{4,8},{5,9},{6,10},{7,11},{8,12},{9,13},{1... | collective-permute-start | bytes 196616 | tf_op jit(solution)/shard_map/ppermute | solution.py:573
  29.2 5.6 %collective-permute-start.1 = (s16[16,16,128]{2,1,0:T(8,128)(2,1)S(1)}, s16[16,16,128]{2,1,0:T(8,128)(2,1)S(1)}, u32[]{:S(2)}, u32[]{:S(2)}) collective-permute-start(s16[16,16,128]{2,1,0:T(8,128)(2,1)S(1)} %get-tuple-element.26), channel_id=1, source_target_pairs={{4,0},{5,1},{6,2},{7,3},{8,4},{9,5},{10,6},{11,7},{12,8},{13,9},{1... | collective-permute-start | bytes 196616 | tf_op jit(solution)/shard_map/ppermute | solution.py:574
  31.5 16.0 %copy-start.4 = (s16[16,16,128]{2,1,0:T(8,128)(2,1)}, s16[16,16,128]{2,1,0:T(8,128)(2,1)S(1)}, u32[]{:S(2)}) copy-start(s16[16,16,128]{2,1,0:T(8,128)(2,1)S(1)} %collective-permute-done.left_ref) | copy-start | bytes 196612
  34.8 12.8 %copy-start.5 = (s16[16,16,128]{2,1,0:T(8,128)(2,1)}, s16[16,16,128]{2,1,0:T(8,128)(2,1)S(1)}, u32[]{:S(2)}) copy-start(s16[16,16,128]{2,1,0:T(8,128)(2,1)S(1)} %collective-permute-done.1.right_ref) | copy-start | bytes 196612
  34.8 33.2 %all-to-all-start.1 = ((bf16[64,2,16,128]{3,2,1,0:T(8,128)(2,1)}), bf16[64,2,16,128]{3,2,1,0:T(8,128)(2,1)S(1)}, u32[]{:S(2)}, u32[]{:S(2)}) async-start(bf16[64,2,16,128]{3,2,1,0:T(8,128)(2,1)} %bitcast.20), calls=%async_computation.1 | async-start | bytes 1048576 | tf_op jit(solution)/shard_map/all_to_all | solution.py:554
  68.0 0.8 copy-start.1
  71.5 24.7 %collective-permute-start.2 = (bf16[2,2048,128]{2,1,0:T(8,128)(2,1)}, bf16[2,2048,128]{2,1,0:T(8,128)(2,1)S(1)}, u32[]{:S(2)}, u32[]{:S(2)}) collective-permute-start(bf16[2,2048,128]{2,1,0:T(8,128)(2,1)} %own_columns.1.columns_ref), channel_id=1, source_target_pairs={{0,4},{4,0},{1,5},{5,1},{2,6},{6,2},{3,7},{7,3},{8,12},{12,8},{9,1... | collective-permute-start | bytes 3145736 | tf_op jit(solution)/shard_map/ppermute | solution.py:584
  72.0 37.2 %all-to-all-start.2 = ((bf16[64,2,16,128]{3,2,1,0:T(8,128)(2,1)}), bf16[64,2,16,128]{3,2,1,0:T(8,128)(2,1)S(1)}, u32[]{:S(2)}, u32[]{:S(2)}) async-start(bf16[64,2,16,128]{3,2,1,0:T(8,128)(2,1)} %bitcast.12), calls=%async_computation.2 | async-start | bytes 1048576 | tf_op jit(solution)/shard_map/all_to_all | solution.py:554
  96.2 1.0 copy-start.2
  109.2 7.6 %copy-start = (bf16[64,2,16,128]{3,2,1,0:T(8,128)(2,1)}, bf16[64,2,16,128]{3,2,1,0:T(8,128)(2,1)S(1)}, u32[]{:S(2)}) copy-start(bf16[64,2,16,128]{3,2,1,0:T(8,128)(2,1)S(1)} %all-to-all-done.2) | copy-start | bytes 1572868
  109.2 24.5 %all-to-all-start.3 = ((bf16[32,2,64,128]{3,2,1,0:T(8,128)(2,1)}), bf16[32,2,64,128]{3,2,1,0:T(8,128)(2,1)S(1)}, u32[]{:S(2)}, u32[]{:S(2)}) async-start(bf16[32,2,64,128]{3,2,1,0:T(8,128)(2,1)} %second_grads.1), calls=%async_computation.3 | async-start | bytes 2097152 | tf_op jit(solution)/shard_map/all_to_all | solution.py:554
  133.9 5.7 %collective-permute-start.5 = (bf16[2,64,128]{2,1,0:T(8,128)(2,1)S(1)}, bf16[2,64,128]{2,1,0:T(8,128)(2,1)S(1)}, u32[]{:S(2)}, u32[]{:S(2)}) collective-permute-start(bf16[2,64,128]{2,1,0:T(8,128)(2,1)S(1)} %plane_sum.1.own_ref), channel_id=1, source_target_pairs={{0,34},{2,32},{32,2},{34,0},{1,35},{3,33},{33,3},{35,1},{4,38},{6,... | collective-permute-start | bytes 98312 | tf_op jit(solution)/shard_map/ppermute | solution.py:592
  136.5 6.7 %collective-permute-start.4 = (bf16[2,64,128]{2,1,0:T(8,128)(2,1)S(1)}, bf16[2,64,128]{2,1,0:T(8,128)(2,1)S(1)}, u32[]{:S(2)}, u32[]{:S(2)}) collective-permute-start(bf16[2,64,128]{2,1,0:T(8,128)(2,1)S(1)} %plane_sum.1.own_ref), channel_id=1, source_target_pairs={{0,32},{2,34},{32,0},{34,2},{1,33},{3,35},{33,1},{35,3},{4,36},{6,... | collective-permute-start | bytes 98312 | tf_op jit(solution)/shard_map/ppermute | solution.py:592
  139.2 4.7 %collective-permute-start.3 = (bf16[2,64,128]{2,1,0:T(8,128)(2,1)S(1)}, bf16[2,64,128]{2,1,0:T(8,128)(2,1)S(1)}, u32[]{:S(2)}, u32[]{:S(2)}) collective-permute-start(bf16[2,64,128]{2,1,0:T(8,128)(2,1)S(1)} %plane_sum.1.own_ref), channel_id=1, source_target_pairs={{0,2},{2,0},{32,34},{34,32},{1,3},{3,1},{33,35},{35,33},{4,6},{6,4... | collective-permute-start | bytes 98312 | tf_op jit(solution)/shard_map/ppermute | solution.py:592
  164.1 5.7 %collective-permute-start.6 = (s16[32,144,128]{2,1,0:T(8,128)(2,1)S(1)}, s16[32,144,128]{2,1,0:T(8,128)(2,1)S(1)}, u32[]{:S(2)}, u32[]{:S(2)}) collective-permute-start(s16[32,144,128]{2,1,0:T(8,128)(2,1)S(1)} %all_to_all.25.code_ref), channel_id=1, source_target_pairs={{0,4},{4,0},{1,5},{5,1},{2,6},{6,2},{3,7},{7,3},{8,12},{12,8},{9,1... | collective-permute-start | bytes 3538952 | tf_op jit(solution)/shard_map/ppermute | solution.py:595

commit v5 on v4

--- a/solution.py
+++ b/solution.py
@@ -75,7 +75,7 @@
     return value * (jnp.exp2(power - 15.0) * UNIT)
 
 
-def init_kernel(meta_ref, plan_ref, state_ref, land_ref, levels_ref, msg_ref):
+def init_kernel(section_ref, plan_ref, state_ref, land_ref, levels_ref, msg_ref):
     power = exponent(jnp.max(jnp.abs(state_ref[0]), keepdims=True))
     code = [encode(state_ref[0, pl.ds(x, F, stride=2), :], power).T for x in range(2)]
     depth = jnp.where(land_ref[...] == 1, levels_ref[...], 0).astype(jnp.float32)
@@ -90,24 +90,24 @@
         msg_ref[j] = to_int16(jnp.concatenate(first + [extra] + middle + last + [extra], axis=0))
 
 
-def init_slabs(meta, plan, states, land_mask, wet_levels):
-    whole = lambda i, meta, plan: (0, 0)
+def init_slabs(section, plan, states, land_mask, wet_levels):
+    whole = lambda i, sec, plan: (0, 0)
     return pl.pallas_call(
         init_kernel,
         grid_spec=pltpu.PrefetchScalarGridSpec(
             num_scalar_prefetch=2,
             grid=(2,),
             in_specs=[
-                pl.BlockSpec((1, 2 * F, 128), lambda i, meta, plan: (plan[2 * meta[0] + i], 0, 0)),
+                pl.BlockSpec((1, 2 * F, 128), lambda i, sec, plan: (plan[2 * sec[0] + i], 0, 0)),
                 pl.BlockSpec((2, 128), whole),
                 pl.BlockSpec((2, 128), whole),
             ],
-            out_specs=pl.BlockSpec((8, MSG, F), lambda i, meta, plan: (i, 0, 0)),
+            out_specs=pl.BlockSpec((8, MSG, F), lambda i, sec, plan: (i, 0, 0)),
         ),
         out_shape=jax.ShapeDtypeStruct((16, MSG, F), jnp.int16),
         compiler_params=params(("arbitrary",)),
         name="init_slabs",
-    )(meta, plan, states, land_mask, wet_levels)
+    )(section, plan, states, land_mask, wet_levels)
 
 
 def levels():
@@ -137,7 +137,7 @@
 
 
 def rollout_kernel(
-    meta_ref, msg_ref, left_ref, right_ref, w_in_t, w_out_t, mode_ref, mode_t, diff_ref, stiff_ref,
+    chunk_ref, msg_ref, left_ref, right_ref, w_in_t, w_out_t, mode_ref, mode_t, diff_ref, stiff_ref,
     traj_ref, inputs_ref, tend_ref, own_wet_ref,
     state, wet, modal, acc, x_scr, gain, pull, depth, depth_t, before, hidden, split,
 ):
@@ -156,7 +156,7 @@
                 depth[n // 2 if n else 0, 2 * t : 2 * t + 2] = piece[8:10]
     for n in range(3):
         depth_t[n] = depth[n].T
-    mine = meta_ref[1]
+    mine = chunk_ref[0]
     y_own = pl.multiple_of(mine * CHUNK, CHUNK)
     y_right = pl.multiple_of(lax.rem(mine + 1, 8) * CHUNK, CHUNK)
     y_left = pl.multiple_of(lax.rem(mine + 7, 8) * CHUNK + 8, 8)
@@ -259,7 +259,7 @@
             state[:, :CHUNK] = result
 
 
-def rollout(meta, msg, left, right, w_in_t, w_out_t, diffusivity, stiffness):
+def rollout(chunk, msg, left, right, w_in_t, w_out_t, diffusivity, stiffness):
     block = mode_block()
     vmem = pl.BlockSpec(memory_space=pltpu.VMEM)
     return pl.pallas_call(
@@ -292,7 +292,7 @@
         ),
         name="rollout",
     )(
-        meta,
+        chunk,
         msg,
         left,
         right,
@@ -364,32 +364,36 @@
     )(arrived)
 
 
-def grad_block(x_ref, x_t, misfit, misfit_t, w_in_ref, w_out_t_ref, scratch):
+def grad_block(columns, w_in_ref, w_out_t_ref, scratch):
     before, back, hidden, change = scratch
     rows = w_in_ref.shape[0]
-
-    def front(part):
-        at = slice(part * WIDE, (part + 1) * WIDE)
-        before[part % 2] = jnp.dot(w_in_ref[...], x_t[:, at], preferred_element_type=jnp.float32)
-        back[part % 2] = jnp.dot(
+    parts = [
+        (refs, slice(part * WIDE, (part + 1) * WIDE))
+        for refs in columns
+        for part in range(COLS // WIDE)
+    ]
+
+    def front(n):
+        (_, x_t, _, misfit_t), at = parts[n]
+        before[n % 2] = jnp.dot(w_in_ref[...], x_t[:, at], preferred_element_type=jnp.float32)
+        back[n % 2] = jnp.dot(
             w_out_t_ref[...], misfit_t[:, at], preferred_element_type=jnp.float32
         )
-        return at
 
     grad_in = jnp.zeros((rows, F), jnp.float32)
     grad_out = jnp.zeros((rows, F), jnp.float32)
-    at = front(0)
-    for part in range(COLS // WIDE):
-        following = front(part + 1) if part + 1 < COLS // WIDE else None
-        n = part % 2
+    front(0)
+    for n, ((x_ref, _, misfit, _), at) in enumerate(parts):
+        if n + 1 < len(parts):
+            front(n + 1)
+        m = n % 2
         for r in range(0, rows, STRIP):
-            strip = jnp.tanh(before[n, r : r + STRIP])
-            hidden[n, r : r + STRIP] = strip.astype(jnp.bfloat16)
-            strip = back[n, r : r + STRIP] * (1.0 - strip * strip)
-            change[n, r : r + STRIP] = strip.astype(jnp.bfloat16)
-        grad_out += jnp.dot(hidden[n], misfit[at], preferred_element_type=jnp.float32)
-        grad_in += jnp.dot(change[n], x_ref[at], preferred_element_type=jnp.float32)
-        at = following
+            strip = jnp.tanh(before[m, r : r + STRIP])
+            hidden[m, r : r + STRIP] = strip.astype(jnp.bfloat16)
+            strip = back[m, r : r + STRIP] * (1.0 - strip * strip)
+            change[m, r : r + STRIP] = strip.astype(jnp.bfloat16)
+        grad_out += jnp.dot(hidden[m], misfit[at], preferred_element_type=jnp.float32)
+        grad_in += jnp.dot(change[m], x_ref[at], preferred_element_type=jnp.float32)
     shape = (rows // ROWS, ROWS, F)
     return grad_in.reshape(shape), grad_out.reshape(shape)
 
@@ -414,55 +418,46 @@
     )(inputs, tend, target, wet)
 
 
-def grad_kernel(half_ref, columns_ref, w_in_ref, w_out_ref, *refs):
-    *add_ref, out_ref, x_t, misfit_t, before, back, hidden, change = refs
+def grad_kernel(half_ref, own_ref, their_ref, w_in_ref, w_out_ref, out_ref, turned, *scratch):
+    both = (own_ref, their_ref)
 
     @pl.when(pl.program_id(0) == 0)
     def _():
-        for part in range(STEPS):
-            at = slice(part * OWN, (part + 1) * OWN)
-            x_t[:, at] = columns_ref[0, at].T
-            misfit_t[:, at] = columns_ref[1, at].T
-
-    grads = grad_block(
-        columns_ref.at[0],
-        x_t,
-        columns_ref.at[1],
-        misfit_t,
-        w_in_ref,
-        w_out_ref,
-        (before, back, hidden, change),
-    )
-    for n, grad in enumerate(grads):
-        if add_ref:
-            grad = grad + add_ref[0][:, n]
-        out_ref[:, n] = grad.astype(out_ref.dtype)
-
-
-def half_grads(half, columns, w_in, w_out_t, add=None):
+        for n, ref in enumerate(both):
+            for part in range(STEPS):
+                at = slice(part * OWN, (part + 1) * OWN)
+                turned[n, 0, :, at] = ref[0, at].T
+                turned[n, 1, :, at] = ref[1, at].T
+
+    columns = [
+        (ref.at[0], turned.at[n, 0], ref.at[1], turned.at[n, 1]) for n, ref in enumerate(both)
+    ]
+    for n, grad in enumerate(grad_block(columns, w_in_ref, w_out_ref, scratch)):
+        out_ref[:, n] = grad.astype(jnp.bfloat16)
+
+
+def half_grads(half, own, theirs, w_in, w_out_t):
     blocks = HALF // HB2
     weight = pl.BlockSpec((HB2, F), lambda i, half: (half[0] * blocks + i, 0))
-    rows = pl.BlockSpec((HB2 // ROWS, 2, ROWS, F), lambda i, half: (i, 0, 0, 0))
-    first = add is None
+    whole = pl.BlockSpec((2, COLS, F), lambda i, half: (0, 0, 0))
     return pl.pallas_call(
         grad_kernel,
         grid_spec=pltpu.PrefetchScalarGridSpec(
             num_scalar_prefetch=1,
             grid=(blocks,),
-            in_specs=[pl.BlockSpec((2, COLS, F), lambda i, half: (0, 0, 0)), weight, weight]
-            + ([] if first else [rows]),
-            out_specs=rows,
-            scratch_shapes=[pltpu.VMEM((F, COLS), jnp.bfloat16)] * 2
+            in_specs=[whole, whole, weight, weight],
+            out_specs=pl.BlockSpec((HB2 // ROWS, 2, ROWS, F), lambda i, half: (i, 0, 0, 0)),
+            scratch_shapes=[pltpu.VMEM((2, 2, F, COLS), jnp.bfloat16)]
             + [pltpu.VMEM((2, HB2, WIDE), jnp.float32)] * 2
             + [pltpu.VMEM((2, HB2, WIDE), jnp.bfloat16)] * 2,
         ),
-        out_shape=jax.ShapeDtypeStruct(
-            (PARTS, 2, ROWS, F), jnp.float32 if first else jnp.bfloat16
+        out_shape=jax.ShapeDtypeStruct((PARTS, 2, ROWS, F), jnp.bfloat16),
+        compiler_params=params(("arbitrary",)),
+        cost_estimate=pl.CostEstimate(
+            flops=16 * COLS * F * HALF, bytes_accessed=5 * 2**20, transcendentals=2 * COLS * HALF
         ),
-        compiler_params=params(("arbitrary",)),
-        cost_estimate=pl.CostEstimate(flops=10**8, bytes_accessed=2**20, transcendentals=0),
-        name="first_grads" if first else "second_grads",
-    )(half, columns, w_in, w_out_t, *(() if first else (add,)))
+        name="half_grads",
+    )(half, own, theirs, w_in, w_out_t)
 
 
 def plane_kernel(in_ref, out_ref):
@@ -556,10 +551,11 @@
 
 def local(initial_states, targets, w_in, w_out, diffusivity, stiffness, land_mask, wet_levels, plan):
     core = lax.axis_index("core").astype(jnp.int32).reshape(1)
-    meta = jnp.stack([lax.axis_index("sec"), lax.axis_index(TILE) % 8]).astype(jnp.int32)
+    section = lax.axis_index("sec").astype(jnp.int32).reshape(1)
+    chunk = (lax.axis_index(("cx", "core"))).astype(jnp.int32).reshape(1)
 
     states = initial_states.reshape(MB, 2 * F, 128)
-    msg = swap(init_slabs(meta, plan, states, land_mask, wet_levels), TILE)
+    msg = swap(init_slabs(section, plan, states, land_mask, wet_levels), TILE)
     place = lambda half, chunk, col: (half * 8 + chunk) * 4 + col
     forward = [
         (place(h, j, c), place(h, (j + 1) % 8, c + (j + 1) // 8))
@@ -575,14 +571,14 @@
     left, right, target = lax.optimization_barrier((left, right, target))
     target = swap(target.reshape(64, 2, CHUNK, F), ("sec",) + TILE).reshape(COLS, F)
 
-    traj, inputs, tend, wet = rollout(meta, msg, left, right, w_in_t, w_out_t, diffusivity, stiffness)
+    traj, inputs, tend, wet = rollout(chunk, msg, left, right, w_in_t, w_out_t, diffusivity, stiffness)
     arrived = swap(traj.reshape(64, 2, CHUNK, F), ("sec",) + TILE)
 
     own = own_columns(
         inputs.reshape(COLS, F), tend.reshape(COLS, F), target, wet.reshape(OWN, F)
     )
     theirs = lax.ppermute(own, "core", [(0, 1), (1, 0)])
-    pair = half_grads(core, theirs, w_in, w_out_t, half_grads(core, own, w_in, w_out_t))
+    pair = half_grads(core, own, theirs, w_in, w_out_t)
     pair, arrived = lax.optimization_barrier((pair, arrived))
 
     trajectory = spread_trajectory(arrived.reshape(MB, 8, 2, CHUNK, F))

time: 172 us -> 169 us (0.983)
  Pallas kernels: 65 us -> 62.1 us
    pallas_call x2 -> x1, Pallas kernels: 23.7 us -> 20.9 us  [half_grads(): pl.pallas_call(grad_kernel, grid_spec=pltpu.PrefetchScalarGridSpec(num_sc...]
  transfers between devices with their start and end apart: 11 -> 11, of which waited for: 6 -> 6; matrix products, arithmetic and copies ran while one was open for 0% -> 0% of each run, Pallas kernels for 34% -> 33%
where the time goes in v5:
time: 169 us; the launch traced here: 168 us
  Pallas kernels  62.1 us (37%)
  starting transfers between devices  58.9 us (35%)
  waiting for transfers between devices  24.1 us (14%)
  blocking collectives  20 us (12%)
  local copies, waits for them, and re-layouts  1.79 us (1%)
    all_to_all x4, starting transfers between devices, swap(): return lax.all_to_all(value, axes, split_axis=0, concat_axis=0, tiled=True)  45.2 us
    pallas_call x1, Pallas kernels, half_grads(): pl.pallas_call(grad_kernel, grid_spec=pltpu.PrefetchScalarGridSpec(num_sc...  20.9 us
    pallas_call x1, Pallas kernels, rollout(): pl.pallas_call(rollout_kernel, out_shape=[jax.ShapeDtypeStruct((STEPS, NX...  20.4 us
    all_to_all x1, blocking collectives, swap(): return lax.all_to_all(value, axes, split_axis=0, concat_axis=0, tiled=True)  20 us
    all_to_all x4, waiting for transfers between devices, swap(): return lax.all_to_all(value, axes, split_axis=0, concat_axis=0, tiled=True)  15.5 us
    pallas_call x1, Pallas kernels, prepare(): pl.pallas_call(prepare_kernel, grid_spec=pltpu.PrefetchScalarGridSpec(num...  6.89 us
    ppermute x3, starting transfers between devices, local(): lax.ppermute(plane, ('zh', 'c1'), [(i, i ^ n) for i in range(4)])  5.74 us
    pallas_call x1, Pallas kernels, spread_trajectory(): pl.pallas_call(spread_kernel, grid=(MB,), in_specs=[pl.BlockSpec((1, 8, 2...  5.24 us
  transfers between devices with their start and end apart: 11, of which 6 were waited for; matrix products, arithmetic and copies ran while one was open for 0% of the time, Pallas kernels for 33%

profile of v5, /device:TPU:1, one launch (start us, length us, event | category | flops | bytes accessed | tf_op | source)
XLA Modules:
  0.0 167.7 jit_solution(1936233691933224319)
XLA Ops:
  0.6 2.8 %init_slabs.1 = s16[16,48,128]{2,1,0:T(8,128)(2,1)} custom-call(s32[1]{0:T(128)} %bitcast.2.section_ref, s32[8]{0:T(128)} %plan_ref.3, f32[8,256,128]{2,1,0:T(8,128)} %bitcast.18, s32[2,128]{1,0:T(2,128)} %land_ref.1, s32[2,128]{1,0:T(2,128)} %levels_ref.1), custom_call_target="tpu_custom_call" | custom-call | tf_op jit(solution)/shard_map/init_slabs/pallas_call | solution.py:95
  3.4 12.4 %all-to-all-start = ((s16[16,48,128]{2,1,0:T(8,128)(2,1)}), s16[16,48,128]{2,1,0:T(8,128)(2,1)S(1)}, u32[]{:S(2)}, u32[]{:S(2)}) async-start(s16[16,48,128]{2,1,0:T(8,128)(2,1)} %init_slabs.1), calls=%async_computation | async-start | bytes 393216 | tf_op jit(solution)/shard_map/all_to_all | solution.py:549
  15.8 6.9 %prepare.1 = (bf16[8,8,2,16,128]{4,3,2,1,0:T(8,128)(2,1)}, bf16[128,4096]{1,0:T(8,128)(2,1)}, bf16[4096,128]{1,0:T(8,128)(2,1)}) custom-call(s32[8]{0:T(128)} %plan_ref.3, bf16[8,256,128]{2,1,0:T(8,128)(2,1)} %bitcast.21, bf16[4096,128]{1,0:T(8,128)(2,1)} %w_in_ref.3, bf16[128,4096]{1,0:T(8,128)(2,1)} %w_out_ref.1), custom_call_target="tpu_custom_call" | custom-call | bytes 6291456 | tf_op jit(solution)/shard_map/prepare/pallas_call | solution.py:321
  22.7 3.8 %all-to-all-done.msg_ref = s16[16,48,128]{2,1,0:T(8,128)(2,1)S(1)} async-done(((s16[16,48,128]{2,1,0:T(8,128)(2,1)}), s16[16,48,128]{2,1,0:T(8,128)(2,1)S(1)}, u32[]{:S(2)}, u32[]{:S(2)}) %all-to-all-start) | async-done | bytes 196640 | tf_op jit(solution)/shard_map/all_to_all | solution.py:549
  26.5 0.0 copy-start.2
  26.5 2.0 %collective-permute-start = (s16[16,16,128]{2,1,0:T(8,128)(2,1)S(1)}, s16[16,16,128]{2,1,0:T(8,128)(2,1)S(1)}, u32[]{:S(2)}, u32[]{:S(2)}) collective-permute-start(s16[16,16,128]{2,1,0:T(8,128)(2,1)S(1)} %get-tuple-element.25), channel_id=1, source_target_pairs={{0,4},{1,5},{2,6},{3,7},{4,8},{5,9},{6,10},{7,11},{8,12},{9,13},{1... | collective-permute-start | bytes 196616 | tf_op jit(solution)/shard_map/ppermute | solution.py:569
  28.5 2.3 %collective-permute-start.1 = (s16[16,16,128]{2,1,0:T(8,128)(2,1)S(1)}, s16[16,16,128]{2,1,0:T(8,128)(2,1)S(1)}, u32[]{:S(2)}, u32[]{:S(2)}) collective-permute-start(s16[16,16,128]{2,1,0:T(8,128)(2,1)S(1)} %get-tuple-element.26), channel_id=1, source_target_pairs={{4,0},{5,1},{6,2},{7,3},{8,4},{9,5},{10,6},{11,7},{12,8},{13,9},{1... | collective-permute-start | bytes 196616 | tf_op jit(solution)/shard_map/ppermute | solution.py:570
  30.8 0.0 collective-permute-done.left_ref
  30.9 0.0 copy-start.4
  30.9 3.2 %collective-permute-done.1.right_ref = s16[16,16,128]{2,1,0:T(8,128)(2,1)S(1)} collective-permute-done((s16[16,16,128]{2,1,0:T(8,128)(2,1)S(1)}, s16[16,16,128]{2,1,0:T(8,128)(2,1)S(1)}, u32[]{:S(2)}, u32[]{:S(2)}) %collective-permute-start.1) | collective-permute-done | bytes 65568 | tf_op jit(solution)/shard_map/ppermute | solution.py:570
  34.1 0.0 copy-start.5
  34.1 12.7 %all-to-all-start.1 = ((bf16[64,2,16,128]{3,2,1,0:T(8,128)(2,1)}), bf16[64,2,16,128]{3,2,1,0:T(8,128)(2,1)S(1)}, u32[]{:S(2)}, u32[]{:S(2)}) async-start(bf16[64,2,16,128]{3,2,1,0:T(8,128)(2,1)} %bitcast.20), calls=%async_computation.1 | async-start | bytes 1048576 | tf_op jit(solution)/shard_map/all_to_all | solution.py:549
  46.9 0.0 copy-done.2
  46.9 0.0 copy-done.4
  46.9 0.0 copy-done.5
  46.9 20.4 %rollout.1 = (bf16[4,32,16,128]{3,2,1,0:T(8,128)(2,1)}, bf16[4,32,16,128]{3,2,1,0:T(8,128)(2,1)}, f32[4,32,16,128]{3,2,1,0:T(8,128)}, f32[32,16,128]{2,1,0:T(8,128)}) custom-call(s32[1]{0:T(128)} %bitcast.1.chunk_ref, s16[16,48,128]{2,1,0:T(8,128)(2,1)} %copy-done.2, s16[16,16,128]{2,1,0:T(8,128)(2,1)} %copy-done.4, s16[16,16,128]{2,1,0:T(8,128)(2,1)} %copy-done.5, ...), custom_call_target="tpu_custom_call" | custom-call | flops 5905580032 | bytes 6291456 | tf_op jit(solution)/shard_map/rollout/pallas_call | solution.py:265
  67.3 0.0 all-to-all-done.1
  67.3 0.0 copy-start.1
  67.3 0.8 copy-done.1
  68.1 2.7 %own_columns.1.own_ref = bf16[2,2048,128]{2,1,0:T(8,128)(2,1)} custom-call(bf16[2048,128]{1,0:T(8,128)(2,1)} %bitcast.22, f32[2048,128]{1,0:T(8,128)} %bitcast.19, bf16[2048,128]{1,0:T(8,128)(2,1)} %bitcast.16, f32[512,128]{1,0:T(8,128)} %bitcast.23), custom_call_target="tpu_custom_call" | custom-call | tf_op jit(solution)/shard_map/own_columns/pallas_call | solution.py:411
  70.9 0.5 collective-permute-start.2
  71.3 12.5 %all-to-all-start.2 = ((bf16[64,2,16,128]{3,2,1,0:T(8,128)(2,1)}), bf16[64,2,16,128]{3,2,1,0:T(8,128)(2,1)S(1)}, u32[]{:S(2)}, u32[]{:S(2)}) async-start(bf16[64,2,16,128]{3,2,1,0:T(8,128)(2,1)} %bitcast.12), calls=%async_computation.2 | async-start | bytes 1048576 | tf_op jit(solution)/shard_map/all_to_all | solution.py:549
  83.8 0.0 collective-permute-done.2.their_ref
  83.8 0.0 copy-start.3
  83.8 1.0 copy-done.3
  84.8 20.9 %half_grads.1 = bf16[32,2,64,128]{3,2,1,0:T(8,128)(2,1)} custom-call(s32[1]{0:T(128)} %bitcast.half_ref, bf16[2,2048,128]{2,1,0:T(8,128)(2,1)} %own_columns.1.own_ref, bf16[2,2048,128]{2,1,0:T(8,128)(2,1)} %copy-done.3, bf16[4096,128]{1,0:T(8,128)(2,1)} %w_in_ref.3, bf16[4096,128]{1,0:T(8,128)(2,1)} %get-tuple-element.31.w_out_t.w_out_ref), custom_call_target="tpu_custom_call" | custom-call | flops 8589934592 | bytes 5242880 | tf_op jit(solution)/shard_map/half_grads/pallas_call | solution.py:443
  105.6 0.0 all-to-all-done.2
  105.6 0.0 copy-start
  105.6 7.6 %all-to-all-start.3 = ((bf16[32,2,64,128]{3,2,1,0:T(8,128)(2,1)}), bf16[32,2,64,128]{3,2,1,0:T(8,128)(2,1)S(1)}, u32[]{:S(2)}, u32[]{:S(2)}) async-start(bf16[32,2,64,128]{3,2,1,0:T(8,128)(2,1)} %half_grads.1), calls=%async_computation.3 | async-start | bytes 2097152 | tf_op jit(solution)/shard_map/all_to_all | solution.py:549
  113.2 0.0 copy-done
  113.2 5.2 %spread_trajectory.1 = f32[8,256,128]{2,1,0:T(8,128)} custom-call(bf16[8,8,2,16,128]{4,3,2,1,0:T(8,128)(2,1)} %bitcast.15), custom_call_target="tpu_custom_call" | custom-call | tf_op jit(solution)/shard_map/spread_trajectory/pallas_call | solution.py:356
  118.4 11.7 %all-to-all-done.3.in_ref = bf16[32,2,64,128]{3,2,1,0:T(8,128)(2,1)S(1)} async-done(((bf16[32,2,64,128]{3,2,1,0:T(8,128)(2,1)}), bf16[32,2,64,128]{3,2,1,0:T(8,128)(2,1)S(1)}, u32[]{:S(2)}, u32[]{:S(2)}) %all-to-all-start.3) | async-done | bytes 1048608 | tf_op jit(solution)/shard_map/all_to_all | solution.py:549
  130.2 0.1 plane_sum.1.own_ref
  130.3 2.7 %collective-permute-start.5 = (bf16[2,64,128]{2,1,0:T(8,128)(2,1)S(1)}, bf16[2,64,128]{2,1,0:T(8,128)(2,1)S(1)}, u32[]{:S(2)}, u32[]{:S(2)}) collective-permute-start(bf16[2,64,128]{2,1,0:T(8,128)(2,1)S(1)} %plane_sum.1.own_ref), channel_id=1, source_target_pairs={{0,34},{2,32},{32,2},{34,0},{1,35},{3,33},{33,3},{35,1},{4,38},{6,... | collective-permute-start | bytes 98312 | tf_op jit(solution)/shard_map/ppermute | solution.py:588
  133.0 2.7 %collective-permute-start.4 = (bf16[2,64,128]{2,1,0:T(8,128)(2,1)S(1)}, bf16[2,64,128]{2,1,0:T(8,128)(2,1)S(1)}, u32[]{:S(2)}, u32[]{:S(2)}) collective-permute-start(bf16[2,64,128]{2,1,0:T(8,128)(2,1)S(1)} %plane_sum.1.own_ref), channel_id=1, source_target_pairs={{0,32},{2,34},{32,0},{34,2},{1,33},{3,35},{33,1},{35,3},{4,36},{6,... | collective-permute-start | bytes 98312 | tf_op jit(solution)/shard_map/ppermute | solution.py:588
  135.7 0.4 collective-permute-start.3
  136.1 0.0 collective-permute-done.5.both_ref
  136.1 3.6 %collective-permute-done.4.far_ref = bf16[2,64,128]{2,1,0:T(8,128)(2,1)S(1)} collective-permute-done((bf16[2,64,128]{2,1,0:T(8,128)(2,1)S(1)}, bf16[2,64,128]{2,1,0:T(8,128)(2,1)S(1)}, u32[]{:S(2)}, u32[]{:S(2)}) %collective-permute-start.4) | collective-permute-done | bytes 32800 | tf_op jit(solution)/shard_map/ppermute | solution.py:588
  139.7 0.7 collective-permute-done.3.near_ref
  140.4 0.2 column_copies.1
  140.6 20.0 %all_to_all.25.code_ref = s16[32,144,128]{2,1,0:T(8,128)(2,1)S(1)} all-to-all(s16[32,144,128]{2,1,0:T(8,128)(2,1)S(1)} %column_copies.1), channel_id=1, replica_groups=mesh['sec'=4,'zh'=2,'cx'=4,'core'=2,'c1'=2,'c0'=2] {'sec','cx','c0'}, dimensions={0} | all-to-all | bytes 2359296 | tf_op jit(solution)/shard_map/all_to_all | solution.py:549
  160.6 3.2 %collective-permute-start.6 = (s16[32,144,128]{2,1,0:T(8,128)(2,1)S(1)}, s16[32,144,128]{2,1,0:T(8,128)(2,1)S(1)}, u32[]{:S(2)}, u32[]{:S(2)}) collective-permute-start(s16[32,144,128]{2,1,0:T(8,128)(2,1)S(1)} %all_to_all.25.code_ref), channel_id=1, source_target_pairs={{0,4},{4,0},{1,5},{5,1},{2,6},{6,2},{3,7},{7,3},{8,12},{12,8},{9,1... | collective-permute-start | bytes 3538952 | tf_op jit(solution)/shard_map/ppermute | solution.py:591
  163.8 1.4 finish_half.2
  165.2 1.0 collective-permute-done.6.code_ref
  166.3 1.4 finish_half.3
  (1 shorter events, 0.0 us)
Async XLA Ops:
  3.4 23.1 %all-to-all-start = ((s16[16,48,128]{2,1,0:T(8,128)(2,1)}), s16[16,48,128]{2,1,0:T(8,128)(2,1)S(1)}, u32[]{:S(2)}, u32[]{:S(2)}) async-start(s16[16,48,128]{2,1,0:T(8,128)(2,1)} %init_slabs.1), calls=%async_computation | async-start | bytes 393216 | tf_op jit(solution)/shard_map/all_to_all | solution.py:549
  26.5 20.4 %copy-start.2 = (s16[16,48,128]{2,1,0:T(8,128)(2,1)}, s16[16,48,128]{2,1,0:T(8,128)(2,1)S(1)}, u32[]{:S(2)}) copy-start(s16[16,48,128]{2,1,0:T(8,128)(2,1)S(1)} %all-to-all-done.msg_ref) | copy-start | bytes 589828
  26.5 4.3 %collective-permute-start = (s16[16,16,128]{2,1,0:T(8,128)(2,1)S(1)}, s16[16,16,128]{2,1,0:T(8,128)(2,1)S(1)}, u32[]{:S(2)}, u32[]{:S(2)}) collective-permute-start(s16[16,16,128]{2,1,0:T(8,128)(2,1)S(1)} %get-tuple-element.25), channel_id=1, source_target_pairs={{0,4},{1,5},{2,6},{3,7},{4,8},{5,9},{6,10},{7,11},{8,12},{9,13},{1... | collective-permute-start | bytes 196616 | tf_op jit(solution)/shard_map/ppermute | solution.py:569
  28.5 5.6 %collective-permute-start.1 = (s16[16,16,128]{2,1,0:T(8,128)(2,1)S(1)}, s16[16,16,128]{2,1,0:T(8,128)(2,1)S(1)}, u32[]{:S(2)}, u32[]{:S(2)}) collective-permute-start(s16[16,16,128]{2,1,0:T(8,128)(2,1)S(1)} %get-tuple-element.26), channel_id=1, source_target_pairs={{4,0},{5,1},{6,2},{7,3},{8,4},{9,5},{10,6},{11,7},{12,8},{13,9},{1... | collective-permute-start | bytes 196616 | tf_op jit(solution)/shard_map/ppermute | solution.py:570
  30.9 16.0 %copy-start.4 = (s16[16,16,128]{2,1,0:T(8,128)(2,1)}, s16[16,16,128]{2,1,0:T(8,128)(2,1)S(1)}, u32[]{:S(2)}) copy-start(s16[16,16,128]{2,1,0:T(8,128)(2,1)S(1)} %collective-permute-done.left_ref) | copy-start | bytes 196612
  34.1 12.8 %copy-start.5 = (s16[16,16,128]{2,1,0:T(8,128)(2,1)}, s16[16,16,128]{2,1,0:T(8,128)(2,1)S(1)}, u32[]{:S(2)}) copy-start(s16[16,16,128]{2,1,0:T(8,128)(2,1)S(1)} %collective-permute-done.1.right_ref) | copy-start | bytes 196612
  34.1 33.2 %all-to-all-start.1 = ((bf16[64,2,16,128]{3,2,1,0:T(8,128)(2,1)}), bf16[64,2,16,128]{3,2,1,0:T(8,128)(2,1)S(1)}, u32[]{:S(2)}, u32[]{:S(2)}) async-start(bf16[64,2,16,128]{3,2,1,0:T(8,128)(2,1)} %bitcast.20), calls=%async_computation.1 | async-start | bytes 1048576 | tf_op jit(solution)/shard_map/all_to_all | solution.py:549
  67.3 0.8 copy-start.1
  70.9 12.9 %collective-permute-start.2 = (bf16[2,2048,128]{2,1,0:T(8,128)(2,1)}, bf16[2,2048,128]{2,1,0:T(8,128)(2,1)S(1)}, u32[]{:S(2)}, u32[]{:S(2)}) collective-permute-start(bf16[2,2048,128]{2,1,0:T(8,128)(2,1)} %own_columns.1.own_ref), channel_id=1, source_target_pairs={{0,4},{4,0},{1,5},{5,1},{2,6},{6,2},{3,7},{7,3},{8,12},{12,8},{9,1... | collective-permute-start | bytes 3145736 | tf_op jit(solution)/shard_map/ppermute | solution.py:580
  71.3 34.3 %all-to-all-start.2 = ((bf16[64,2,16,128]{3,2,1,0:T(8,128)(2,1)}), bf16[64,2,16,128]{3,2,1,0:T(8,128)(2,1)S(1)}, u32[]{:S(2)}, u32[]{:S(2)}) async-start(bf16[64,2,16,128]{3,2,1,0:T(8,128)(2,1)} %bitcast.12), calls=%async_computation.2 | async-start | bytes 1048576 | tf_op jit(solution)/shard_map/all_to_all | solution.py:549
  83.8 1.0 copy-start.3
  105.6 7.6 %copy-start = (bf16[64,2,16,128]{3,2,1,0:T(8,128)(2,1)}, bf16[64,2,16,128]{3,2,1,0:T(8,128)(2,1)S(1)}, u32[]{:S(2)}) copy-start(bf16[64,2,16,128]{3,2,1,0:T(8,128)(2,1)S(1)} %all-to-all-done.2) | copy-start | bytes 1572868
  105.6 24.5 %all-to-all-start.3 = ((bf16[32,2,64,128]{3,2,1,0:T(8,128)(2,1)}), bf16[32,2,64,128]{3,2,1,0:T(8,128)(2,1)S(1)}, u32[]{:S(2)}, u32[]{:S(2)}) async-start(bf16[32,2,64,128]{3,2,1,0:T(8,128)(2,1)} %half_grads.1), calls=%async_computation.3 | async-start | bytes 2097152 | tf_op jit(solution)/shard_map/all_to_all | solution.py:549
  130.3 5.7 %collective-permute-start.5 = (bf16[2,64,128]{2,1,0:T(8,128)(2,1)S(1)}, bf16[2,64,128]{2,1,0:T(8,128)(2,1)S(1)}, u32[]{:S(2)}, u32[]{:S(2)}) collective-permute-start(bf16[2,64,128]{2,1,0:T(8,128)(2,1)S(1)} %plane_sum.1.own_ref), channel_id=1, source_target_pairs={{0,34},{2,32},{32,2},{34,0},{1,35},{3,33},{33,3},{35,1},{4,38},{6,... | collective-permute-start | bytes 98312 | tf_op jit(solution)/shard_map/ppermute | solution.py:588
  133.0 6.7 %collective-permute-start.4 = (bf16[2,64,128]{2,1,0:T(8,128)(2,1)S(1)}, bf16[2,64,128]{2,1,0:T(8,128)(2,1)S(1)}, u32[]{:S(2)}, u32[]{:S(2)}) collective-permute-start(bf16[2,64,128]{2,1,0:T(8,128)(2,1)S(1)} %plane_sum.1.own_ref), channel_id=1, source_target_pairs={{0,32},{2,34},{32,0},{34,2},{1,33},{3,35},{33,1},{35,3},{4,36},{6,... | collective-permute-start | bytes 98312 | tf_op jit(solution)/shard_map/ppermute | solution.py:588
  135.7 4.7 %collective-permute-start.3 = (bf16[2,64,128]{2,1,0:T(8,128)(2,1)S(1)}, bf16[2,64,128]{2,1,0:T(8,128)(2,1)S(1)}, u32[]{:S(2)}, u32[]{:S(2)}) collective-permute-start(bf16[2,64,128]{2,1,0:T(8,128)(2,1)S(1)} %plane_sum.1.own_ref), channel_id=1, source_target_pairs={{0,2},{2,0},{32,34},{34,32},{1,3},{3,1},{33,35},{35,33},{4,6},{6,4... | collective-permute-start | bytes 98312 | tf_op jit(solution)/shard_map/ppermute | solution.py:588
  160.6 5.7 %collective-permute-start.6 = (s16[32,144,128]{2,1,0:T(8,128)(2,1)S(1)}, s16[32,144,128]{2,1,0:T(8,128)(2,1)S(1)}, u32[]{:S(2)}, u32[]{:S(2)}) collective-permute-start(s16[32,144,128]{2,1,0:T(8,128)(2,1)S(1)} %all_to_all.25.code_ref), channel_id=1, source_target_pairs={{0,4},{4,0},{1,5},{5,1},{2,6},{6,2},{3,7},{7,3},{8,12},{12,8},{9,1... | collective-permute-start | bytes 3538952 | tf_op jit(solution)/shard_map/ppermute | solution.py:591

commit v6 on v5

--- a/solution.py
+++ b/solution.py
@@ -32,6 +32,8 @@
 GRAD_SCALE = 1.0 / math.sqrt(MB * STEPS * NX * NY)
 TILE = ("zh", "cx", "core")
 COL = ("c1", "c0")
+SAME_CORE = ("sec", "zh", "cx")
+ACROSS = [(0, 1), (1, 0)]
 SPREAD = ("sec", "cx", "c0")
 PARTS = 32
 ROWS = H // 2 // PARTS
@@ -305,63 +307,83 @@
     )
 
 
-def prepare_kernel(plan_ref, target_ref, w_in_ref, w_out_ref, out_ref, w_in_t, w_out_t, wide):
-    wide[...] = target_ref[0].astype(jnp.float32)
-    for x in range(2):
-        t = wide[pl.ds(x, F, stride=2), :].T
-        out_ref[0, :, x] = t.reshape(8, CHUNK, F).astype(jnp.bfloat16)
+def prepare_kernel(
+    plan_ref, core_ref, own_ref, their_ref, w_in_ref, w_out_ref, out_ref, w_in_t, w_out_t, wide, turned
+):
+    core = core_ref[0]
+    for source, ref in ((core, own_ref), (1 - core, their_ref)):
+        wide[...] = ref[0].astype(jnp.float32)
+        for x in range(2):
+            turned[x] = wide[pl.ds(x, F, stride=2), :].T
+            for cx in range(4):
+                at = pl.multiple_of((2 * cx + core) * CHUNK, CHUNK)
+                out_ref[0, cx, source, x] = turned[x, pl.ds(at, CHUNK)].astype(jnp.bfloat16)
     w_in_t[...] = w_in_ref[...].T
     w_out_t[...] = w_out_ref[...].T
 
 
-def prepare(targets, w_in, w_out, plan):
+def prepare(targets, theirs, w_in, w_out, plan, core):
     part = H // MB
-    down = lambda i, plan: (i, 0)
-    along = lambda i, plan: (0, i)
+    down = lambda i, plan, core: (i, 0)
+    along = lambda i, plan, core: (0, i)
+    sample = pl.BlockSpec((1, 2 * F, 128), lambda i, plan, core: (plan[i], 0, 0))
     return pl.pallas_call(
         prepare_kernel,
         grid_spec=pltpu.PrefetchScalarGridSpec(
-            num_scalar_prefetch=1,
+            num_scalar_prefetch=2,
             grid=(MB,),
             in_specs=[
-                pl.BlockSpec((1, 2 * F, 128), lambda i, plan: (plan[i], 0, 0)),
+                sample,
+                sample,
                 pl.BlockSpec((part, F), down),
                 pl.BlockSpec((F, part), along),
             ],
             out_specs=[
-                pl.BlockSpec((1, 8, 2, CHUNK, F), lambda i, plan: (i, 0, 0, 0, 0)),
+                pl.BlockSpec((1, 4, 2, 2, CHUNK, F), lambda i, plan, core: (i, 0, 0, 0, 0, 0)),
                 pl.BlockSpec((F, part), along),
                 pl.BlockSpec((part, F), down),
             ],
-            scratch_shapes=[pltpu.VMEM((2 * F, 128), jnp.float32)],
+            scratch_shapes=[
+                pltpu.VMEM((2 * F, 128), jnp.float32),
+                pltpu.VMEM((2, 128, F), jnp.float32),
+            ],
         ),
         out_shape=[
-            jax.ShapeDtypeStruct((MB, 8, 2, CHUNK, F), jnp.bfloat16),
+            jax.ShapeDtypeStruct((MB, 4, 2, 2, CHUNK, F), jnp.bfloat16),
             jax.ShapeDtypeStruct((F, H), jnp.bfloat16),
             jax.ShapeDtypeStruct((H, F), jnp.bfloat16),
         ],
         compiler_params=params(),
         cost_estimate=pl.CostEstimate(flops=0, bytes_accessed=6 * 2**20, transcendentals=0),
         name="prepare",
-    )(plan, targets, w_in, w_out)
-
-
-def spread_kernel(in_ref, out_ref):
+    )(plan, core, targets, theirs, w_in, w_out)
+
+
+def spread_kernel(core_ref, own_ref, their_ref, out_ref):
+    even = core_ref[0] == 0
     for x in range(2):
-        block = in_ref[0, :, x].astype(jnp.float32).reshape(128, F)
-        out_ref[0, pl.ds(x, F, stride=2), :] = block.T
-
-
-def spread_trajectory(arrived):
+        chunks = []
+        for cx in range(4):
+            own = own_ref[0, cx, 0, x].astype(jnp.float32)
+            their = their_ref[0, cx, 0, x].astype(jnp.float32)
+            chunks += [jnp.where(even, own, their), jnp.where(even, their, own)]
+        out_ref[0, pl.ds(x, F, stride=2), :] = jnp.concatenate(chunks, axis=0).T
+
+
+def spread_trajectory(core, own, theirs):
+    block = pl.BlockSpec((1, 4, 1, 2, CHUNK, F), lambda i, core: (i, 0, core[0], 0, 0, 0))
     return pl.pallas_call(
         spread_kernel,
-        grid=(MB,),
-        in_specs=[pl.BlockSpec((1, 8, 2, CHUNK, F), lambda i: (i, 0, 0, 0, 0))],
-        out_specs=pl.BlockSpec((1, 2 * F, 128), lambda i: (i, 0, 0)),
+        grid_spec=pltpu.PrefetchScalarGridSpec(
+            num_scalar_prefetch=1,
+            grid=(MB,),
+            in_specs=[block, block],
+            out_specs=pl.BlockSpec((1, 2 * F, 128), lambda i, core: (i, 0, 0)),
+        ),
         out_shape=jax.ShapeDtypeStruct((MB, 2 * F, 128), jnp.float32),
         compiler_params=params(),
         name="spread_trajectory",
-    )(arrived)
+    )(core, own, theirs)
 
 
 def grad_block(columns, w_in_ref, w_out_t_ref, scratch):
@@ -564,31 +586,34 @@
         for c in range(4)
         if c + (j + 1) // 8 < 4
     ]
-    target, w_in_t, w_out_t = prepare(targets.reshape(MB, 2 * F, 128), w_in, w_out, plan)
+    targets = targets.reshape(MB, 2 * F, 128)
+    their_targets = lax.ppermute(targets, "core", ACROSS)
+    target, w_in_t, w_out_t = prepare(targets, their_targets, w_in, w_out, plan, core)
     last, first, target = lax.optimization_barrier((msg[:, 32:48], msg[:, 0:16], target))
     left = lax.ppermute(last, TILE + COL, forward)
     right = lax.ppermute(first, TILE + COL, [(b, a) for a, b in forward])
     left, right, target = lax.optimization_barrier((left, right, target))
-    target = swap(target.reshape(64, 2, CHUNK, F), ("sec",) + TILE).reshape(COLS, F)
+    target = swap(target.reshape(32, 2, 2, CHUNK, F), SAME_CORE).reshape(COLS, F)
 
     traj, inputs, tend, wet = rollout(chunk, msg, left, right, w_in_t, w_out_t, diffusivity, stiffness)
-    arrived = swap(traj.reshape(64, 2, CHUNK, F), ("sec",) + TILE)
+    arrived = swap(traj.reshape(32, 2, 2, CHUNK, F), SAME_CORE)
 
     own = own_columns(
         inputs.reshape(COLS, F), tend.reshape(COLS, F), target, wet.reshape(OWN, F)
     )
-    theirs = lax.ppermute(own, "core", [(0, 1), (1, 0)])
+    theirs = lax.ppermute(own, "core", ACROSS)
     pair = half_grads(core, own, theirs, w_in, w_out_t)
     pair, arrived = lax.optimization_barrier((pair, arrived))
 
-    trajectory = spread_trajectory(arrived.reshape(MB, 8, 2, CHUNK, F))
+    arrived = arrived.reshape(MB, 4, 2, 2, CHUNK, F)
+    trajectory = spread_trajectory(core, arrived, lax.ppermute(arrived, "core", ACROSS))
     plane = plane_sum(swap(pair, SPREAD))
     plane, trajectory = lax.optimization_barrier((plane, trajectory))
     others = [
         lax.ppermute(plane, ("zh", "c1"), [(i, i ^ n) for i in range(4)]) for n in range(1, 4)
     ]
     code = swap(column_copies(plane, *others), SPREAD)
-    across = lax.ppermute(code, "core", [(0, 1), (1, 0)])
+    across = lax.ppermute(code, "core", ACROSS)
     grad_in, grad_out = finish_half(1 - core, across, finish_half(core, code))
     return (trajectory.reshape(1, MB, F, 2, 128), grad_in, grad_out)
 

time: 169 us -> 175 us (1.036)
  waiting for transfers between devices: 24.1 us -> 27.2 us
    all_to_all x4, waiting for transfers between devices: 15.5 us -> 18.2 us  [swap(): return lax.all_to_all(value, axes, split_axis=0, concat_axis=0, tiled=True)]
    ppermute x2 -> x4, starting transfers between devices: 3.68 us -> 4.84 us  [the longest x1 3.23 us: local(): across = lax.ppermute(code, 'core', ACROSS)]
  transfers between devices with their start and end apart: 11 -> 13, of which waited for: 6 -> 7; matrix products, arithmetic and copies ran while one was open for 0% -> 0% of each run, Pallas kernels for 33% -> 27%
where the time goes in v6:
time: 175 us; the launch traced here: 174 us
  Pallas kernels  62.2 us (36%)
  starting transfers between devices  58.4 us (33%)
  waiting for transfers between devices  27.2 us (16%)
  blocking collectives  21.6 us (12%)
  local copies, waits for them, and re-layouts  3.41 us (2%)
    all_to_all x4, starting transfers between devices, swap(): return lax.all_to_all(value, axes, split_axis=0, concat_axis=0, tiled=True)  43.5 us
    all_to_all x1, blocking collectives, swap(): return lax.all_to_all(value, axes, split_axis=0, concat_axis=0, tiled=True)  21.6 us
    pallas_call x1, Pallas kernels, half_grads(): pl.pallas_call(grad_kernel, grid_spec=pltpu.PrefetchScalarGridSpec(num_sc...  20.9 us
    pallas_call x1, Pallas kernels, rollout(): pl.pallas_call(rollout_kernel, out_shape=[jax.ShapeDtypeStruct((STEPS, NX...  20.4 us
    all_to_all x4, waiting for transfers between devices, swap(): return lax.all_to_all(value, axes, split_axis=0, concat_axis=0, tiled=True)  18.2 us
    pallas_call x1, Pallas kernels, prepare(): pl.pallas_call(prepare_kernel, grid_spec=pltpu.PrefetchScalarGridSpec(num...  7.29 us
    ppermute x3, starting transfers between devices, local(): lax.ppermute(plane, ('zh', 'c1'), [(i, i ^ n) for i in range(4)])  5.74 us
    pallas_call x1, Pallas kernels, spread_trajectory(): pl.pallas_call(spread_kernel, grid_spec=pltpu.PrefetchScalarGridSpec(num_...  4.98 us
  transfers between devices with their start and end apart: 13, of which 7 were waited for; matrix products, arithmetic and copies ran while one was open for 0% of the time, Pallas kernels for 27%

profile of v6, /device:TPU:1, one launch (start us, length us, event | category | flops | bytes accessed | tf_op | source)
XLA Modules:
  0.0 173.7 jit_solution(2177636131519810050)
XLA Ops:
  0.6 2.8 %init_slabs.1 = s16[16,48,128]{2,1,0:T(8,128)(2,1)} custom-call(s32[1]{0:T(128)} %bitcast.2.section_ref, s32[8]{0:T(128)} %plan_ref.3, f32[8,256,128]{2,1,0:T(8,128)} %bitcast.19, s32[2,128]{1,0:T(2,128)} %land_ref.1, s32[2,128]{1,0:T(2,128)} %levels_ref.1), custom_call_target="tpu_custom_call" | custom-call | tf_op jit(solution)/shard_map/init_slabs/pallas_call | solution.py:97
  3.4 12.4 %all-to-all-start = ((s16[16,48,128]{2,1,0:T(8,128)(2,1)}), s16[16,48,128]{2,1,0:T(8,128)(2,1)S(1)}, u32[]{:S(2)}, u32[]{:S(2)}) async-start(s16[16,48,128]{2,1,0:T(8,128)(2,1)} %init_slabs.1), calls=%async_computation | async-start | bytes 393216 | tf_op jit(solution)/shard_map/all_to_all | solution.py:571
  15.8 0.2 collective-permute-start
  16.0 10.5 %all-to-all-done.msg_ref = s16[16,48,128]{2,1,0:T(8,128)(2,1)S(1)} async-done(((s16[16,48,128]{2,1,0:T(8,128)(2,1)}), s16[16,48,128]{2,1,0:T(8,128)(2,1)S(1)}, u32[]{:S(2)}, u32[]{:S(2)}) %all-to-all-start) | async-done | bytes 196640 | tf_op jit(solution)/shard_map/all_to_all | solution.py:571
  26.5 0.0 copy-start.2
  26.5 0.0 collective-permute-done.their_ref
  26.5 0.0 copy-start.4
  26.5 0.8 copy-done.4
  27.3 7.3 %prepare.1 = (bf16[8,4,2,2,16,128]{5,4,3,2,1,0:T(8,128)(2,1)}, bf16[128,4096]{1,0:T(8,128)(2,1)}, bf16[4096,128]{1,0:T(8,128)(2,1)}) custom-call(s32[8]{0:T(128)} %plan_ref.3, s32[1]{0:T(128)} %bitcast.core_ref.half_ref, bf16[8,256,128]{2,1,0:T(8,128)(2,1)} %bitcast.23, bf16[8,256,128]{2,1,0:T(8,128)(2,1)} %copy-done.4, bf16[4096,128]{1,0:T(8,128)(2,1)} %w_in_ref.3, ...), custom_call_target="tpu_custom_call" | custom-call | bytes 6291456 | tf_op jit(solution)/shard_map/prepare/pallas_call | solution.py:330
  34.6 2.0 %collective-permute-start.1 = (s16[16,16,128]{2,1,0:T(8,128)(2,1)S(1)}, s16[16,16,128]{2,1,0:T(8,128)(2,1)S(1)}, u32[]{:S(2)}, u32[]{:S(2)}) collective-permute-start(s16[16,16,128]{2,1,0:T(8,128)(2,1)S(1)} %get-tuple-element.25), channel_id=1, source_target_pairs={{0,4},{1,5},{2,6},{3,7},{4,8},{5,9},{6,10},{7,11},{8,12},{9,13},{1... | collective-permute-start | bytes 196616 | tf_op jit(solution)/shard_map/ppermute | solution.py:593
  36.6 2.3 %collective-permute-start.2 = (s16[16,16,128]{2,1,0:T(8,128)(2,1)S(1)}, s16[16,16,128]{2,1,0:T(8,128)(2,1)S(1)}, u32[]{:S(2)}, u32[]{:S(2)}) collective-permute-start(s16[16,16,128]{2,1,0:T(8,128)(2,1)S(1)} %get-tuple-element.26), channel_id=1, source_target_pairs={{4,0},{5,1},{6,2},{7,3},{8,4},{9,5},{10,6},{11,7},{12,8},{13,9},{1... | collective-permute-start | bytes 196616 | tf_op jit(solution)/shard_map/ppermute | solution.py:594
  39.0 0.0 collective-permute-done.1.left_ref
  39.0 0.0 copy-start.6
  39.0 3.2 %collective-permute-done.2.right_ref = s16[16,16,128]{2,1,0:T(8,128)(2,1)S(1)} collective-permute-done((s16[16,16,128]{2,1,0:T(8,128)(2,1)S(1)}, s16[16,16,128]{2,1,0:T(8,128)(2,1)S(1)}, u32[]{:S(2)}, u32[]{:S(2)}) %collective-permute-start.2) | collective-permute-done | bytes 65568 | tf_op jit(solution)/shard_map/ppermute | solution.py:594
  42.2 0.0 copy-start.7
  42.2 0.0 copy-done.2
  42.2 12.2 %all-to-all-start.1 = ((bf16[32,2,2,16,128]{4,3,2,1,0:T(8,128)(2,1)}), bf16[32,2,2,16,128]{4,3,2,1,0:T(8,128)(2,1)S(1)}, u32[]{:S(2)}, u32[]{:S(2)}) async-start(bf16[32,2,2,16,128]{4,3,2,1,0:T(8,128)(2,1)} %bitcast.21), calls=%async_computation.1 | async-start | bytes 1048576 | tf_op jit(solution)/shard_map/all_to_all | solution.py:571
  54.4 0.0 copy-done.6
  54.4 0.0 copy-done.7
  54.4 20.4 %rollout.1 = (bf16[4,32,16,128]{3,2,1,0:T(8,128)(2,1)}, bf16[4,32,16,128]{3,2,1,0:T(8,128)(2,1)}, f32[4,32,16,128]{3,2,1,0:T(8,128)}, f32[32,16,128]{2,1,0:T(8,128)}) custom-call(s32[1]{0:T(128)} %bitcast.1.chunk_ref, s16[16,48,128]{2,1,0:T(8,128)(2,1)} %copy-done.2, s16[16,16,128]{2,1,0:T(8,128)(2,1)} %copy-done.6, s16[16,16,128]{2,1,0:T(8,128)(2,1)} %copy-done.7, ...), custom_call_target="tpu_custom_call" | custom-call | flops 5905580032 | bytes 6291456 | tf_op jit(solution)/shard_map/rollout/pallas_call | solution.py:267
  74.9 0.0 all-to-all-done.1
  74.9 0.0 copy-start.1
  74.9 0.8 copy-done.1
  75.7 2.7 %own_columns.1.own_ref = bf16[2,2048,128]{2,1,0:T(8,128)(2,1)} custom-call(bf16[2048,128]{1,0:T(8,128)(2,1)} %bitcast.24, f32[2048,128]{1,0:T(8,128)} %bitcast.20, bf16[2048,128]{1,0:T(8,128)(2,1)} %bitcast.17, f32[512,128]{1,0:T(8,128)} %bitcast.25), custom_call_target="tpu_custom_call" | custom-call | tf_op jit(solution)/shard_map/own_columns/pallas_call | solution.py:433
  78.4 0.0 collective-permute-start.3
  78.4 11.8 %all-to-all-start.2 = ((bf16[32,2,2,16,128]{4,3,2,1,0:T(8,128)(2,1)}), bf16[32,2,2,16,128]{4,3,2,1,0:T(8,128)(2,1)S(1)}, u32[]{:S(2)}, u32[]{:S(2)}) async-start(bf16[32,2,2,16,128]{4,3,2,1,0:T(8,128)(2,1)} %bitcast.12), calls=%async_computation.2 | async-start | bytes 1048576 | tf_op jit(solution)/shard_map/all_to_all | solution.py:571
  90.2 0.0 collective-permute-done.3.their_ref
  90.3 0.0 copy-start.5
  90.3 1.0 copy-done.5
  91.2 20.9 %half_grads.1 = bf16[32,2,64,128]{3,2,1,0:T(8,128)(2,1)} custom-call(s32[1]{0:T(128)} %bitcast.core_ref.half_ref, bf16[2,2048,128]{2,1,0:T(8,128)(2,1)} %own_columns.1.own_ref, bf16[2,2048,128]{2,1,0:T(8,128)(2,1)} %copy-done.5, bf16[4096,128]{1,0:T(8,128)(2,1)} %w_in_ref.3, bf16[4096,128]{1,0:T(8,128)(2,1)} %get-tuple-element.31.w_out_t.w_out_ref), custom_call_target="tpu_custom_call" | custom-call | flops 8589934592 | bytes 5242880 | tf_op jit(solution)/shard_map/half_grads/pallas_call | solution.py:465
  112.1 0.0 all-to-all-done.2
  112.1 0.0 copy-start
  112.1 7.1 %all-to-all-start.3 = ((bf16[32,2,64,128]{3,2,1,0:T(8,128)(2,1)}), bf16[32,2,64,128]{3,2,1,0:T(8,128)(2,1)S(1)}, u32[]{:S(2)}, u32[]{:S(2)}) async-start(bf16[32,2,64,128]{3,2,1,0:T(8,128)(2,1)} %half_grads.1), calls=%async_computation.3 | async-start | bytes 2097152 | tf_op jit(solution)/shard_map/all_to_all | solution.py:571
  119.2 1.4 collective-permute-start.4
  120.6 1.5 collective-permute-done.4.their_ref
  122.2 0.0 copy-done
  122.2 0.0 copy-start.3
  122.2 0.8 copy-done.3
  123.0 5.0 %spread_trajectory.1 = f32[8,256,128]{2,1,0:T(8,128)} custom-call(s32[1]{0:T(128)} %bitcast.core_ref.half_ref, bf16[8,4,2,2,16,128]{5,4,3,2,1,0:T(8,128)(2,1)} %bitcast.16, bf16[8,4,2,2,16,128]{5,4,3,2,1,0:T(8,128)(2,1)} %copy-done.3), custom_call_target="tpu_custom_call" | custom-call | tf_op jit(solution)/shard_map/spread_trajectory/pallas_call | solution.py:375
  128.0 7.7 %all-to-all-done.3.in_ref = bf16[32,2,64,128]{3,2,1,0:T(8,128)(2,1)S(1)} async-done(((bf16[32,2,64,128]{3,2,1,0:T(8,128)(2,1)}), bf16[32,2,64,128]{3,2,1,0:T(8,128)(2,1)S(1)}, u32[]{:S(2)}, u32[]{:S(2)}) %all-to-all-start.3) | async-done | bytes 1048608 | tf_op jit(solution)/shard_map/all_to_all | solution.py:571
  135.6 0.1 plane_sum.1.own_ref
  135.8 1.9 %collective-permute-start.7 = (bf16[2,64,128]{2,1,0:T(8,128)(2,1)S(1)}, bf16[2,64,128]{2,1,0:T(8,128)(2,1)S(1)}, u32[]{:S(2)}, u32[]{:S(2)}) collective-permute-start(bf16[2,64,128]{2,1,0:T(8,128)(2,1)S(1)} %plane_sum.1.own_ref), channel_id=1, source_target_pairs={{0,34},{2,32},{32,2},{34,0},{1,35},{3,33},{33,3},{35,1},{4,38},{6,... | collective-permute-start | bytes 98312 | tf_op jit(solution)/shard_map/ppermute | solution.py:613
  137.7 3.4 %collective-permute-start.6 = (bf16[2,64,128]{2,1,0:T(8,128)(2,1)S(1)}, bf16[2,64,128]{2,1,0:T(8,128)(2,1)S(1)}, u32[]{:S(2)}, u32[]{:S(2)}) collective-permute-start(bf16[2,64,128]{2,1,0:T(8,128)(2,1)S(1)} %plane_sum.1.own_ref), channel_id=1, source_target_pairs={{0,32},{2,34},{32,0},{34,2},{1,33},{3,35},{33,1},{35,3},{4,36},{6,... | collective-permute-start | bytes 98312 | tf_op jit(solution)/shard_map/ppermute | solution.py:613
  141.1 0.5 collective-permute-start.5
  141.5 0.0 collective-permute-done.7.both_ref
  141.5 3.0 %collective-permute-done.6.far_ref = bf16[2,64,128]{2,1,0:T(8,128)(2,1)S(1)} collective-permute-done((bf16[2,64,128]{2,1,0:T(8,128)(2,1)S(1)}, bf16[2,64,128]{2,1,0:T(8,128)(2,1)S(1)}, u32[]{:S(2)}, u32[]{:S(2)}) %collective-permute-start.6) | collective-permute-done | bytes 32800 | tf_op jit(solution)/shard_map/ppermute | solution.py:613
  144.6 0.2 collective-permute-done.5.near_ref
  144.7 0.2 column_copies.1
  144.9 21.6 %all_to_all.25.code_ref = s16[32,144,128]{2,1,0:T(8,128)(2,1)S(1)} all-to-all(s16[32,144,128]{2,1,0:T(8,128)(2,1)S(1)} %column_copies.1), channel_id=1, replica_groups=mesh['sec'=4,'zh'=2,'cx'=4,'core'=2,'c1'=2,'c0'=2] {'sec','cx','c0'}, dimensions={0} | all-to-all | bytes 2359296 | tf_op jit(solution)/shard_map/all_to_all | solution.py:571
  166.6 3.2 %collective-permute-start.8 = (s16[32,144,128]{2,1,0:T(8,128)(2,1)S(1)}, s16[32,144,128]{2,1,0:T(8,128)(2,1)S(1)}, u32[]{:S(2)}, u32[]{:S(2)}) collective-permute-start(s16[32,144,128]{2,1,0:T(8,128)(2,1)S(1)} %all_to_all.25.code_ref), channel_id=1, source_target_pairs={{0,4},{4,0},{1,5},{5,1},{2,6},{6,2},{3,7},{7,3},{8,12},{12,8},{9,1... | collective-permute-start | bytes 3538952 | tf_op jit(solution)/shard_map/ppermute | solution.py:616
  169.8 1.4 finish_half.2
  171.2 1.0 collective-permute-done.8.code_ref
  172.3 1.4 finish_half.3
  (1 shorter events, 0.0 us)
Async XLA Ops:
  3.4 23.1 %all-to-all-start = ((s16[16,48,128]{2,1,0:T(8,128)(2,1)}), s16[16,48,128]{2,1,0:T(8,128)(2,1)S(1)}, u32[]{:S(2)}, u32[]{:S(2)}) async-start(s16[16,48,128]{2,1,0:T(8,128)(2,1)} %init_slabs.1), calls=%async_computation | async-start | bytes 393216 | tf_op jit(solution)/shard_map/all_to_all | solution.py:571
  15.8 10.7 %collective-permute-start = (bf16[8,256,128]{2,1,0:T(8,128)(2,1)}, bf16[8,256,128]{2,1,0:T(8,128)(2,1)S(1)}, u32[]{:S(2)}, u32[]{:S(2)}) collective-permute-start(bf16[8,256,128]{2,1,0:T(8,128)(2,1)} %bitcast.22), channel_id=1, source_target_pairs={{0,4},{4,0},{1,5},{5,1},{2,6},{6,2},{3,7},{7,3},{8,12},{12,8},{9,1... | collective-permute-start | bytes 1572872 | tf_op jit(solution)/shard_map/ppermute | solution.py:590
  26.5 15.7 %copy-start.2 = (s16[16,48,128]{2,1,0:T(8,128)(2,1)}, s16[16,48,128]{2,1,0:T(8,128)(2,1)S(1)}, u32[]{:S(2)}) copy-start(s16[16,48,128]{2,1,0:T(8,128)(2,1)S(1)} %all-to-all-done.msg_ref) | copy-start | bytes 589828
  26.5 0.8 copy-start.4
  34.6 4.3 %collective-permute-start.1 = (s16[16,16,128]{2,1,0:T(8,128)(2,1)S(1)}, s16[16,16,128]{2,1,0:T(8,128)(2,1)S(1)}, u32[]{:S(2)}, u32[]{:S(2)}) collective-permute-start(s16[16,16,128]{2,1,0:T(8,128)(2,1)S(1)} %get-tuple-element.25), channel_id=1, source_target_pairs={{0,4},{1,5},{2,6},{3,7},{4,8},{5,9},{6,10},{7,11},{8,12},{9,13},{1... | collective-permute-start | bytes 196616 | tf_op jit(solution)/shard_map/ppermute | solution.py:593
  36.6 5.6 %collective-permute-start.2 = (s16[16,16,128]{2,1,0:T(8,128)(2,1)S(1)}, s16[16,16,128]{2,1,0:T(8,128)(2,1)S(1)}, u32[]{:S(2)}, u32[]{:S(2)}) collective-permute-start(s16[16,16,128]{2,1,0:T(8,128)(2,1)S(1)} %get-tuple-element.26), channel_id=1, source_target_pairs={{4,0},{5,1},{6,2},{7,3},{8,4},{9,5},{10,6},{11,7},{12,8},{13,9},{1... | collective-permute-start | bytes 196616 | tf_op jit(solution)/shard_map/ppermute | solution.py:594
  39.0 15.4 %copy-start.6 = (s16[16,16,128]{2,1,0:T(8,128)(2,1)}, s16[16,16,128]{2,1,0:T(8,128)(2,1)S(1)}, u32[]{:S(2)}) copy-start(s16[16,16,128]{2,1,0:T(8,128)(2,1)S(1)} %collective-permute-done.1.left_ref) | copy-start | bytes 196612
  42.2 12.2 %copy-start.7 = (s16[16,16,128]{2,1,0:T(8,128)(2,1)}, s16[16,16,128]{2,1,0:T(8,128)(2,1)S(1)}, u32[]{:S(2)}) copy-start(s16[16,16,128]{2,1,0:T(8,128)(2,1)S(1)} %collective-permute-done.2.right_ref) | copy-start | bytes 196612
  42.2 32.7 %all-to-all-start.1 = ((bf16[32,2,2,16,128]{4,3,2,1,0:T(8,128)(2,1)}), bf16[32,2,2,16,128]{4,3,2,1,0:T(8,128)(2,1)S(1)}, u32[]{:S(2)}, u32[]{:S(2)}) async-start(bf16[32,2,2,16,128]{4,3,2,1,0:T(8,128)(2,1)} %bitcast.21), calls=%async_computation.1 | async-start | bytes 1048576 | tf_op jit(solution)/shard_map/all_to_all | solution.py:571
  74.9 0.8 copy-start.1
  78.4 11.8 %collective-permute-start.3 = (bf16[2,2048,128]{2,1,0:T(8,128)(2,1)}, bf16[2,2048,128]{2,1,0:T(8,128)(2,1)S(1)}, u32[]{:S(2)}, u32[]{:S(2)}) collective-permute-start(bf16[2,2048,128]{2,1,0:T(8,128)(2,1)} %own_columns.1.own_ref), channel_id=1, source_target_pairs={{0,4},{4,0},{1,5},{5,1},{2,6},{6,2},{3,7},{7,3},{8,12},{12,8},{9,1... | collective-permute-start | bytes 3145736 | tf_op jit(solution)/shard_map/ppermute | solution.py:604
  78.4 33.7 %all-to-all-start.2 = ((bf16[32,2,2,16,128]{4,3,2,1,0:T(8,128)(2,1)}), bf16[32,2,2,16,128]{4,3,2,1,0:T(8,128)(2,1)S(1)}, u32[]{:S(2)}, u32[]{:S(2)}) async-start(bf16[32,2,2,16,128]{4,3,2,1,0:T(8,128)(2,1)} %bitcast.12), calls=%async_computation.2 | async-start | bytes 1048576 | tf_op jit(solution)/shard_map/all_to_all | solution.py:571
  90.3 1.0 copy-start.5
  112.1 10.1 %copy-start = (bf16[32,2,2,16,128]{4,3,2,1,0:T(8,128)(2,1)}, bf16[32,2,2,16,128]{4,3,2,1,0:T(8,128)(2,1)S(1)}, u32[]{:S(2)}) copy-start(bf16[32,2,2,16,128]{4,3,2,1,0:T(8,128)(2,1)S(1)} %all-to-all-done.2) | copy-start | bytes 1572868
  112.1 23.5 %all-to-all-start.3 = ((bf16[32,2,64,128]{3,2,1,0:T(8,128)(2,1)}), bf16[32,2,64,128]{3,2,1,0:T(8,128)(2,1)S(1)}, u32[]{:S(2)}, u32[]{:S(2)}) async-start(bf16[32,2,64,128]{3,2,1,0:T(8,128)(2,1)} %half_grads.1), calls=%async_computation.3 | async-start | bytes 2097152 | tf_op jit(solution)/shard_map/all_to_all | solution.py:571
  119.2 3.0 %collective-permute-start.4 = (bf16[8,4,2,2,16,128]{5,4,3,2,1,0:T(8,128)(2,1)S(1)}, bf16[8,4,2,2,16,128]{5,4,3,2,1,0:T(8,128)(2,1)S(1)}, u32[]{:S(2)}, u32[]{:S(2)}) collective-permute-start(bf16[8,4,2,2,16,128]{5,4,3,2,1,0:T(8,128)(2,1)S(1)} %bitcast.15), channel_id=1, source_target_pairs={{0,4},{4,0},{1,5},{5,1},{2,6},{6,2},{3,7},{7,3},{8,12},{12,8},{9,1... | collective-permute-start | bytes 1572872 | tf_op jit(solution)/shard_map/ppermute | solution.py:609
  122.2 0.8 copy-start.3
  135.8 5.7 %collective-permute-start.7 = (bf16[2,64,128]{2,1,0:T(8,128)(2,1)S(1)}, bf16[2,64,128]{2,1,0:T(8,128)(2,1)S(1)}, u32[]{:S(2)}, u32[]{:S(2)}) collective-permute-start(bf16[2,64,128]{2,1,0:T(8,128)(2,1)S(1)} %plane_sum.1.own_ref), channel_id=1, source_target_pairs={{0,34},{2,32},{32,2},{34,0},{1,35},{3,33},{33,3},{35,1},{4,38},{6,... | collective-permute-start | bytes 98312 | tf_op jit(solution)/shard_map/ppermute | solution.py:613
  137.7 6.9 %collective-permute-start.6 = (bf16[2,64,128]{2,1,0:T(8,128)(2,1)S(1)}, bf16[2,64,128]{2,1,0:T(8,128)(2,1)S(1)}, u32[]{:S(2)}, u32[]{:S(2)}) collective-permute-start(bf16[2,64,128]{2,1,0:T(8,128)(2,1)S(1)} %plane_sum.1.own_ref), channel_id=1, source_target_pairs={{0,32},{2,34},{32,0},{34,2},{1,33},{3,35},{33,1},{35,3},{4,36},{6,... | collective-permute-start | bytes 98312 | tf_op jit(solution)/shard_map/ppermute | solution.py:613
  141.1 3.7 %collective-permute-start.5 = (bf16[2,64,128]{2,1,0:T(8,128)(2,1)S(1)}, bf16[2,64,128]{2,1,0:T(8,128)(2,1)S(1)}, u32[]{:S(2)}, u32[]{:S(2)}) collective-permute-start(bf16[2,64,128]{2,1,0:T(8,128)(2,1)S(1)} %plane_sum.1.own_ref), channel_id=1, source_target_pairs={{0,2},{2,0},{32,34},{34,32},{1,3},{3,1},{33,35},{35,33},{4,6},{6,4... | collective-permute-start | bytes 98312 | tf_op jit(solution)/shard_map/ppermute | solution.py:613
  166.6 5.7 %collective-permute-start.8 = (s16[32,144,128]{2,1,0:T(8,128)(2,1)S(1)}, s16[32,144,128]{2,1,0:T(8,128)(2,1)S(1)}, u32[]{:S(2)}, u32[]{:S(2)}) collective-permute-start(s16[32,144,128]{2,1,0:T(8,128)(2,1)S(1)} %all_to_all.25.code_ref), channel_id=1, source_target_pairs={{0,4},{4,0},{1,5},{5,1},{2,6},{6,2},{3,7},{7,3},{8,12},{12,8},{9,1... | collective-permute-start | bytes 3538952 | tf_op jit(solution)/shard_map/ppermute | solution.py:616

commit v7 on v5

--- a/solution.py
+++ b/solution.py
@@ -413,7 +413,7 @@
         out_shape=jax.ShapeDtypeStruct((2, COLS, F), jnp.bfloat16),
         in_specs=[pl.BlockSpec(memory_space=pltpu.VMEM)] * 4,
         out_specs=pl.BlockSpec(memory_space=pltpu.VMEM),
-        compiler_params=params(),
+        compiler_params=params(mib=24),
         name="own_columns",
     )(inputs, tend, target, wet)
 
@@ -452,7 +452,7 @@
             + [pltpu.VMEM((2, HB2, WIDE), jnp.bfloat16)] * 2,
         ),
         out_shape=jax.ShapeDtypeStruct((PARTS, 2, ROWS, F), jnp.bfloat16),
-        compiler_params=params(("arbitrary",)),
+        compiler_params=params(("arbitrary",), 40),
         cost_estimate=pl.CostEstimate(
             flops=16 * COLS * F * HALF, bytes_accessed=5 * 2**20, transcendentals=2 * COLS * HALF
         ),

time: 169 us -> 169 us (level)
  Pallas kernels: 62.1 us -> 58.2 us
  local copies, waits for them, and re-layouts: 1.79 us -> 5.42 us
    unnamed x12 -> x20, local copies, waits for them, and re-layouts: 1.78 us -> 5.41 us
    pallas_call x1, Pallas kernels: 2.71 us -> 0.16 us  [own_columns(): pl.pallas_call(columns_kernel, out_shape=jax.ShapeDtypeStruct((2, COLS, F...]
  transfers between devices with their start and end apart: 11 -> 11, of which waited for: 6 -> 6; matrix products, arithmetic and copies ran while one was open for 0% -> 0% of each run, Pallas kernels for 33% -> 32%
where the time goes in v7:
time: 169 us; the launch traced here: 168 us
  starting transfers between devices  59 us (35%)
  Pallas kernels  58.2 us (34%)
  waiting for transfers between devices  24.1 us (14%)
  blocking collectives  20 us (12%)
  local copies, waits for them, and re-layouts  5.42 us (3%)
    all_to_all x4, starting transfers between devices, swap(): return lax.all_to_all(value, axes, split_axis=0, concat_axis=0, tiled=True)  45.2 us
    pallas_call x1, Pallas kernels, rollout(): pl.pallas_call(rollout_kernel, out_shape=[jax.ShapeDtypeStruct((STEPS, NX...  20.4 us
    all_to_all x1, blocking collectives, swap(): return lax.all_to_all(value, axes, split_axis=0, concat_axis=0, tiled=True)  20 us
    pallas_call x1, Pallas kernels, half_grads(): pl.pallas_call(grad_kernel, grid_spec=pltpu.PrefetchScalarGridSpec(num_sc...  19.5 us
    all_to_all x4, waiting for transfers between devices, swap(): return lax.all_to_all(value, axes, split_axis=0, concat_axis=0, tiled=True)  15.5 us
    pallas_call x1, Pallas kernels, prepare(): pl.pallas_call(prepare_kernel, grid_spec=pltpu.PrefetchScalarGridSpec(num...  6.89 us
    ppermute x3, starting transfers between devices, local(): lax.ppermute(plane, ('zh', 'c1'), [(i, i ^ n) for i in range(4)])  5.74 us
    unnamed x20, local copies, waits for them, and re-layouts  5.41 us
  transfers between devices with their start and end apart: 11, of which 6 were waited for; matrix products, arithmetic and copies ran while one was open for 0% of the time, Pallas kernels for 32%

profile of v7, /device:TPU:1, one launch (start us, length us, event | category | flops | bytes accessed | tf_op | source)
XLA Modules:
  0.0 167.6 jit_solution(9282850212314602972)
XLA Ops:
  0.6 2.8 %init_slabs.1 = s16[16,48,128]{2,1,0:T(8,128)(2,1)} custom-call(s32[1]{0:T(128)} %bitcast.2.section_ref, s32[8]{0:T(128)} %plan_ref.3, f32[8,256,128]{2,1,0:T(8,128)} %bitcast.21, s32[2,128]{1,0:T(2,128)} %land_ref.1, s32[2,128]{1,0:T(2,128)} %levels_ref.1), custom_call_target="tpu_custom_call" | custom-call | tf_op jit(solution)/shard_map/init_slabs/pallas_call | solution.py:95
  3.4 12.4 %all-to-all-start = ((s16[16,48,128]{2,1,0:T(8,128)(2,1)}), s16[16,48,128]{2,1,0:T(8,128)(2,1)S(1)}, u32[]{:S(2)}, u32[]{:S(2)}) async-start(s16[16,48,128]{2,1,0:T(8,128)(2,1)} %init_slabs.1), calls=%async_computation | async-start | bytes 393216 | tf_op jit(solution)/shard_map/all_to_all | solution.py:549
  15.8 6.9 %prepare.1 = (bf16[8,8,2,16,128]{4,3,2,1,0:T(8,128)(2,1)}, bf16[128,4096]{1,0:T(8,128)(2,1)}, bf16[4096,128]{1,0:T(8,128)(2,1)}) custom-call(s32[8]{0:T(128)} %plan_ref.3, bf16[8,256,128]{2,1,0:T(8,128)(2,1)} %bitcast.23, bf16[4096,128]{1,0:T(8,128)(2,1)} %w_in_ref.3, bf16[128,4096]{1,0:T(8,128)(2,1)} %w_out_ref.1), custom_call_target="tpu_custom_call" | custom-call | bytes 6291456 | tf_op jit(solution)/shard_map/prepare/pallas_call | solution.py:321
  22.7 3.8 %all-to-all-done.msg_ref = s16[16,48,128]{2,1,0:T(8,128)(2,1)S(1)} async-done(((s16[16,48,128]{2,1,0:T(8,128)(2,1)}), s16[16,48,128]{2,1,0:T(8,128)(2,1)S(1)}, u32[]{:S(2)}, u32[]{:S(2)}) %all-to-all-start) | async-done | bytes 196640 | tf_op jit(solution)/shard_map/all_to_all | solution.py:549
  26.5 0.0 copy-start.7
  26.5 2.0 %collective-permute-start = (s16[16,16,128]{2,1,0:T(8,128)(2,1)S(1)}, s16[16,16,128]{2,1,0:T(8,128)(2,1)S(1)}, u32[]{:S(2)}, u32[]{:S(2)}) collective-permute-start(s16[16,16,128]{2,1,0:T(8,128)(2,1)S(1)} %get-tuple-element.25), channel_id=1, source_target_pairs={{0,4},{1,5},{2,6},{3,7},{4,8},{5,9},{6,10},{7,11},{8,12},{9,13},{1... | collective-permute-start | bytes 196616 | tf_op jit(solution)/shard_map/ppermute | solution.py:569
  28.5 2.3 %collective-permute-start.1 = (s16[16,16,128]{2,1,0:T(8,128)(2,1)S(1)}, s16[16,16,128]{2,1,0:T(8,128)(2,1)S(1)}, u32[]{:S(2)}, u32[]{:S(2)}) collective-permute-start(s16[16,16,128]{2,1,0:T(8,128)(2,1)S(1)} %get-tuple-element.26), channel_id=1, source_target_pairs={{4,0},{5,1},{6,2},{7,3},{8,4},{9,5},{10,6},{11,7},{12,8},{13,9},{1... | collective-permute-start | bytes 196616 | tf_op jit(solution)/shard_map/ppermute | solution.py:570
  30.8 0.0 collective-permute-done.left_ref
  30.9 0.0 copy-start.8
  30.9 3.2 %collective-permute-done.1.right_ref = s16[16,16,128]{2,1,0:T(8,128)(2,1)S(1)} collective-permute-done((s16[16,16,128]{2,1,0:T(8,128)(2,1)S(1)}, s16[16,16,128]{2,1,0:T(8,128)(2,1)S(1)}, u32[]{:S(2)}, u32[]{:S(2)}) %collective-permute-start.1) | collective-permute-done | bytes 65568 | tf_op jit(solution)/shard_map/ppermute | solution.py:570
  34.1 0.0 copy-start.9
  34.1 12.7 %all-to-all-start.1 = ((bf16[64,2,16,128]{3,2,1,0:T(8,128)(2,1)}), bf16[64,2,16,128]{3,2,1,0:T(8,128)(2,1)S(1)}, u32[]{:S(2)}, u32[]{:S(2)}) async-start(bf16[64,2,16,128]{3,2,1,0:T(8,128)(2,1)} %bitcast.22), calls=%async_computation.1 | async-start | bytes 1048576 | tf_op jit(solution)/shard_map/all_to_all | solution.py:549
  46.9 0.0 copy-done.7
  46.9 0.0 copy-done.8
  46.9 0.0 copy-done.9
  46.9 20.4 %rollout.1 = (bf16[4,32,16,128]{3,2,1,0:T(8,128)(2,1)}, bf16[4,32,16,128]{3,2,1,0:T(8,128)(2,1)}, f32[4,32,16,128]{3,2,1,0:T(8,128)}, f32[32,16,128]{2,1,0:T(8,128)}) custom-call(s32[1]{0:T(128)} %bitcast.1.chunk_ref, s16[16,48,128]{2,1,0:T(8,128)(2,1)} %copy-done.7, s16[16,16,128]{2,1,0:T(8,128)(2,1)} %copy-done.8, s16[16,16,128]{2,1,0:T(8,128)(2,1)} %copy-done.9, ...), custom_call_target="tpu_custom_call" | custom-call | flops 5905580032 | bytes 6291456 | tf_op jit(solution)/shard_map/rollout/pallas_call | solution.py:265
  67.3 0.0 all-to-all-done.1
  67.3 0.0 copy-start.1
  67.3 1.2 copy-done.1
  68.6 0.0 copy-start.3
  68.6 1.0 copy-done.3
  69.6 0.0 copy-start.4
  69.6 0.9 copy-done.4
  70.6 0.0 copy-start
  70.6 0.2 own_columns.1.own_ref
  70.7 0.5 collective-permute-start.2
  71.3 12.5 %all-to-all-start.2 = ((bf16[64,2,16,128]{3,2,1,0:T(8,128)(2,1)}), bf16[64,2,16,128]{3,2,1,0:T(8,128)(2,1)S(1)}, u32[]{:S(2)}, u32[]{:S(2)}) async-start(bf16[64,2,16,128]{3,2,1,0:T(8,128)(2,1)} %bitcast.12), calls=%async_computation.2 | async-start | bytes 1048576 | tf_op jit(solution)/shard_map/all_to_all | solution.py:549
  83.7 0.0 collective-permute-done.2.their_ref
  83.7 0.0 copy-done
  83.8 0.0 copy-start.5
  83.8 1.2 copy-done.5
  85.0 19.5 %half_grads.1 = bf16[32,2,64,128]{3,2,1,0:T(8,128)(2,1)S(1)} custom-call(s32[1]{0:T(128)} %bitcast.half_ref, bf16[2,2048,128]{2,1,0:T(8,128)(2,1)S(1)} %own_columns.1.own_ref, bf16[2,2048,128]{2,1,0:T(8,128)(2,1)} %collective-permute-done.2.their_ref, bf16[4096,128]{1,0:T(8,128)(2,1)S(1)} %copy-done, bf16[4096,128]{1,0:T(8,128)(2,1)S(1)} %copy-done.5), custom_call_target="tpu_custom_call" | custom-call | flops 8589934592 | bytes 5242880 | tf_op jit(solution)/shard_map/half_grads/pallas_call | solution.py:443
  104.5 0.0 copy-start.2
  104.6 1.0 copy-done.2
  105.5 0.0 all-to-all-done.2
  105.5 0.0 copy-start.6
  105.5 7.5 %all-to-all-start.3 = ((bf16[32,2,64,128]{3,2,1,0:T(8,128)(2,1)}), bf16[32,2,64,128]{3,2,1,0:T(8,128)(2,1)S(1)}, u32[]{:S(2)}, u32[]{:S(2)}) async-start(bf16[32,2,64,128]{3,2,1,0:T(8,128)(2,1)} %copy-done.2), calls=%async_computation.3 | async-start | bytes 2097152 | tf_op jit(solution)/shard_map/all_to_all | solution.py:549
  113.1 0.0 copy-done.6
  113.1 5.2 %spread_trajectory.1 = f32[8,256,128]{2,1,0:T(8,128)} custom-call(bf16[8,8,2,16,128]{4,3,2,1,0:T(8,128)(2,1)} %bitcast.19), custom_call_target="tpu_custom_call" | custom-call | tf_op jit(solution)/shard_map/spread_trajectory/pallas_call | solution.py:356
  118.3 11.7 %all-to-all-done.3.in_ref = bf16[32,2,64,128]{3,2,1,0:T(8,128)(2,1)S(1)} async-done(((bf16[32,2,64,128]{3,2,1,0:T(8,128)(2,1)}), bf16[32,2,64,128]{3,2,1,0:T(8,128)(2,1)S(1)}, u32[]{:S(2)}, u32[]{:S(2)}) %all-to-all-start.3) | async-done | bytes 1048608 | tf_op jit(solution)/shard_map/all_to_all | solution.py:549
  130.1 0.1 plane_sum.1.own_ref
  130.2 2.7 %collective-permute-start.5 = (bf16[2,64,128]{2,1,0:T(8,128)(2,1)S(1)}, bf16[2,64,128]{2,1,0:T(8,128)(2,1)S(1)}, u32[]{:S(2)}, u32[]{:S(2)}) collective-permute-start(bf16[2,64,128]{2,1,0:T(8,128)(2,1)S(1)} %plane_sum.1.own_ref), channel_id=1, source_target_pairs={{0,34},{2,32},{32,2},{34,0},{1,35},{3,33},{33,3},{35,1},{4,38},{6,... | collective-permute-start | bytes 98312 | tf_op jit(solution)/shard_map/ppermute | solution.py:588
  132.9 2.7 %collective-permute-start.4 = (bf16[2,64,128]{2,1,0:T(8,128)(2,1)S(1)}, bf16[2,64,128]{2,1,0:T(8,128)(2,1)S(1)}, u32[]{:S(2)}, u32[]{:S(2)}) collective-permute-start(bf16[2,64,128]{2,1,0:T(8,128)(2,1)S(1)} %plane_sum.1.own_ref), channel_id=1, source_target_pairs={{0,32},{2,34},{32,0},{34,2},{1,33},{3,35},{33,1},{35,3},{4,36},{6,... | collective-permute-start | bytes 98312 | tf_op jit(solution)/shard_map/ppermute | solution.py:588
  135.5 0.4 collective-permute-start.3
  136.0 0.0 collective-permute-done.5.both_ref
  136.0 3.6 %collective-permute-done.4.far_ref = bf16[2,64,128]{2,1,0:T(8,128)(2,1)S(1)} collective-permute-done((bf16[2,64,128]{2,1,0:T(8,128)(2,1)S(1)}, bf16[2,64,128]{2,1,0:T(8,128)(2,1)S(1)}, u32[]{:S(2)}, u32[]{:S(2)}) %collective-permute-start.4) | collective-permute-done | bytes 32800 | tf_op jit(solution)/shard_map/ppermute | solution.py:588
  139.6 0.7 collective-permute-done.3.near_ref
  140.3 0.2 column_copies.1
  140.5 20.0 %all_to_all.25.code_ref = s16[32,144,128]{2,1,0:T(8,128)(2,1)S(1)} all-to-all(s16[32,144,128]{2,1,0:T(8,128)(2,1)S(1)} %column_copies.1), channel_id=1, replica_groups=mesh['sec'=4,'zh'=2,'cx'=4,'core'=2,'c1'=2,'c0'=2] {'sec','cx','c0'}, dimensions={0} | all-to-all | bytes 2359296 | tf_op jit(solution)/shard_map/all_to_all | solution.py:549
  160.4 3.2 %collective-permute-start.6 = (s16[32,144,128]{2,1,0:T(8,128)(2,1)S(1)}, s16[32,144,128]{2,1,0:T(8,128)(2,1)S(1)}, u32[]{:S(2)}, u32[]{:S(2)}) collective-permute-start(s16[32,144,128]{2,1,0:T(8,128)(2,1)S(1)} %all_to_all.25.code_ref), channel_id=1, source_target_pairs={{0,4},{4,0},{1,5},{5,1},{2,6},{6,2},{3,7},{7,3},{8,12},{12,8},{9,1... | collective-permute-start | bytes 3538952 | tf_op jit(solution)/shard_map/ppermute | solution.py:591
  163.7 1.4 finish_half.2
  165.1 1.0 collective-permute-done.6.code_ref
  166.2 1.4 finish_half.3
  (1 shorter events, 0.0 us)
Async XLA Ops:
  3.4 23.1 %all-to-all-start = ((s16[16,48,128]{2,1,0:T(8,128)(2,1)}), s16[16,48,128]{2,1,0:T(8,128)(2,1)S(1)}, u32[]{:S(2)}, u32[]{:S(2)}) async-start(s16[16,48,128]{2,1,0:T(8,128)(2,1)} %init_slabs.1), calls=%async_computation | async-start | bytes 393216 | tf_op jit(solution)/shard_map/all_to_all | solution.py:549
  26.5 20.4 %copy-start.7 = (s16[16,48,128]{2,1,0:T(8,128)(2,1)}, s16[16,48,128]{2,1,0:T(8,128)(2,1)S(1)}, u32[]{:S(2)}) copy-start(s16[16,48,128]{2,1,0:T(8,128)(2,1)S(1)} %all-to-all-done.msg_ref) | copy-start | bytes 589828
  26.5 4.3 %collective-permute-start = (s16[16,16,128]{2,1,0:T(8,128)(2,1)S(1)}, s16[16,16,128]{2,1,0:T(8,128)(2,1)S(1)}, u32[]{:S(2)}, u32[]{:S(2)}) collective-permute-start(s16[16,16,128]{2,1,0:T(8,128)(2,1)S(1)} %get-tuple-element.25), channel_id=1, source_target_pairs={{0,4},{1,5},{2,6},{3,7},{4,8},{5,9},{6,10},{7,11},{8,12},{9,13},{1... | collective-permute-start | bytes 196616 | tf_op jit(solution)/shard_map/ppermute | solution.py:569
  28.5 5.6 %collective-permute-start.1 = (s16[16,16,128]{2,1,0:T(8,128)(2,1)S(1)}, s16[16,16,128]{2,1,0:T(8,128)(2,1)S(1)}, u32[]{:S(2)}, u32[]{:S(2)}) collective-permute-start(s16[16,16,128]{2,1,0:T(8,128)(2,1)S(1)} %get-tuple-element.26), channel_id=1, source_target_pairs={{4,0},{5,1},{6,2},{7,3},{8,4},{9,5},{10,6},{11,7},{12,8},{13,9},{1... | collective-permute-start | bytes 196616 | tf_op jit(solution)/shard_map/ppermute | solution.py:570
  30.9 16.0 %copy-start.8 = (s16[16,16,128]{2,1,0:T(8,128)(2,1)}, s16[16,16,128]{2,1,0:T(8,128)(2,1)S(1)}, u32[]{:S(2)}) copy-start(s16[16,16,128]{2,1,0:T(8,128)(2,1)S(1)} %collective-permute-done.left_ref) | copy-start | bytes 196612
  34.1 12.8 %copy-start.9 = (s16[16,16,128]{2,1,0:T(8,128)(2,1)}, s16[16,16,128]{2,1,0:T(8,128)(2,1)S(1)}, u32[]{:S(2)}) copy-start(s16[16,16,128]{2,1,0:T(8,128)(2,1)S(1)} %collective-permute-done.1.right_ref) | copy-start | bytes 196612
  34.1 33.2 %all-to-all-start.1 = ((bf16[64,2,16,128]{3,2,1,0:T(8,128)(2,1)}), bf16[64,2,16,128]{3,2,1,0:T(8,128)(2,1)S(1)}, u32[]{:S(2)}, u32[]{:S(2)}) async-start(bf16[64,2,16,128]{3,2,1,0:T(8,128)(2,1)} %bitcast.22), calls=%async_computation.1 | async-start | bytes 1048576 | tf_op jit(solution)/shard_map/all_to_all | solution.py:549
  67.3 1.2 copy-start.1
  68.6 1.0 copy-start.3
  69.6 0.9 copy-start.4
  70.6 13.2 %copy-start = (bf16[4096,128]{1,0:T(8,128)(2,1)S(1)}, bf16[4096,128]{1,0:T(8,128)(2,1)}, u32[]{:S(2)}) copy-start(bf16[4096,128]{1,0:T(8,128)(2,1)} %w_in_ref.3) | copy-start | bytes 3145732
  70.7 13.0 %collective-permute-start.2 = (bf16[2,2048,128]{2,1,0:T(8,128)(2,1)S(1)}, bf16[2,2048,128]{2,1,0:T(8,128)(2,1)}, u32[]{:S(2)}, u32[]{:S(2)}) collective-permute-start(bf16[2,2048,128]{2,1,0:T(8,128)(2,1)S(1)} %own_columns.1.own_ref), channel_id=1, source_target_pairs={{0,4},{4,0},{1,5},{5,1},{2,6},{6,2},{3,7},{7,3},{8,12},{12,8},{9,1... | collective-permute-start | bytes 3145736 | tf_op jit(solution)/shard_map/ppermute | solution.py:580
  71.3 34.3 %all-to-all-start.2 = ((bf16[64,2,16,128]{3,2,1,0:T(8,128)(2,1)}), bf16[64,2,16,128]{3,2,1,0:T(8,128)(2,1)S(1)}, u32[]{:S(2)}, u32[]{:S(2)}) async-start(bf16[64,2,16,128]{3,2,1,0:T(8,128)(2,1)} %bitcast.12), calls=%async_computation.2 | async-start | bytes 1048576 | tf_op jit(solution)/shard_map/all_to_all | solution.py:549
  83.8 1.2 copy-start.5
  104.5 1.0 copy-start.2
  105.5 7.6 %copy-start.6 = (bf16[64,2,16,128]{3,2,1,0:T(8,128)(2,1)}, bf16[64,2,16,128]{3,2,1,0:T(8,128)(2,1)S(1)}, u32[]{:S(2)}) copy-start(bf16[64,2,16,128]{3,2,1,0:T(8,128)(2,1)S(1)} %all-to-all-done.2) | copy-start | bytes 1572868
  105.5 24.5 %all-to-all-start.3 = ((bf16[32,2,64,128]{3,2,1,0:T(8,128)(2,1)}), bf16[32,2,64,128]{3,2,1,0:T(8,128)(2,1)S(1)}, u32[]{:S(2)}, u32[]{:S(2)}) async-start(bf16[32,2,64,128]{3,2,1,0:T(8,128)(2,1)} %copy-done.2), calls=%async_computation.3 | async-start | bytes 2097152 | tf_op jit(solution)/shard_map/all_to_all | solution.py:549
  130.2 5.7 %collective-permute-start.5 = (bf16[2,64,128]{2,1,0:T(8,128)(2,1)S(1)}, bf16[2,64,128]{2,1,0:T(8,128)(2,1)S(1)}, u32[]{:S(2)}, u32[]{:S(2)}) collective-permute-start(bf16[2,64,128]{2,1,0:T(8,128)(2,1)S(1)} %plane_sum.1.own_ref), channel_id=1, source_target_pairs={{0,34},{2,32},{32,2},{34,0},{1,35},{3,33},{33,3},{35,1},{4,38},{6,... | collective-permute-start | bytes 98312 | tf_op jit(solution)/shard_map/ppermute | solution.py:588
  132.9 6.7 %collective-permute-start.4 = (bf16[2,64,128]{2,1,0:T(8,128)(2,1)S(1)}, bf16[2,64,128]{2,1,0:T(8,128)(2,1)S(1)}, u32[]{:S(2)}, u32[]{:S(2)}) collective-permute-start(bf16[2,64,128]{2,1,0:T(8,128)(2,1)S(1)} %plane_sum.1.own_ref), channel_id=1, source_target_pairs={{0,32},{2,34},{32,0},{34,2},{1,33},{3,35},{33,1},{35,3},{4,36},{6,... | collective-permute-start | bytes 98312 | tf_op jit(solution)/shard_map/ppermute | solution.py:588
  135.5 4.7 %collective-permute-start.3 = (bf16[2,64,128]{2,1,0:T(8,128)(2,1)S(1)}, bf16[2,64,128]{2,1,0:T(8,128)(2,1)S(1)}, u32[]{:S(2)}, u32[]{:S(2)}) collective-permute-start(bf16[2,64,128]{2,1,0:T(8,128)(2,1)S(1)} %plane_sum.1.own_ref), channel_id=1, source_target_pairs={{0,2},{2,0},{32,34},{34,32},{1,3},{3,1},{33,35},{35,33},{4,6},{6,4... | collective-permute-start | bytes 98312 | tf_op jit(solution)/shard_map/ppermute | solution.py:588
  160.4 5.7 %collective-permute-start.6 = (s16[32,144,128]{2,1,0:T(8,128)(2,1)S(1)}, s16[32,144,128]{2,1,0:T(8,128)(2,1)S(1)}, u32[]{:S(2)}, u32[]{:S(2)}) collective-permute-start(s16[32,144,128]{2,1,0:T(8,128)(2,1)S(1)} %all_to_all.25.code_ref), channel_id=1, source_target_pairs={{0,4},{4,0},{1,5},{5,1},{2,6},{6,2},{3,7},{7,3},{8,12},{12,8},{9,1... | collective-permute-start | bytes 3538952 | tf_op jit(solution)/shard_map/ppermute | solution.py:591

commit v8 on v5

--- a/solution.py
+++ b/solution.py
@@ -25,7 +25,7 @@
 OWN = NX * CHUNK
 COLS = STEPS * OWN
 HB1 = 2048
-HB2 = 1024
+HB2 = 2048
 WIDE = 512
 STRIP = 32
 HALF = H // 2

time: 169 us -> 169 us (level)
  no operation moved by 1% of the time
where the time goes in v8:
time: 169 us; the launch traced here: 168 us
  Pallas kernels  62 us (37%)
  starting transfers between devices  59.1 us (35%)
  waiting for transfers between devices  24.1 us (14%)
  blocking collectives  20 us (12%)
  local copies, waits for them, and re-layouts  1.79 us (1%)
    all_to_all x4, starting transfers between devices, swap(): return lax.all_to_all(value, axes, split_axis=0, concat_axis=0, tiled=True)  45.4 us
    pallas_call x1, Pallas kernels, half_grads(): pl.pallas_call(grad_kernel, grid_spec=pltpu.PrefetchScalarGridSpec(num_sc...  20.8 us
    pallas_call x1, Pallas kernels, rollout(): pl.pallas_call(rollout_kernel, out_shape=[jax.ShapeDtypeStruct((STEPS, NX...  20.4 us
    all_to_all x1, blocking collectives, swap(): return lax.all_to_all(value, axes, split_axis=0, concat_axis=0, tiled=True)  20 us
    all_to_all x4, waiting for transfers between devices, swap(): return lax.all_to_all(value, axes, split_axis=0, concat_axis=0, tiled=True)  15.5 us
    pallas_call x1, Pallas kernels, prepare(): pl.pallas_call(prepare_kernel, grid_spec=pltpu.PrefetchScalarGridSpec(num...  6.89 us
    ppermute x3, starting transfers between devices, local(): lax.ppermute(plane, ('zh', 'c1'), [(i, i ^ n) for i in range(4)])  5.74 us
    pallas_call x1, Pallas kernels, spread_trajectory(): pl.pallas_call(spread_kernel, grid=(MB,), in_specs=[pl.BlockSpec((1, 8, 2...  5.24 us
  transfers between devices with their start and end apart: 11, of which 6 were waited for; matrix products, arithmetic and copies ran while one was open for 0% of the time, Pallas kernels for 33%

profile of v8, /device:TPU:1, one launch (start us, length us, event | category | flops | bytes accessed | tf_op | source)
XLA Modules:
  0.0 167.8 jit_solution(9490496184390114050)
XLA Ops:
  0.6 2.8 %init_slabs.1 = s16[16,48,128]{2,1,0:T(8,128)(2,1)} custom-call(s32[1]{0:T(128)} %bitcast.2.section_ref, s32[8]{0:T(128)} %plan_ref.3, f32[8,256,128]{2,1,0:T(8,128)} %bitcast.18, s32[2,128]{1,0:T(2,128)} %land_ref.1, s32[2,128]{1,0:T(2,128)} %levels_ref.1), custom_call_target="tpu_custom_call" | custom-call | tf_op jit(solution)/shard_map/init_slabs/pallas_call | solution.py:95
  3.4 12.4 %all-to-all-start = ((s16[16,48,128]{2,1,0:T(8,128)(2,1)}), s16[16,48,128]{2,1,0:T(8,128)(2,1)S(1)}, u32[]{:S(2)}, u32[]{:S(2)}) async-start(s16[16,48,128]{2,1,0:T(8,128)(2,1)} %init_slabs.1), calls=%async_computation | async-start | bytes 393216 | tf_op jit(solution)/shard_map/all_to_all | solution.py:549
  15.8 6.9 %prepare.1 = (bf16[8,8,2,16,128]{4,3,2,1,0:T(8,128)(2,1)}, bf16[128,4096]{1,0:T(8,128)(2,1)}, bf16[4096,128]{1,0:T(8,128)(2,1)}) custom-call(s32[8]{0:T(128)} %plan_ref.3, bf16[8,256,128]{2,1,0:T(8,128)(2,1)} %bitcast.21, bf16[4096,128]{1,0:T(8,128)(2,1)} %w_in_ref.3, bf16[128,4096]{1,0:T(8,128)(2,1)} %w_out_ref.1), custom_call_target="tpu_custom_call" | custom-call | bytes 6291456 | tf_op jit(solution)/shard_map/prepare/pallas_call | solution.py:321
  22.7 3.8 %all-to-all-done.msg_ref = s16[16,48,128]{2,1,0:T(8,128)(2,1)S(1)} async-done(((s16[16,48,128]{2,1,0:T(8,128)(2,1)}), s16[16,48,128]{2,1,0:T(8,128)(2,1)S(1)}, u32[]{:S(2)}, u32[]{:S(2)}) %all-to-all-start) | async-done | bytes 196640 | tf_op jit(solution)/shard_map/all_to_all | solution.py:549
  26.5 0.0 copy-start.2
  26.5 2.0 %collective-permute-start = (s16[16,16,128]{2,1,0:T(8,128)(2,1)S(1)}, s16[16,16,128]{2,1,0:T(8,128)(2,1)S(1)}, u32[]{:S(2)}, u32[]{:S(2)}) collective-permute-start(s16[16,16,128]{2,1,0:T(8,128)(2,1)S(1)} %get-tuple-element.25), channel_id=1, source_target_pairs={{0,4},{1,5},{2,6},{3,7},{4,8},{5,9},{6,10},{7,11},{8,12},{9,13},{1... | collective-permute-start | bytes 196616 | tf_op jit(solution)/shard_map/ppermute | solution.py:569
  28.5 2.3 %collective-permute-start.1 = (s16[16,16,128]{2,1,0:T(8,128)(2,1)S(1)}, s16[16,16,128]{2,1,0:T(8,128)(2,1)S(1)}, u32[]{:S(2)}, u32[]{:S(2)}) collective-permute-start(s16[16,16,128]{2,1,0:T(8,128)(2,1)S(1)} %get-tuple-element.26), channel_id=1, source_target_pairs={{4,0},{5,1},{6,2},{7,3},{8,4},{9,5},{10,6},{11,7},{12,8},{13,9},{1... | collective-permute-start | bytes 196616 | tf_op jit(solution)/shard_map/ppermute | solution.py:570
  30.8 0.0 collective-permute-done.left_ref
  30.9 0.0 copy-start.4
  30.9 3.2 %collective-permute-done.1.right_ref = s16[16,16,128]{2,1,0:T(8,128)(2,1)S(1)} collective-permute-done((s16[16,16,128]{2,1,0:T(8,128)(2,1)S(1)}, s16[16,16,128]{2,1,0:T(8,128)(2,1)S(1)}, u32[]{:S(2)}, u32[]{:S(2)}) %collective-permute-start.1) | collective-permute-done | bytes 65568 | tf_op jit(solution)/shard_map/ppermute | solution.py:570
  34.1 0.0 copy-start.5
  34.1 12.7 %all-to-all-start.1 = ((bf16[64,2,16,128]{3,2,1,0:T(8,128)(2,1)}), bf16[64,2,16,128]{3,2,1,0:T(8,128)(2,1)S(1)}, u32[]{:S(2)}, u32[]{:S(2)}) async-start(bf16[64,2,16,128]{3,2,1,0:T(8,128)(2,1)} %bitcast.20), calls=%async_computation.1 | async-start | bytes 1048576 | tf_op jit(solution)/shard_map/all_to_all | solution.py:549
  46.9 0.0 copy-done.2
  46.9 0.0 copy-done.4
  46.9 0.0 copy-done.5
  46.9 20.4 %rollout.1 = (bf16[4,32,16,128]{3,2,1,0:T(8,128)(2,1)}, bf16[4,32,16,128]{3,2,1,0:T(8,128)(2,1)}, f32[4,32,16,128]{3,2,1,0:T(8,128)}, f32[32,16,128]{2,1,0:T(8,128)}) custom-call(s32[1]{0:T(128)} %bitcast.1.chunk_ref, s16[16,48,128]{2,1,0:T(8,128)(2,1)} %copy-done.2, s16[16,16,128]{2,1,0:T(8,128)(2,1)} %copy-done.4, s16[16,16,128]{2,1,0:T(8,128)(2,1)} %copy-done.5, ...), custom_call_target="tpu_custom_call" | custom-call | flops 5905580032 | bytes 6291456 | tf_op jit(solution)/shard_map/rollout/pallas_call | solution.py:265
  67.3 0.0 all-to-all-done.1
  67.3 0.0 copy-start.1
  67.3 0.8 copy-done.1
  68.1 2.7 %own_columns.1.own_ref = bf16[2,2048,128]{2,1,0:T(8,128)(2,1)} custom-call(bf16[2048,128]{1,0:T(8,128)(2,1)} %bitcast.22, f32[2048,128]{1,0:T(8,128)} %bitcast.19, bf16[2048,128]{1,0:T(8,128)(2,1)} %bitcast.16, f32[512,128]{1,0:T(8,128)} %bitcast.23), custom_call_target="tpu_custom_call" | custom-call | tf_op jit(solution)/shard_map/own_columns/pallas_call | solution.py:411
  70.9 0.5 collective-permute-start.2
  71.3 12.6 %all-to-all-start.2 = ((bf16[64,2,16,128]{3,2,1,0:T(8,128)(2,1)}), bf16[64,2,16,128]{3,2,1,0:T(8,128)(2,1)S(1)}, u32[]{:S(2)}, u32[]{:S(2)}) async-start(bf16[64,2,16,128]{3,2,1,0:T(8,128)(2,1)} %bitcast.12), calls=%async_computation.2 | async-start | bytes 1048576 | tf_op jit(solution)/shard_map/all_to_all | solution.py:549
  84.0 0.0 collective-permute-done.2.their_ref
  84.0 0.0 copy-start.3
  84.0 1.0 copy-done.3
  84.9 20.8 %half_grads.1 = bf16[32,2,64,128]{3,2,1,0:T(8,128)(2,1)} custom-call(s32[1]{0:T(128)} %bitcast.half_ref, bf16[2,2048,128]{2,1,0:T(8,128)(2,1)} %own_columns.1.own_ref, bf16[2,2048,128]{2,1,0:T(8,128)(2,1)} %copy-done.3, bf16[4096,128]{1,0:T(8,128)(2,1)} %w_in_ref.3, bf16[4096,128]{1,0:T(8,128)(2,1)} %get-tuple-element.31.w_out_t.w_out_ref), custom_call_target="tpu_custom_call" | custom-call | flops 8589934592 | bytes 5242880 | tf_op jit(solution)/shard_map/half_grads/pallas_call | solution.py:443
  105.7 0.0 all-to-all-done.2
  105.7 0.0 copy-start
  105.7 7.5 %all-to-all-start.3 = ((bf16[32,2,64,128]{3,2,1,0:T(8,128)(2,1)}), bf16[32,2,64,128]{3,2,1,0:T(8,128)(2,1)S(1)}, u32[]{:S(2)}, u32[]{:S(2)}) async-start(bf16[32,2,64,128]{3,2,1,0:T(8,128)(2,1)} %half_grads.1), calls=%async_computation.3 | async-start | bytes 2097152 | tf_op jit(solution)/shard_map/all_to_all | solution.py:549
  113.3 0.0 copy-done
  113.3 5.2 %spread_trajectory.1 = f32[8,256,128]{2,1,0:T(8,128)} custom-call(bf16[8,8,2,16,128]{4,3,2,1,0:T(8,128)(2,1)} %bitcast.15), custom_call_target="tpu_custom_call" | custom-call | tf_op jit(solution)/shard_map/spread_trajectory/pallas_call | solution.py:356
  118.5 11.7 %all-to-all-done.3.in_ref = bf16[32,2,64,128]{3,2,1,0:T(8,128)(2,1)S(1)} async-done(((bf16[32,2,64,128]{3,2,1,0:T(8,128)(2,1)}), bf16[32,2,64,128]{3,2,1,0:T(8,128)(2,1)S(1)}, u32[]{:S(2)}, u32[]{:S(2)}) %all-to-all-start.3) | async-done | bytes 1048608 | tf_op jit(solution)/shard_map/all_to_all | solution.py:549
  130.3 0.1 plane_sum.1.own_ref
  130.4 2.7 %collective-permute-start.5 = (bf16[2,64,128]{2,1,0:T(8,128)(2,1)S(1)}, bf16[2,64,128]{2,1,0:T(8,128)(2,1)S(1)}, u32[]{:S(2)}, u32[]{:S(2)}) collective-permute-start(bf16[2,64,128]{2,1,0:T(8,128)(2,1)S(1)} %plane_sum.1.own_ref), channel_id=1, source_target_pairs={{0,34},{2,32},{32,2},{34,0},{1,35},{3,33},{33,3},{35,1},{4,38},{6,... | collective-permute-start | bytes 98312 | tf_op jit(solution)/shard_map/ppermute | solution.py:588
  133.1 2.7 %collective-permute-start.4 = (bf16[2,64,128]{2,1,0:T(8,128)(2,1)S(1)}, bf16[2,64,128]{2,1,0:T(8,128)(2,1)S(1)}, u32[]{:S(2)}, u32[]{:S(2)}) collective-permute-start(bf16[2,64,128]{2,1,0:T(8,128)(2,1)S(1)} %plane_sum.1.own_ref), channel_id=1, source_target_pairs={{0,32},{2,34},{32,0},{34,2},{1,33},{3,35},{33,1},{35,3},{4,36},{6,... | collective-permute-start | bytes 98312 | tf_op jit(solution)/shard_map/ppermute | solution.py:588
  135.7 0.4 collective-permute-start.3
  136.2 0.0 collective-permute-done.5.both_ref
  136.2 3.6 %collective-permute-done.4.far_ref = bf16[2,64,128]{2,1,0:T(8,128)(2,1)S(1)} collective-permute-done((bf16[2,64,128]{2,1,0:T(8,128)(2,1)S(1)}, bf16[2,64,128]{2,1,0:T(8,128)(2,1)S(1)}, u32[]{:S(2)}, u32[]{:S(2)}) %collective-permute-start.4) | collective-permute-done | bytes 32800 | tf_op jit(solution)/shard_map/ppermute | solution.py:588
  139.8 0.7 collective-permute-done.3.near_ref
  140.5 0.2 column_copies.1
  140.7 20.0 %all_to_all.25.code_ref = s16[32,144,128]{2,1,0:T(8,128)(2,1)S(1)} all-to-all(s16[32,144,128]{2,1,0:T(8,128)(2,1)S(1)} %column_copies.1), channel_id=1, replica_groups=mesh['sec'=4,'zh'=2,'cx'=4,'core'=2,'c1'=2,'c0'=2] {'sec','cx','c0'}, dimensions={0} | all-to-all | bytes 2359296 | tf_op jit(solution)/shard_map/all_to_all | solution.py:549
  160.6 3.2 %collective-permute-start.6 = (s16[32,144,128]{2,1,0:T(8,128)(2,1)S(1)}, s16[32,144,128]{2,1,0:T(8,128)(2,1)S(1)}, u32[]{:S(2)}, u32[]{:S(2)}) collective-permute-start(s16[32,144,128]{2,1,0:T(8,128)(2,1)S(1)} %all_to_all.25.code_ref), channel_id=1, source_target_pairs={{0,4},{4,0},{1,5},{5,1},{2,6},{6,2},{3,7},{7,3},{8,12},{12,8},{9,1... | collective-permute-start | bytes 3538952 | tf_op jit(solution)/shard_map/ppermute | solution.py:591
  163.9 1.4 finish_half.2
  165.3 1.0 collective-permute-done.6.code_ref
  166.4 1.4 finish_half.3
  (1 shorter events, 0.0 us)
Async XLA Ops:
  3.4 23.1 %all-to-all-start = ((s16[16,48,128]{2,1,0:T(8,128)(2,1)}), s16[16,48,128]{2,1,0:T(8,128)(2,1)S(1)}, u32[]{:S(2)}, u32[]{:S(2)}) async-start(s16[16,48,128]{2,1,0:T(8,128)(2,1)} %init_slabs.1), calls=%async_computation | async-start | bytes 393216 | tf_op jit(solution)/shard_map/all_to_all | solution.py:549
  26.5 20.4 %copy-start.2 = (s16[16,48,128]{2,1,0:T(8,128)(2,1)}, s16[16,48,128]{2,1,0:T(8,128)(2,1)S(1)}, u32[]{:S(2)}) copy-start(s16[16,48,128]{2,1,0:T(8,128)(2,1)S(1)} %all-to-all-done.msg_ref) | copy-start | bytes 589828
  26.5 4.3 %collective-permute-start = (s16[16,16,128]{2,1,0:T(8,128)(2,1)S(1)}, s16[16,16,128]{2,1,0:T(8,128)(2,1)S(1)}, u32[]{:S(2)}, u32[]{:S(2)}) collective-permute-start(s16[16,16,128]{2,1,0:T(8,128)(2,1)S(1)} %get-tuple-element.25), channel_id=1, source_target_pairs={{0,4},{1,5},{2,6},{3,7},{4,8},{5,9},{6,10},{7,11},{8,12},{9,13},{1... | collective-permute-start | bytes 196616 | tf_op jit(solution)/shard_map/ppermute | solution.py:569
  28.5 5.6 %collective-permute-start.1 = (s16[16,16,128]{2,1,0:T(8,128)(2,1)S(1)}, s16[16,16,128]{2,1,0:T(8,128)(2,1)S(1)}, u32[]{:S(2)}, u32[]{:S(2)}) collective-permute-start(s16[16,16,128]{2,1,0:T(8,128)(2,1)S(1)} %get-tuple-element.26), channel_id=1, source_target_pairs={{4,0},{5,1},{6,2},{7,3},{8,4},{9,5},{10,6},{11,7},{12,8},{13,9},{1... | collective-permute-start | bytes 196616 | tf_op jit(solution)/shard_map/ppermute | solution.py:570
  30.9 16.0 %copy-start.4 = (s16[16,16,128]{2,1,0:T(8,128)(2,1)}, s16[16,16,128]{2,1,0:T(8,128)(2,1)S(1)}, u32[]{:S(2)}) copy-start(s16[16,16,128]{2,1,0:T(8,128)(2,1)S(1)} %collective-permute-done.left_ref) | copy-start | bytes 196612
  34.1 12.8 %copy-start.5 = (s16[16,16,128]{2,1,0:T(8,128)(2,1)}, s16[16,16,128]{2,1,0:T(8,128)(2,1)S(1)}, u32[]{:S(2)}) copy-start(s16[16,16,128]{2,1,0:T(8,128)(2,1)S(1)} %collective-permute-done.1.right_ref) | copy-start | bytes 196612
  34.1 33.2 %all-to-all-start.1 = ((bf16[64,2,16,128]{3,2,1,0:T(8,128)(2,1)}), bf16[64,2,16,128]{3,2,1,0:T(8,128)(2,1)S(1)}, u32[]{:S(2)}, u32[]{:S(2)}) async-start(bf16[64,2,16,128]{3,2,1,0:T(8,128)(2,1)} %bitcast.20), calls=%async_computation.1 | async-start | bytes 1048576 | tf_op jit(solution)/shard_map/all_to_all | solution.py:549
  67.3 0.8 copy-start.1
  70.9 13.1 %collective-permute-start.2 = (bf16[2,2048,128]{2,1,0:T(8,128)(2,1)}, bf16[2,2048,128]{2,1,0:T(8,128)(2,1)S(1)}, u32[]{:S(2)}, u32[]{:S(2)}) collective-permute-start(bf16[2,2048,128]{2,1,0:T(8,128)(2,1)} %own_columns.1.own_ref), channel_id=1, source_target_pairs={{0,4},{4,0},{1,5},{5,1},{2,6},{6,2},{3,7},{7,3},{8,12},{12,8},{9,1... | collective-permute-start | bytes 3145736 | tf_op jit(solution)/shard_map/ppermute | solution.py:580
  71.3 34.4 %all-to-all-start.2 = ((bf16[64,2,16,128]{3,2,1,0:T(8,128)(2,1)}), bf16[64,2,16,128]{3,2,1,0:T(8,128)(2,1)S(1)}, u32[]{:S(2)}, u32[]{:S(2)}) async-start(bf16[64,2,16,128]{3,2,1,0:T(8,128)(2,1)} %bitcast.12), calls=%async_computation.2 | async-start | bytes 1048576 | tf_op jit(solution)/shard_map/all_to_all | solution.py:549
  84.0 1.0 copy-start.3
  105.7 7.6 %copy-start = (bf16[64,2,16,128]{3,2,1,0:T(8,128)(2,1)}, bf16[64,2,16,128]{3,2,1,0:T(8,128)(2,1)S(1)}, u32[]{:S(2)}) copy-start(bf16[64,2,16,128]{3,2,1,0:T(8,128)(2,1)S(1)} %all-to-all-done.2) | copy-start | bytes 1572868
  105.7 24.5 %all-to-all-start.3 = ((bf16[32,2,64,128]{3,2,1,0:T(8,128)(2,1)}), bf16[32,2,64,128]{3,2,1,0:T(8,128)(2,1)S(1)}, u32[]{:S(2)}, u32[]{:S(2)}) async-start(bf16[32,2,64,128]{3,2,1,0:T(8,128)(2,1)} %half_grads.1), calls=%async_computation.3 | async-start | bytes 2097152 | tf_op jit(solution)/shard_map/all_to_all | solution.py:549
  130.4 5.7 %collective-permute-start.5 = (bf16[2,64,128]{2,1,0:T(8,128)(2,1)S(1)}, bf16[2,64,128]{2,1,0:T(8,128)(2,1)S(1)}, u32[]{:S(2)}, u32[]{:S(2)}) collective-permute-start(bf16[2,64,128]{2,1,0:T(8,128)(2,1)S(1)} %plane_sum.1.own_ref), channel_id=1, source_target_pairs={{0,34},{2,32},{32,2},{34,0},{1,35},{3,33},{33,3},{35,1},{4,38},{6,... | collective-permute-start | bytes 98312 | tf_op jit(solution)/shard_map/ppermute | solution.py:588
  133.1 6.7 %collective-permute-start.4 = (bf16[2,64,128]{2,1,0:T(8,128)(2,1)S(1)}, bf16[2,64,128]{2,1,0:T(8,128)(2,1)S(1)}, u32[]{:S(2)}, u32[]{:S(2)}) collective-permute-start(bf16[2,64,128]{2,1,0:T(8,128)(2,1)S(1)} %plane_sum.1.own_ref), channel_id=1, source_target_pairs={{0,32},{2,34},{32,0},{34,2},{1,33},{3,35},{33,1},{35,3},{4,36},{6,... | collective-permute-start | bytes 98312 | tf_op jit(solution)/shard_map/ppermute | solution.py:588
  135.7 4.7 %collective-permute-start.3 = (bf16[2,64,128]{2,1,0:T(8,128)(2,1)S(1)}, bf16[2,64,128]{2,1,0:T(8,128)(2,1)S(1)}, u32[]{:S(2)}, u32[]{:S(2)}) collective-permute-start(bf16[2,64,128]{2,1,0:T(8,128)(2,1)S(1)} %plane_sum.1.own_ref), channel_id=1, source_target_pairs={{0,2},{2,0},{32,34},{34,32},{1,3},{3,1},{33,35},{35,33},{4,6},{6,4... | collective-permute-start | bytes 98312 | tf_op jit(solution)/shard_map/ppermute | solution.py:588
  160.6 5.7 %collective-permute-start.6 = (s16[32,144,128]{2,1,0:T(8,128)(2,1)S(1)}, s16[32,144,128]{2,1,0:T(8,128)(2,1)S(1)}, u32[]{:S(2)}, u32[]{:S(2)}) collective-permute-start(s16[32,144,128]{2,1,0:T(8,128)(2,1)S(1)} %all_to_all.25.code_ref), channel_id=1, source_target_pairs={{0,4},{4,0},{1,5},{5,1},{2,6},{6,2},{3,7},{7,3},{8,12},{12,8},{9,1... | collective-permute-start | bytes 3538952 | tf_op jit(solution)/shard_map/ppermute | solution.py:591
